TPU v7x, 128 devices: a whole 4x4x4 slice. The times are simulated.
128 devices in a mesh: fsdp: 8 (over x, z_hi), ctx: 4 (over z_lo, core), tp: 4 (over y).
Axes of the slice: x: 4, y: 4, z: 4 (z_hi: 2, z_lo: 2; z = z_hi * 2 + z_lo), core: 2. Of those that a mesh axis runs over, the one named last changes fastest.
Arguments:
- hidden_in: bfloat16 [8192, 1536], P(('fsdp', 'ctx')), may hold values from -6 to 6
- cotangent: bfloat16 [8192, 1536], P(('fsdp', 'ctx')), may hold values from -6 to 6
- seq_lengths: int32 [32], replicated, may hold values from 1 to 1021, as said below
- deal_order: int32 [8192], replicated, may hold values from 0 to 8191, as said below
- mixer_gain: bfloat16 [1536], P(('fsdp', 'ctx')), may hold values from 0.5 to 1.5
- mixer_project: bfloat16 [1536, 3, 1536], P(('fsdp', 'ctx'), None, 'tp'), may hold values from -0.15625 to 0.15625
- mixer_kernel: bfloat16 [3, 1536], replicated, may hold values from -2.390625 to 2.390625
- mixer_output: bfloat16 [1536, 1536], P('tp', ('fsdp', 'ctx')), may hold values from -0.15625 to 0.15625
- first_gain: bfloat16 [1536], P(('fsdp', 'ctx')), may hold values from 0.5 to 1.5
- first_gateup: bfloat16 [1536, 2, 6912], P(('fsdp', 'ctx'), None, 'tp'), may hold values from -0.15625 to 0.15625
- first_down: bfloat16 [6912, 1536], P('tp', ('fsdp', 'ctx')), may hold values from -0.078125 to 0.078125
- attend_gain: bfloat16 [1536], P(('fsdp', 'ctx')), may hold values from 0.5 to 1.5
- attend_project: bfloat16 [1536, 2560], P(('fsdp', 'ctx'), 'tp'), may hold values from -0.15625 to 0.15625
- query_gain: bfloat16 [64], replicated, may hold values from 0.5 to 1.5
- key_gain: bfloat16 [64], replicated, may hold values from 0.5 to 1.5
- attend_output: bfloat16 [1536, 1536], P('tp', ('fsdp', 'ctx')), may hold values from -0.875 to 0.875
- second_gain: bfloat16 [1536], P(('fsdp', 'ctx')), may hold values from 0.5 to 1.5
- second_gateup: bfloat16 [1536, 2, 6912], P(('fsdp', 'ctx'), None, 'tp'), may hold values from -0.15625 to 0.15625
- second_down: bfloat16 [6912, 1536], P('tp', ('fsdp', 'ctx')), may hold values from -0.078125 to 0.078125
Outputs:
- layer_out: bfloat16 [8192, 1536], P(('fsdp', 'ctx'))
- input_gradient: bfloat16 [8192, 1536], P(('fsdp', 'ctx'))
- mixer_gain_gradient: float32 [1536], P(('fsdp', 'ctx'))
- mixer_project_gradient: float32 [1536, 3, 1536], P(('fsdp', 'ctx'), None, 'tp')
- mixer_kernel_gradient: float32 [3, 1536], replicated
- mixer_output_gradient: float32 [1536, 1536], P('tp', ('fsdp', 'ctx'))
- first_gain_gradient: float32 [1536], P(('fsdp', 'ctx'))
- first_gateup_gradient: float32 [1536, 2, 6912], P(('fsdp', 'ctx'), None, 'tp')
- first_down_gradient: float32 [6912, 1536], P('tp', ('fsdp', 'ctx'))
- attend_gain_gradient: float32 [1536], P(('fsdp', 'ctx'))
- attend_project_gradient: float32 [1536, 2560], P(('fsdp', 'ctx'), 'tp')
- query_gain_gradient: float32 [64], replicated
- key_gain_gradient: float32 [64], replicated
- attend_output_gradient: float32 [1536, 1536], P('tp', ('fsdp', 'ctx'))
- second_gain_gradient: float32 [1536], P(('fsdp', 'ctx'))
- second_gateup_gradient: float32 [1536, 2, 6912], P(('fsdp', 'ctx'), None, 'tp')
- second_down_gradient: float32 [6912, 1536], P('tp', ('fsdp', 'ctx'))
Inputs may be any that keep to these rules, and one draw needn't show every extreme that they name: `seq_lengths`: sequences 4 * g to 4 * g + 3 fill dealt rows g * 1024 to (g + 1) * 1024 - 1 exactly; in each such group one sequence covers all but at most 128 of its rows. deal_order is a permutation. Dealt rows come in aligned blocks of 8; each block holds 8 consecutive arrival tokens in order, starting at a multiple of 8; the 256 dealt rows of each device take exactly one block from the 256 arrival rows of every device.
All inputs are finite; a program needn't handle non-finite values.
Results may differ from a plain program's by a relative error of at most 0.02.
The roundings to bfloat16 on the way count: a program that leaves them out, or rounds other values in their place, can miss the bound.
Values may be sent and summed in bfloat16 or wider, within the bound.
No kernel may reach another device: no remote copies, remote signals or barrier semaphores. Data moves between devices by JAX's collectives and lax.ppermute only.
A program may use at most 256 MiB of HBM per device.

v0:
```python
import functools

import jax
import jax.numpy as jnp
from jax import lax
from jax.experimental import pallas as pl
from jax.experimental.pallas import tpu as pltpu
from jax.sharding import Mesh, PartitionSpec as P

H = 24
KVH = 8
HD = 64

EPSILON = 1e-05
ROPE_BASE = 1000000.0
NEGATIVE = -1e30

CHIP_AXES = ("x", "z_hi", "z_lo")
TOKEN_AXES = CHIP_AXES + ("core",)
GROUP_AXES = ("x", "z_hi")
CTX_AXES = ("z_lo", "core")
Z_AXES = ("z_hi", "z_lo")
CORES = 2
TILE = 256
VMEM_LIMIT = 48 * 1024 * 1024
MIDDLE_LIMIT = 24 * 1024 * 1024
SMALL_LIMIT = 12 * 1024 * 1024
F32 = jnp.float32
BF16 = jnp.bfloat16


def norm_rows(values, scales):
    return values * lax.rsqrt(jnp.mean(values * values, axis=-1, keepdims=True) + EPSILON) * scales


def locate(lengths, positions):
    seq_ends = jnp.cumsum(lengths)
    segment = jnp.sum((positions[:, None] >= seq_ends[None, :]).astype(jnp.int32), axis=1)
    starts = seq_ends - lengths
    first_row = jnp.sum(
        jnp.where(segment[:, None] == jnp.arange(lengths.shape[0])[None, :], starts[None, :], 0),
        axis=1,
    )
    return (segment, positions - first_row)


def shortconv(extended, kernel_in, segment):
    kernel_taps = kernel_in.shape[0]
    out_rows = extended.shape[0] - kernel_taps + 1
    result = kernel_in[0] * extended[kernel_taps - 1 :]
    for t in range(1, kernel_taps):
        earlier = extended[kernel_taps - 1 - t : kernel_taps - 1 - t + out_rows]
        same_seq = (
            segment[kernel_taps - 1 - t : kernel_taps - 1 - t + out_rows]
            == segment[kernel_taps - 1 :]
        ).astype(F32)[:, None]
        result = result + kernel_in[t] * earlier * same_seq
    return result


def from_behind(block, distance):
    devices = range(lax.axis_size(CTX_AXES))
    route = [(i - distance, i) for i in devices if i - distance in devices]
    return lax.ppermute(block, CTX_AXES, route)


def swap_ctx(block, mask):
    return lax.ppermute(block, CTX_AXES, [(i, i ^ mask) for i in range(lax.axis_size(CTX_AXES))])


def swap_core(block):
    return lax.ppermute(block, "core", [(0, 1), (1, 0)])


def shift_tp(block, distance):
    members = lax.axis_size("tp")
    return lax.ppermute(block, "tp", [(i, (i + distance) % members) for i in range(members)])


def tp_gather(shard):
    return [shard] + [shift_tp(shard, k) for k in range(1, lax.axis_size("tp"))]


def tp_chunks(partial):
    rows = partial.shape[0] // lax.axis_size("tp")
    return [
        partial[k * rows : (k + 1) * rows].astype(F32 if k == 0 else BF16)
        for k in range(lax.axis_size("tp"))
    ]


def tp_scatter(chunks):
    return [chunks[0]] + [shift_tp(chunks[k], -k) for k in range(1, len(chunks))]


def add_parts(parts):
    total = parts[0]
    for part in parts[1:]:
        total = total + part.astype(F32)
    return total


def arrange(order, rows):
    return times(order, rows).astype(BF16)


def times(left, right):
    return lax.dot_general(left, right, (((1,), (0,)), ((), ())), preferred_element_type=F32)


def times_t(left, right):
    return lax.dot_general(left, right, (((1,), (1,)), ((), ())), preferred_element_type=F32)


def times_rows(left, right):
    return lax.dot_general(left, right, (((0,), (0,)), ((), ())), preferred_element_type=F32)


def assemble(chunk_refs, target):
    rows = chunk_refs[0].shape[0]
    for k, ref in enumerate(chunk_refs):
        target[k * rows : (k + 1) * rows, :] = ref[...]


def spread(total, chunk_refs):
    rows = chunk_refs[0].shape[0]
    for k, ref in enumerate(chunk_refs):
        ref[...] = total[k * rows : (k + 1) * rows, :].astype(ref.dtype)


def whole(shape):
    return pl.BlockSpec(shape, lambda *_: (0,) * len(shape))


def one_step(kernel, operands, out_shape, limit, name, flops):
    size = sum(v.size * v.dtype.itemsize for v in list(operands) + list(out_shape))
    return pl.pallas_call(
        kernel,
        grid=(1,),
        in_specs=[whole(v.shape) for v in operands],
        out_specs=[whole(v.shape) for v in out_shape],
        out_shape=out_shape,
        compiler_params=pltpu.CompilerParams(vmem_limit_bytes=limit),
        cost_estimate=pl.CostEstimate(flops=flops, bytes_accessed=size, transcendentals=0),
        name=name,
    )(*operands)


def sum_refs(refs):
    total = refs[0][...]
    for ref in refs[1:]:
        total = total + ref[...].astype(F32)
    return total


def add_norm_kernel(*refs):
    stream_ref, gain_ref, out_ref, normed_ref = refs[-4:]
    stream = stream_ref[...] + sum_refs(refs[:-4])
    out_ref[...] = stream
    normed_ref[...] = norm_rows(stream, gain_ref[...]).astype(BF16)


def add_norm(parts, stream, gain):
    return one_step(
        add_norm_kernel,
        [*parts, stream, gain[None]],
        [jax.ShapeDtypeStruct(stream.shape, F32), jax.ShapeDtypeStruct(stream.shape, BF16)],
        SMALL_LIMIT,
        "add_norm",
        10 * stream.size,
    )


def norm_backward_kernel(*refs):
    stream_ref, gain_ref, upward_ref, out_ref, rounded_ref, gain_grad_ref = refs[-6:]
    stream = stream_ref[...]
    d_normed = sum_refs(refs[:-6])
    spread_of = lax.rsqrt(jnp.mean(stream * stream, axis=1, keepdims=True) + EPSILON)
    gain_grad_ref[...] = jnp.sum(d_normed * stream * spread_of, axis=0, keepdims=True)
    scaled = d_normed * gain_ref[...]
    inner = jnp.mean(scaled * stream, axis=1, keepdims=True)
    result = upward_ref[...] + spread_of * scaled - stream * (
        spread_of * spread_of * spread_of * inner
    )
    out_ref[...] = result
    rounded_ref[...] = result.astype(BF16)


def norm_backward(parts, stream, gain, upward):
    out, rounded, gain_grad = one_step(
        norm_backward_kernel,
        [*parts, stream, gain[None], upward],
        [
            jax.ShapeDtypeStruct(stream.shape, F32),
            jax.ShapeDtypeStruct(stream.shape, BF16),
            jax.ShapeDtypeStruct((1, stream.shape[1]), F32),
        ],
        SMALL_LIMIT,
        "norm_backward",
        20 * stream.size,
    )
    return out, rounded, gain_grad[0]


def weight_specs(depth, steps):
    return [
        pl.BlockSpec((depth, 2 * TILE), lambda j: (0, j)),
        pl.BlockSpec((depth, TILE), lambda j: (0, 2 * steps + j)),
    ]


def chunk_shapes(count, rows, width):
    return [jax.ShapeDtypeStruct((rows, width), F32 if k == 0 else BF16) for k in range(count)]


def ffn_forward_kernel(count, *refs):
    x_refs, (gu_ref, dn_ref), outs = refs[:count], refs[count : count + 2], refs[count + 2 : -2]
    x_all, total = refs[-2:]
    step = pl.program_id(0)

    @pl.when(step == 0)
    def _():
        assemble(x_refs, x_all)
        total[...] = jnp.zeros_like(total)

    both = times(x_all[...], gu_ref[...])
    gate, up = both[:, :TILE], both[:, TILE:]
    active = (gate * jax.nn.sigmoid(gate) * up).astype(BF16)
    total[...] += times_t(active, dn_ref[...])

    @pl.when(step == pl.num_programs(0) - 1)
    def _():
        spread(total[...], outs)


def ffn_forward(chunks, pack, steps):
    count, (rows, width) = len(chunks), chunks[0].shape
    tokens = count * rows
    return pl.pallas_call(
        functools.partial(ffn_forward_kernel, count),
        grid=(steps,),
        in_specs=[whole((rows, width))] * count + weight_specs(width, steps),
        out_specs=[whole((rows, width))] * count,
        out_shape=chunk_shapes(count, rows, width),
        scratch_shapes=[pltpu.VMEM((tokens, width), BF16), pltpu.VMEM((tokens, width), F32)],
        compiler_params=pltpu.CompilerParams(vmem_limit_bytes=VMEM_LIMIT),
        cost_estimate=pl.CostEstimate(
            flops=2 * tokens * width * 3 * TILE * steps,
            bytes_accessed=2 * width * 3 * TILE * steps,
            transcendentals=tokens * TILE * steps,
        ),
        name="ffn_forward",
    )(*chunks, pack, pack)


def ffn_backward_kernel(count, forward, core_ref, *refs):
    x_refs, b_refs = refs[:count], refs[count : 2 * count]
    gu_ref, dn_ref = refs[2 * count : 2 * count + 2]
    place = 2 * count + 2
    back_outs = refs[place : place + count]
    place += count
    if forward:
        outs = refs[place : place + count]
        place += count
    keep_ref, side_ref = refs[place : place + 2]
    scratch = refs[place + 2 :]
    x_all, b_all, d_total = scratch[:3]
    step = pl.program_id(0)
    width = x_all.shape[1]

    @pl.when(step == 0)
    def _():
        assemble(x_refs, x_all)
        assemble(b_refs, b_all)
        if forward:
            side_ref[:, :width] = x_all[...]
            side_ref[:, width : 2 * width] = b_all[...]
        d_total[...] = jnp.zeros_like(d_total)
        if forward:
            scratch[3][...] = jnp.zeros_like(scratch[3])

    both = times(x_all[...], gu_ref[...])
    gate, up = both[:, :TILE], both[:, TILE:]
    d_active = times(b_all[...], dn_ref[...])
    sigmoid = jax.nn.sigmoid(gate)
    silu = gate * sigmoid
    active = (silu * up).astype(BF16)
    if forward:
        scratch[3][...] += times_t(active, dn_ref[...])
    d_gate = (d_active * up * (sigmoid * (1.0 + gate * (1.0 - sigmoid)))).astype(BF16)
    d_up = (d_active * silu).astype(BF16)
    d_total[...] += times_t(jnp.concatenate([d_gate, d_up], axis=1), gu_ref[...])
    first = core_ref[0] == 0
    half = TILE // 2
    low, high = active[:, :half], active[:, half:]
    offset = 2 * width if forward else 0
    wide = pl.multiple_of(step * TILE, TILE)
    narrow = pl.multiple_of(pl.num_programs(0) * TILE + step * half, half)
    side_wide = pl.multiple_of(offset + wide, TILE)
    side_narrow = pl.multiple_of(offset + narrow, half)

    @pl.when(first)
    def _():
        keep_ref[:, pl.ds(wide, TILE)] = d_gate
        keep_ref[:, pl.ds(narrow, half)] = low
        side_ref[:, pl.ds(side_wide, TILE)] = d_up
        side_ref[:, pl.ds(side_narrow, half)] = high

    @pl.when(jnp.logical_not(first))
    def _():
        keep_ref[:, pl.ds(wide, TILE)] = d_up
        keep_ref[:, pl.ds(narrow, half)] = high
        side_ref[:, pl.ds(side_wide, TILE)] = d_gate
        side_ref[:, pl.ds(side_narrow, half)] = low

    @pl.when(step == pl.num_programs(0) - 1)
    def _():
        spread(d_total[...], back_outs)
        if forward:
            spread(scratch[3][...], outs)


def ffn_backward(core, chunks, back_chunks, pack, steps, forward):
    count, (rows, width) = len(chunks), chunks[0].shape
    tokens = count * rows
    block = TILE + TILE // 2
    ways = 2 if forward else 1
    side_width = (2 * width if forward else 0) + steps * block
    results = pl.pallas_call(
        functools.partial(ffn_backward_kernel, count, forward),
        grid=(steps,),
        in_specs=[pl.BlockSpec(memory_space=pltpu.SMEM)]
        + [whole((rows, width))] * (2 * count)
        + weight_specs(width, steps),
        out_specs=[whole((rows, width))] * (ways * count)
        + [whole((tokens, steps * block)), whole((tokens, side_width))],
        out_shape=chunk_shapes(count, rows, width) * ways
        + [
            jax.ShapeDtypeStruct((tokens, steps * block), BF16),
            jax.ShapeDtypeStruct((tokens, side_width), BF16),
        ],
        scratch_shapes=[pltpu.VMEM((tokens, width), BF16)] * 2
        + [pltpu.VMEM((tokens, width), F32)] * ways,
        compiler_params=pltpu.CompilerParams(vmem_limit_bytes=VMEM_LIMIT),
        cost_estimate=pl.CostEstimate(
            flops=2 * tokens * width * (4 + ways) * TILE * steps,
            bytes_accessed=2 * width * 3 * TILE * steps + 4 * tokens * side_width,
            transcendentals=tokens * TILE * steps,
        ),
        name="ffn_both" if forward else "ffn_backward",
    )(core, *chunks, *back_chunks, pack, pack)
    return results[:count], results[count : ways * count], results[-2], results[-1]


def gradient_kernel(edge, cut, *refs):
    one_own, one_other, two_own, two_other, own_ref, other_ref = refs[:6]
    out_ref = refs[-1]
    step = pl.program_id(0)

    def product(own_left, other_left, columns):
        total = times_rows(own_left[...], own_ref[:, columns])
        total += times_rows(other_left[...], other_ref[:, columns])
        out_ref[:, columns] = total.astype(BF16)

    @pl.when(step < edge)
    def _():
        product(one_own, one_other, slice(None))

    @pl.when(step > edge if cut else step >= edge)
    def _():
        product(two_own, two_other, slice(None))

    if cut:

        @pl.when(step == edge)
        def _():
            product(one_own, one_other, slice(0, cut))
            product(two_own, two_other, slice(cut, None))


def gradient(lefts, own, other, other_start, block, steps, columns, width, out_width, out_start, target):
    tokens = own.shape[0]
    edge, cut = divmod(columns, block)

    def left_spec(index):
        return pl.BlockSpec((tokens, width), lambda j: (0, index))

    in_specs = [left_spec(index) for unused, index in lefts] + [
        pl.BlockSpec((tokens, block), lambda j: (0, j)),
        pl.BlockSpec((tokens, block), lambda j: (0, other_start + j)),
    ]
    operands = [array for array, unused in lefts] + [own, other]
    aliases = {}
    if target is not None:
        in_specs.append(pl.BlockSpec(memory_space=pl.ANY))
        operands.append(target)
        aliases = {len(operands) - 1: 0}
    return pl.pallas_call(
        functools.partial(gradient_kernel, edge, cut),
        grid=(steps,),
        in_specs=in_specs,
        out_specs=pl.BlockSpec((width, block), lambda j: (0, out_start + j)),
        out_shape=jax.ShapeDtypeStruct((width, out_width), BF16),
        input_output_aliases=aliases,
        compiler_params=pltpu.CompilerParams(vmem_limit_bytes=VMEM_LIMIT),
        cost_estimate=pl.CostEstimate(
            flops=4 * tokens * width * block * steps,
            bytes_accessed=2 * width * block * steps,
            transcendentals=0,
        ),
        name="weight_gradient",
    )(*operands)


def turn(rows, cosine, sine):
    half = rows.shape[1] // 2
    first, second = rows[:, :half], rows[:, half:]
    return jnp.concatenate(
        [first * cosine - second * sine, second * cosine + first * sine], axis=1
    )


def head_backward(d_rows, raw, cosine, sine, gain):
    d_normed = turn(d_rows, cosine, -sine)
    spread_of = lax.rsqrt(jnp.mean(raw * raw, axis=1, keepdims=True) + EPSILON)
    d_gain = jnp.sum(d_normed * raw * spread_of, axis=0, keepdims=True)
    scaled = d_normed * gain
    inner = jnp.mean(scaled * raw, axis=1, keepdims=True)
    d_raw = spread_of * scaled - raw * (spread_of * spread_of * spread_of * inner)
    return d_raw.astype(BF16), d_gain


def heads_kernel(groups, raw_ref, cos_ref, sin_ref, query_gain_ref, key_gain_ref, q_ref, kv_ref):
    size = query_gain_ref.shape[1]
    kv_heads = raw_ref.shape[1] // ((groups + 2) * size)
    cosine, sine = cos_ref[...], sin_ref[...]
    for group in range(kv_heads):
        start = group * (groups + 2) * size
        for member in range(groups):
            raw = raw_ref[:, start + member * size : start + (member + 1) * size]
            head = group * groups + member
            rows = turn(norm_rows(raw, query_gain_ref[...]), cosine, sine)
            q_ref[:, head * size : (head + 1) * size] = rows.astype(BF16)
        start += groups * size
        rows = turn(norm_rows(raw_ref[:, start : start + size], key_gain_ref[...]), cosine, sine)
        kv_ref[:, group * size : (group + 1) * size] = rows.astype(BF16)
        value_start = (kv_heads + group) * size
        kv_ref[:, value_start : value_start + size] = raw_ref[
            :, start + size : start + 2 * size
        ].astype(BF16)


def head_probs(key, query, scale, barred):
    scores = times_t(key, query) * scale + barred
    probs = jnp.exp(scores - jnp.max(scores, axis=0, keepdims=True))
    return probs / jnp.sum(probs, axis=0, keepdims=True)


def attend_kernel(scale, size, q_ref, kv_ref, barred_ref, out_ref):
    kv_heads = kv_ref.shape[1] // (2 * size)
    groups = q_ref.shape[1] // (kv_heads * size)
    barred = barred_ref[...].astype(F32)
    for head in range(kv_heads * groups):
        group = head // groups
        columns = slice(head * size, (head + 1) * size)
        key = kv_ref[:, group * size : (group + 1) * size]
        value = kv_ref[:, (kv_heads + group) * size : (kv_heads + group + 1) * size]
        probs = head_probs(key, q_ref[:, columns], scale, barred).astype(BF16)
        out_ref[:, columns] = times_rows(value, probs).T.astype(BF16)


def attend_backward_kernel(
    scale, q_ref, do_ref, kv_ref, barred_ref, raw_ref, cos_ref, sin_ref, gain_ref,
    dq_ref, near_ref, cross_ref, gain_grad_ref,
):
    size = gain_ref.shape[1]
    kv_heads = kv_ref.shape[1] // (2 * size)
    groups = q_ref.shape[1] // (kv_heads * size)
    rows = kv_ref.shape[0] // 4
    cosine, sine, gain = cos_ref[...], sin_ref[...], gain_ref[...]
    barred = barred_ref[...].astype(F32)
    gain_grad = jnp.zeros_like(gain)
    for group in range(kv_heads):
        columns = slice(group * size, (group + 1) * size)
        value_columns = slice((kv_heads + group) * size, (kv_heads + group + 1) * size)
        key, value = kv_ref[:, columns], kv_ref[:, value_columns]
        d_key = d_value = None
        for member in range(groups):
            head = group * groups + member
            head_columns = slice(head * size, (head + 1) * size)
            query, d_out = q_ref[:, head_columns], do_ref[:, head_columns]
            probs = head_probs(key, query, scale, barred)
            d_probs = times_t(value, d_out)
            inner = jnp.sum(probs * d_probs, axis=0, keepdims=True)
            d_scores = (probs * (d_probs - inner)).astype(BF16)
            part_value = times(probs.astype(BF16), d_out)
            part_key = times(d_scores, query) * scale
            d_value = part_value if d_value is None else d_value + part_value
            d_key = part_key if d_key is None else d_key + part_key
            d_query = (times_rows(key, d_scores) * scale).T
            start = (group * (groups + 2) + member) * size
            d_raw, d_gain = head_backward(
                d_query, raw_ref[:, start : start + size], cosine, sine, gain
            )
            dq_ref[:, head_columns] = d_raw
            gain_grad += d_gain
        for part, place in ((d_key, columns), (d_value, value_columns)):
            near_ref[:rows, place] = part[:rows]
            near_ref[rows:, place] = part[2 * rows : 3 * rows]
            cross_ref[:rows, place] = part[rows : 2 * rows].astype(BF16)
            cross_ref[rows:, place] = part[3 * rows :].astype(BF16)
    gain_grad_ref[...] = gain_grad


def assemble_kernel(groups, dq_ref, near_ref, cross_ref, far_ref, raw_ref, cos_ref, sin_ref, gain_ref, out_ref, gain_grad_ref):
    size = gain_ref.shape[1]
    kv_heads = raw_ref.shape[1] // ((groups + 2) * size)
    rows = raw_ref.shape[0]
    both = near_ref[:rows, :] + cross_ref[:rows, :].astype(F32) + far_ref[...].astype(F32)
    gain_grad = jnp.zeros_like(gain_ref[...])
    for group in range(kv_heads):
        start = group * (groups + 2) * size
        out_ref[:, start : start + groups * size] = dq_ref[
            :, group * groups * size : (group + 1) * groups * size
        ]
        start += groups * size
        d_raw, d_gain = head_backward(
            both[:, group * size : (group + 1) * size],
            raw_ref[:, start : start + size],
            cos_ref[...],
            sin_ref[...],
            gain_ref[...],
        )
        gain_grad += d_gain
        out_ref[:, start : start + size] = d_raw
        value_start = (kv_heads + group) * size
        out_ref[:, start + size : start + 2 * size] = both[
            :, value_start : value_start + size
        ].astype(BF16)
    gain_grad_ref[...] = gain_grad


def sum_chips(partial):
    return lax.psum_scatter(partial, CHIP_AXES, scatter_dimension=0, tiled=True)


def gather_pack(pack):
    chips = lax.axis_size(CHIP_AXES)
    core = lax.axis_index("core")
    plane = lax.all_to_all(
        jnp.broadcast_to(pack, (chips,) + pack.shape),
        CHIP_AXES,
        split_axis=0,
        concat_axis=0,
        tiled=True,
    )
    other = swap_core(plane)
    both = jnp.zeros((chips, CORES) + pack.shape, BF16)
    both = lax.dynamic_update_slice(both, plane[:, None], (0, core, 0, 0))
    both = lax.dynamic_update_slice(both, other[:, None], (0, 1 - core, 0, 0))
    return both.reshape(-1, pack.shape[1])


def finish_kernel(steps, core_ref, sum_ref, other_ref, gateup_ref, down_ref, *rest):
    core = core_ref[0]
    rows, hidden = down_ref.shape
    padded = steps * TILE
    half = TILE // 2
    first = core == 0
    mine = sum_ref[pl.ds(pl.multiple_of(core * rows, rows), rows), :].astype(F32)
    other = other_ref[...].astype(F32)
    low = jnp.where(first, mine, other)
    high = jnp.where(first, other, mine)
    gateup_ref[:, 0, :] = low[:, :hidden]
    gateup_ref[:, 1, :] = high[:, :hidden]
    for step in range(steps):
        source = padded + step * half
        for part, columns in enumerate((low, high)):
            place = step * TILE + part * half
            size = min(half, hidden - place)
            if size > 0:
                down_ref[:, place : place + size] = columns[:, source : source + size]
    for ref in rest:
        start = padded + steps * half
        size = low.shape[1] - start
        ref[:, :size] = low[:, start:]
        ref[:, size:] = high[:, start:]


def finish(summed, steps, hidden):
    core = lax.axis_index("core")
    rows, columns = summed.shape[0] // 2, summed.shape[1]
    other = swap_core(lax.dynamic_slice_in_dim(summed, (1 - core) * rows, rows, 0))
    extra = 2 * (columns - steps * (TILE + TILE // 2))
    return pl.pallas_call(
        functools.partial(finish_kernel, steps),
        grid=(1,),
        in_specs=[
            pl.BlockSpec(memory_space=pltpu.SMEM),
            whole(summed.shape),
            whole(other.shape),
        ],
        out_specs=[whole((rows, 2, hidden)), whole((rows, hidden))]
        + [whole((rows, extra))] * (extra > 0),
        out_shape=[
            jax.ShapeDtypeStruct((rows, 2, hidden), F32),
            jax.ShapeDtypeStruct((rows, hidden), F32),
        ]
        + [jax.ShapeDtypeStruct((rows, extra), F32)] * (extra > 0),
        compiler_params=pltpu.CompilerParams(vmem_limit_bytes=VMEM_LIMIT),
        cost_estimate=pl.CostEstimate(
            flops=4 * rows * columns, bytes_accessed=16 * rows * columns, transcendentals=0
        ),
        name="finish_gradients",
    )(core.reshape(1).astype(jnp.int32), summed, other)


def halves(proj, out):
    first = lax.axis_index("core") == 0
    half = (proj.shape[1] + out.shape[1]) // 2
    late = jnp.concatenate([proj[:, half:], out], axis=1)
    early = proj[:, :half]
    return jnp.where(first, early, late), jnp.where(first, late, early)


def body(
    hidden_in,
    cotangent,
    seq_lengths,
    deal_order,
    mixer_gain,
    mixer_project,
    mixer_kernel,
    mixer_output,
    first_gain,
    first_gateup,
    first_down,
    attend_gain,
    attend_project,
    query_gain,
    key_gain,
    attend_output,
    second_gain,
    second_gateup,
    second_down,
):
    shards = lax.axis_size(TOKEN_AXES)
    contexts = lax.axis_size(CTX_AXES)
    members = lax.axis_size("tp")
    row_count, width = hidden_in.shape
    piece_rows = row_count // shards
    part_rows = piece_rows // members
    chunk = row_count // members
    device = lax.axis_index(TOKEN_AXES)
    own = lax.axis_index("tp")
    core = lax.axis_index("core")
    core_ref = core.reshape(1).astype(jnp.int32)
    depth = mixer_gain.shape[0]
    channels = mixer_output.shape[0]
    hidden = first_down.shape[0]
    heads_width = attend_output.shape[0]
    steps = -(-hidden // TILE)
    padded = steps * TILE
    ffn_width = 3 * padded
    block = TILE + TILE // 2

    def pack_ffn(gateup, down):
        wide = jnp.pad(gateup, ((0, 0), (0, 0), (0, padded - hidden)))
        wide = wide.reshape(depth, 2, steps, TILE).transpose(0, 2, 1, 3).reshape(depth, -1)
        return [wide, jnp.pad(down.T, ((0, 0), (0, padded - hidden)))]

    mixer_pack = jnp.concatenate([mixer_project.reshape(depth, -1), mixer_output.T], axis=1)
    first_pack = jnp.concatenate(
        pack_ffn(first_gateup, first_down) + [attend_project, attend_output.T], axis=1
    )
    second_pack = jnp.concatenate(pack_ffn(second_gateup, second_down), axis=1)
    piece_table = deal_order.reshape(shards, shards, piece_rows)[:, :, 0]
    anchor = piece_table // row_count
    anchor_piece = piece_table % row_count // piece_rows
    send_piece = jnp.sum(jnp.where(anchor == device, anchor_piece, 0), axis=1)
    my_anchor = lax.dynamic_index_in_dim(anchor, device, 0, keepdims=False)
    gains_row = jnp.concatenate(
        [mixer_gain, first_gain, attend_gain, second_gain, jnp.zeros((width - 4 * depth,), BF16)]
    )

    def my_part(rows):
        parts = rows.reshape(shards, members, part_rows, width)
        return lax.dynamic_index_in_dim(parts, own, 1, keepdims=False)[send_piece]

    outgoing = jnp.concatenate(
        [
            my_part(hidden_in),
            my_part(cotangent),
            jnp.broadcast_to(gains_row, (shards, 1, width)),
        ],
        axis=1,
    )
    arrived = lax.all_to_all(outgoing, TOKEN_AXES, split_axis=0, concat_axis=0, tiled=True)
    arrived, mixer_pack, first_pack = lax.optimization_barrier((arrived, mixer_pack, first_pack))
    first_all = lax.all_gather(first_pack, TOKEN_AXES, axis=0, tiled=True)
    second_all = lax.all_gather(second_pack, TOKEN_AXES, axis=0, tiled=True)
    project_b = first_all[:, ffn_width : ffn_width + attend_project.shape[1]]
    output_b_t = first_all[:, ffn_width + attend_project.shape[1] :]
    mixer_all = gather_pack(mixer_pack)
    project_a = mixer_all[:, : 3 * channels]
    output_a_t = mixer_all[:, 3 * channels :]
    gains = (
        arrived[:, 2 * part_rows, : 4 * depth]
        .reshape(shards, 4, depth)
        .transpose(1, 0, 2)
        .reshape(4, width)
        .astype(F32)
    )
    gain_a, gain_f, gain_b, gain_s = gains[0], gains[1], gains[2], gains[3]
    parts = arrived[:, : 2 * part_rows][my_anchor]
    own_tokens = parts[:, :part_rows].reshape(chunk, width)
    own_back = parts[:, part_rows:].reshape(chunk, width)
    stream0 = own_tokens.astype(F32)
    upstream = own_back.astype(F32)
    both = tp_gather(jnp.concatenate([own_tokens, own_back]))
    back_s_chunks = [slot[chunk:] for slot in both]

    gathered = jnp.arange(row_count)
    member_of = (own - gathered // chunk) % members
    offsets = (
        gathered % chunk // part_rows * piece_rows + member_of * part_rows + gathered % part_rows
    )
    to_gathered = (offsets[:, None] == gathered[None, :]).astype(BF16)
    to_dealt = (offsets[None, :] == gathered[:, None]).astype(BF16)
    tokens = times(to_dealt, jnp.concatenate([slot[:chunk] for slot in both]))

    kernel_taps = mixer_kernel.shape[0]
    halo = kernel_taps - 1
    local_rows = device * row_count + jnp.arange(row_count)
    halo_segment, unused = locate(
        seq_lengths, local_rows[0] - halo + jnp.arange(row_count + halo)
    )
    segment, places = locate(seq_lengths, device * row_count + offsets)
    ctx = lax.axis_index(CTX_AXES)
    group_rows = jnp.concatenate(
        [
            (lax.axis_index(GROUP_AXES) * contexts + (ctx ^ mask)) * row_count + offsets
            for mask in range(contexts)
        ]
    )
    key_segment, key_places = locate(seq_lengths, group_rows)
    allowed = (segment[None, :] == key_segment[:, None]) & (key_places[:, None] <= places[None, :])
    barred = jnp.where(allowed, 0.0, NEGATIVE).astype(BF16)
    half_dim = HD // 2
    frequency = ROPE_BASE ** (-(jnp.arange(half_dim).astype(F32) * 2.0 / HD))
    angles = places.astype(F32)[:, None] * frequency[None, :]
    cosine = jnp.cos(angles)
    sine = jnp.sin(angles)

    kernel_local = lax.dynamic_slice_in_dim(mixer_kernel, own * channels, channels, 1).astype(F32)
    mixer_in = norm_rows(tokens, gain_a).astype(BF16)
    mixer_in_other = swap_core(mixer_in)
    halo_pad = 16
    halo_in = from_behind(mixer_in[row_count - halo_pad :], 1)
    proj_a = times(jnp.concatenate([halo_in, mixer_in]), project_a)
    proj_b_part = proj_a[:, :channels]
    proj_c_part = proj_a[halo_pad:, channels : 2 * channels]
    proj_x_part = proj_a[:, 2 * channels :]
    extended = (proj_b_part * proj_x_part)[halo_pad - halo :].astype(BF16).astype(F32)
    conv_out = shortconv(extended, kernel_local, halo_segment)
    gated_rows = (proj_c_part * conv_out).astype(BF16)
    gated_parts = arrange(to_gathered, gated_rows)
    stream1, normed = add_norm(
        tp_scatter(tp_chunks(times_t(gated_parts, output_a_t))), stream0, gain_f
    )

    normed_f = tp_gather(normed)
    stream2, normed = add_norm(
        tp_scatter(ffn_forward(normed_f, first_all, steps)), stream1, gain_b
    )

    groups = H // KVH
    score_scale = HD ** (-0.5)
    qgain_f = query_gain.astype(F32)[None]
    kgain_f = key_gain.astype(F32)[None]
    attend_in = jnp.concatenate(tp_gather(normed))
    proj_b = times(attend_in, project_b)
    kv_width = 2 * HD * (proj_b.shape[1] // (HD * (groups + 2)))
    query_b, key_value = one_step(
        functools.partial(heads_kernel, groups),
        [proj_b, cosine, sine, qgain_f, kgain_f],
        [
            jax.ShapeDtypeStruct((row_count, heads_width), BF16),
            jax.ShapeDtypeStruct((row_count, kv_width), BF16),
        ],
        SMALL_LIMIT,
        "heads",
        20 * proj_b.size,
    )
    key_value_z = swap_ctx(key_value, 2)
    key_value_core = swap_core(jnp.concatenate([key_value, key_value_z]))
    key_value_all = jnp.concatenate(
        [key_value, key_value_core[:row_count], key_value_z, key_value_core[row_count:]]
    )
    attend_flops = 2 * key_value_all.shape[0] * query_b.size
    (attended,) = one_step(
        functools.partial(attend_kernel, score_scale, HD),
        [query_b, key_value_all, barred],
        [jax.ShapeDtypeStruct(query_b.shape, BF16)],
        MIDDLE_LIMIT,
        "attend",
        2 * attend_flops,
    )
    stream3, normed = add_norm(
        tp_scatter(tp_chunks(times_t(attended, output_b_t))), stream2, gain_s
    )

    normed_s = tp_gather(normed)
    d_chunks, out_chunks, keep, side = ffn_backward(
        core_ref, normed_s, back_s_chunks, second_all, steps, True
    )
    d_stream3, back_b, gain_s_grad = norm_backward(
        tp_scatter(d_chunks), stream3, gain_s, upstream
    )
    out_others = [shift_tp(out_chunks[k], -k) for k in range(1, members)]
    side_other = swap_core(side)
    ffn_lefts = [(side, 0), (side_other, 0), (side, 1), (side_other, 1)]
    ffn_cols = steps * block
    side_start = 2 * width // block
    partial = gradient(
        ffn_lefts, keep, side_other, side_start, block, steps, padded, width, ffn_cols, 0, None
    )

    back_b = tp_gather(back_b)
    back_b, partial = lax.optimization_barrier((back_b, partial))
    second_sums = sum_chips(partial)
    back_b = jnp.concatenate(back_b)
    back_b_other = swap_core(back_b)
    attend_in_other = swap_core(attend_in)
    d_attended_b = times(back_b, output_b_t).astype(BF16)
    pair_rows = 2 * row_count
    d_query, near, cross, qgain_grad = one_step(
        functools.partial(attend_backward_kernel, score_scale),
        [query_b, d_attended_b, key_value_all, barred, proj_b, cosine, sine, qgain_f],
        [
            jax.ShapeDtypeStruct(query_b.shape, BF16),
            jax.ShapeDtypeStruct((pair_rows, kv_width), F32),
            jax.ShapeDtypeStruct((pair_rows, kv_width), BF16),
            jax.ShapeDtypeStruct((1, HD), F32),
        ],
        MIDDLE_LIMIT,
        "attend_backward",
        5 * attend_flops,
    )
    cross = swap_core(cross)
    far = (near[row_count:] + cross[row_count:].astype(F32)).astype(BF16)
    d_proj_b, kgain_grad = one_step(
        functools.partial(assemble_kernel, groups),
        [d_query, near, cross, swap_ctx(far, 2), proj_b, cosine, sine, kgain_f],
        [jax.ShapeDtypeStruct(proj_b.shape, BF16), jax.ShapeDtypeStruct((1, HD), F32)],
        SMALL_LIMIT,
        "assemble",
        20 * proj_b.size,
    )
    d_stream2, back_f, gain_b_grad = norm_backward(
        tp_scatter(tp_chunks(times_t(d_proj_b, project_b))), stream2, gain_b, d_stream3
    )
    keep, send = halves(d_proj_b, attended)
    first_core = core == 0
    attend_cols = keep.shape[1]
    small_tile = 2 * (heads_width + attend_project.shape[1]) // 16
    third = gradient(
        [
            (attend_in, 0),
            (attend_in_other, 0),
            (jnp.where(first_core, attend_in, back_b), 0),
            (jnp.where(first_core, attend_in_other, back_b_other), 0),
        ],
        keep,
        swap_core(send),
        0,
        small_tile,
        attend_cols // small_tile,
        attend_project.shape[1] - attend_cols,
        width,
        ffn_cols + attend_cols,
        ffn_cols // small_tile,
        None,
    )

    back_f = tp_gather(back_f)
    back_f, third = lax.optimization_barrier((back_f, third))
    left_x, left_b = jnp.concatenate(normed_f), jnp.concatenate(back_f)
    left_others = [swap_core(left_x), swap_core(left_b)]
    d_chunks, unused, keep, side = ffn_backward(
        core_ref, normed_f, back_f, first_all, steps, False
    )
    d_chunks, left_others = lax.optimization_barrier((d_chunks, left_others))
    d_chunks, side_other = lax.optimization_barrier((d_chunks, swap_core(side)))
    ffn_lefts = [(left_x, 0), (left_others[0], 0), (left_b, 0), (left_others[1], 0)]
    partial = gradient(
        ffn_lefts,
        keep,
        side_other,
        0,
        block,
        steps,
        padded,
        width,
        ffn_cols + attend_cols,
        0,
        third,
    )

    d_parts, partial = lax.optimization_barrier((tp_scatter(d_chunks), partial))
    d_stream1, back_a, gain_f_grad = norm_backward(d_parts, stream1, gain_f, d_stream2)

    back_a = tp_gather(back_a)
    first_sums = sum_chips(partial)
    back_a = arrange(to_dealt, jnp.concatenate(back_a))
    back_a_other = swap_core(back_a)
    d_gated = times(back_a, output_a_t)
    d_cgate = d_gated * conv_out
    d_conv = d_gated * proj_c_part
    unused, pullback = jax.vjp(
        lambda ext_rows, kernel_in: shortconv(ext_rows, kernel_in, halo_segment),
        extended,
        kernel_local,
    )
    d_extended, kernel_grad = pullback(d_conv)
    returned = from_behind(d_extended[:halo], -1)
    d_product = d_extended[halo:] + jnp.concatenate(
        [jnp.zeros((row_count - halo, channels), F32), returned]
    )
    d_proj_a = jnp.concatenate(
        [
            d_product * proj_x_part[halo_pad:],
            d_cgate,
            d_product * proj_b_part[halo_pad:],
        ],
        axis=1,
    ).astype(BF16)
    d_proj_a, out_others = lax.optimization_barrier((d_proj_a, out_others))
    stream4 = stream3 + add_parts([out_chunks[0], *out_others])
    d_chunks = tp_chunks(times_t(arrange(to_gathered, d_proj_a), project_a))
    keep, send = halves(d_proj_a, gated_rows)
    mixer_cols = keep.shape[1]
    partial = gradient(
        [
            (mixer_in, 0),
            (mixer_in_other, 0),
            (jnp.where(first_core, mixer_in, back_a), 0),
            (jnp.where(first_core, mixer_in_other, back_a_other), 0),
        ],
        keep,
        swap_core(send),
        0,
        mixer_cols,
        1,
        3 * channels - mixer_cols,
        width,
        mixer_cols,
        0,
        None,
    )
    kernel_cols = kernel_taps * channels
    gain_start = kernel_cols + 2 * HD
    shared = jnp.concatenate([kernel_grad.reshape(-1), qgain_grad[0], kgain_grad[0]])
    early_gains = [
        grad.reshape(shards, depth) for grad in (gain_f_grad, gain_b_grad, gain_s_grad)
    ]
    early_row = jnp.concatenate(
        [
            jnp.broadcast_to(shared, (shards, gain_start)),
            jnp.pad(
                jnp.concatenate(early_gains, axis=1),
                ((0, 0), (0, width - gain_start - 3 * depth)),
            ),
        ],
        axis=1,
    )
    d_parts, early_row = lax.optimization_barrier((tp_scatter(d_chunks), early_row))
    unused, d_stream0, gain_a_grad = norm_backward(d_parts, stream0, gain_a, d_stream1)

    slot_for_anchor = jnp.sum(
        jnp.where(
            my_anchor[None, :] == jnp.arange(shards)[:, None], jnp.arange(shards)[None, :], 0
        ),
        axis=1,
    )
    late_start = gain_start + 3 * depth
    late_row = jnp.pad(
        gain_a_grad.reshape(shards, depth), ((0, 0), (late_start, width - late_start - depth))
    )
    leaving = jnp.concatenate(
        [d_stream0, stream4.astype(BF16), (early_row + late_row).astype(BF16)]
    )
    line = jnp.arange(shards * piece_rows)
    target, item = line // piece_rows, line % piece_rows
    source = jnp.where(
        item < 2 * part_rows,
        item // part_rows * chunk
        + jnp.repeat(slot_for_anchor, piece_rows) * part_rows
        + item % part_rows,
        jnp.where(item == 2 * part_rows, 2 * chunk + target, -1),
    )
    to_leaving = (source[:, None] == jnp.arange(leaving.shape[0])[None, :]).astype(BF16)
    leaving = arrange(to_leaving, leaving)
    home = lax.all_to_all(
        leaving.reshape(shards, piece_rows, width),
        TOKEN_AXES,
        split_axis=0,
        concat_axis=0,
        tiled=True,
    )
    second_grads = finish(second_sums, steps, hidden)
    home, partial, second_grads = lax.optimization_barrier((home, partial, second_grads))
    place = jnp.arange(2 * chunk + 8)
    small_line = (place == 2 * chunk) | (place == 2 * chunk + 1)
    wanted = (
        place % chunk // part_rows * piece_rows
        + place // chunk * part_rows
        + place % part_rows
    )
    to_payload = jnp.where(
        (place < 2 * chunk)[:, None],
        wanted[:, None] == line[None, :],
        small_line[:, None] & (item == 2 * part_rows)[None, :],
    ).astype(BF16)
    payload = times(to_payload, home.reshape(shards * piece_rows, width))
    rounded = payload.astype(BF16).astype(F32)
    payload = jnp.where((place == 2 * chunk + 1)[:, None], payload - rounded, payload)
    last = tp_gather(payload.astype(BF16))
    mixer_home = lax.all_to_all(
        partial.reshape(shards, depth, mixer_cols),
        TOKEN_AXES,
        split_axis=0,
        concat_axis=0,
        tiled=True,
    )
    home_rows = (
        jnp.repeat(jnp.tile(send_piece, members), part_rows) * piece_rows
        + member_of * part_rows
        + gathered % part_rows
    )
    to_arrival = (home_rows[None, :] == gathered[:, None]).astype(BF16)
    input_gradient = arrange(to_arrival, jnp.concatenate([slot[:chunk] for slot in last]))
    layer_out = arrange(to_arrival, jnp.concatenate([slot[chunk : 2 * chunk] for slot in last]))
    first_sums, layer_out, input_gradient = lax.optimization_barrier(
        (first_sums, layer_out, input_gradient)
    )
    *first_grads, attend_grads = finish(first_sums, steps, hidden)
    first_grads, attend_grads, mixer_home = lax.optimization_barrier(
        (first_grads, attend_grads, mixer_home)
    )
    mixer_home = mixer_home.reshape(shards // CORES, CORES, depth, mixer_cols)
    mixer_grads = jnp.sum(mixer_home.astype(F32), axis=0)
    mixer_grads = jnp.concatenate([mixer_grads[0], mixer_grads[1]], axis=1)
    smalls = [
        slot[2 * chunk].astype(F32) + slot[2 * chunk + 1].astype(F32) for slot in last
    ]
    totals = sum(smalls)
    kernel_rows = jnp.stack([small[:kernel_cols].reshape(kernel_taps, channels) for small in smalls])
    kernel_total = jnp.concatenate(
        [
            lax.dynamic_index_in_dim(kernel_rows, (own - member) % members, 0, keepdims=False)
            for member in range(members)
        ],
        axis=1,
    )
    qgain_total = totals[kernel_cols : kernel_cols + HD]
    kgain_total = totals[kernel_cols + HD : kernel_cols + 2 * HD]
    gain_totals = totals[gain_start : gain_start + 4 * depth].reshape(4, depth)

    gateup_s_grad, down_s_grad = second_grads
    gateup_f_grad, down_f_grad = first_grads
    proj_cols = attend_project.shape[1]
    return (
        layer_out,
        input_gradient,
        gain_totals[3],
        mixer_grads[:, : 3 * channels].reshape(depth, 3, channels),
        kernel_total,
        mixer_grads[:, 3 * channels :].T,
        gain_totals[0],
        gateup_f_grad,
        down_f_grad.T,
        gain_totals[1],
        attend_grads[:, :proj_cols],
        qgain_total,
        kgain_total,
        attend_grads[:, proj_cols:].T,
        gain_totals[2],
        gateup_s_grad,
        down_s_grad.T,
    )


def solution(mesh):
    names = TOKEN_AXES + ("tp",)
    rings = mesh.shape["fsdp"] // 2, 2, mesh.shape["ctx"] // 2, 2, mesh.shape["tp"]
    tokens = P(TOKEN_AXES, None)
    rows = P(TOKEN_AXES)
    three = P(TOKEN_AXES, None, "tp")
    two = P(TOKEN_AXES, "tp")
    turned = P("tp", TOKEN_AXES)
    return jax.shard_map(
        body,
        mesh=Mesh(mesh.devices.reshape(rings), names),
        in_specs=(
            tokens, tokens, P(), P(),
            rows, three, P(), turned,
            rows, three, turned,
            rows, two, P(), P(), turned,
            rows, three, turned,
        ),
        out_specs=(
            tokens, tokens,
            rows, three, P(), turned,
            rows, three, turned,
            rows, two, P(), P(), turned,
            rows, three, turned,
        ),
        check_vma=False,
    )
```

profile of v0, /device:TPU:23, one launch (start us, length us, event | category | flops | bytes accessed | tf_op | source)
XLA Modules:
  0.0 511.0 jit_solution(12953416016323724409)
XLA Ops:
  14.3 8.8 %all-to-all-start = ((bf16[32,5,1536]{2,1,0:T(8,128)(2,1)}), bf16[32,5,1536]{2,1,0:T(8,128)(2,1)S(1)}, u32[]{:S(2)}, u32[]{:S(2)}) async-start(bf16[32,5,1536]{2,1,0:T(8,128)(2,1)} %pad_maximum_fusion), calls=%async_computation | async-start | bytes 1572864 | tf_op jit(solution)/shard_map/all_to_all | solution.py:698
  25.2 10.0 %all-to-all-done = bf16[32,5,1536]{2,1,0:T(8,128)(2,1)S(1)} async-done(((bf16[32,5,1536]{2,1,0:T(8,128)(2,1)}), bf16[32,5,1536]{2,1,0:T(8,128)(2,1)S(1)}, u32[]{:S(2)}, u32[]{:S(2)}) %all-to-all-start) | async-done | bytes 491552 | tf_op jit(solution)/shard_map/all_to_all | solution.py:698
  45.9 5.9 %all-to-all-start.1 = ((bf16[16,48,1536]{2,1,0:T(8,128)(2,1)}), bf16[16,48,1536]{2,1,0:T(8,128)(2,1)S(1)}, u32[]{:S(2)}, u32[]{:S(2)}) async-start(bf16[16,48,1536]{2,1,0:T(8,128)(2,1)} %broadcast_in_dim.85), calls=%async_computation.1 | async-start | bytes 4718592 | tf_op jit(solution)/shard_map/all_to_all | solution.py:550
  55.4 2.6 collective-permute-start.1
  67.2 23.2 %all-to-all-done.1 = bf16[16,48,1536]{2,1,0:T(8,128)(2,1)S(1)} async-done(((bf16[16,48,1536]{2,1,0:T(8,128)(2,1)}), bf16[16,48,1536]{2,1,0:T(8,128)(2,1)S(1)}, u32[]{:S(2)}, u32[]{:S(2)}) %all-to-all-start.1) | async-done | bytes 2359328 | tf_op jit(solution)/shard_map/all_to_all | solution.py:550
  105.0 2.4 collective-permute-start.6
  112.5 5.3 %collective-permute-done.7.refs_3_ = bf16[64,1536]{1,0:T(8,128)(2,1)S(1)} collective-permute-done((bf16[64,1536]{1,0:T(8,128)(2,1)}, bf16[64,1536]{1,0:T(8,128)(2,1)S(1)}, u32[]{:S(2)}, u32[]{:S(2)}) %collective-permute-start.7) | collective-permute-done | bytes 196640 | tf_op jit(solution)/shard_map/ppermute | solution.py:77
  125.6 5.1 collective-permute-done.9.refs_2_
  130.6 7.0 %all-gather.3.cloned.1.call-done.refs_4_.refs_5_.refs_8_.refs_9_ = bf16[1536,6400]{1,0:T(8,128)(2,1)} async-done(((bf16[48,6400]{1,0:T(8,128)(2,1)}), bf16[1536,6400]{1,0:T(8,128)(2,1)}) %all-gather.3.cloned.1.call-update) | async-done | bytes 19660816 | tf_op jit(solution)/shard_map/all_gather | solution.py:700
  137.6 11.2 %ffn_forward.1 = (f32[64,1536]{1,0:T(8,128)S(1)}, bf16[64,1536]{1,0:T(8,128)(2,1)}, bf16[64,1536]{1,0:T(8,128)(2,1)}, bf16[64,1536]{1,0:T(8,128)(2,1)}) custom-call(bf16[64,1536]{1,0:T(8,128)(2,1)S(1)} %get-tuple-element.118.refs_0_, bf16[64,1536]{1,0:T(8,128)(2,1)S(1)} %collective-permute-done.8.refs_1_, ...), custom_call_target="tpu_custom_call" | custom-call | flops 4227858432 | bytes 16515072 | tf_op jit(solution)/shard_map/ffn_forward/pallas_call | solution.py:239
  149.1 2.4 collective-permute-start.12
  152.1 3.2 collective-permute-done.11.refs_1_
  156.9 5.1 collective-permute-done.13.refs_3_
  162.2 2.4 collective-permute-start.15
  168.3 5.3 %collective-permute-done.15 = bf16[64,1536]{1,0:T(8,128)(2,1)S(1)} collective-permute-done((bf16[64,1536]{1,0:T(8,128)(2,1)S(1)}, bf16[64,1536]{1,0:T(8,128)(2,1)S(1)}, u32[]{:S(2)}, u32[]{:S(2)}) %collective-permute-start.15) | collective-permute-done | bytes 196640 | tf_op jit(solution)/shard_map/ppermute | solution.py:77
  176.6 2.5 heads.1
  179.9 7.0 %collective-permute-done.17 = bf16[256,256]{1,0:T(8,128)(2,1)S(1)} collective-permute-done((bf16[256,256]{1,0:T(8,128)(2,1)S(1)}, bf16[256,256]{1,0:T(8,128)(2,1)S(1)}, u32[]{:S(2)}, u32[]{:S(2)}) %collective-permute-start.17) | collective-permute-done | bytes 131104 | tf_op jit(solution)/shard_map/ppermute | solution.py:68
  186.9 2.8 collective-permute-start.18
  190.9 5.3 %attend.1 = bf16[256,384]{1,0:T(8,128)(2,1)S(1)} custom-call(bf16[256,384]{1,0:T(8,128)(2,1)S(1)} %get-tuple-element.126.q_ref, bf16[1024,256]{1,0:T(8,128)(2,1)S(1)} %pad_maximum_fusion.2.kv_ref, bf16[1024,256]{1,0:T(8,128)(2,1)S(1)} %select_convert_fusion.barred_ref), custom_call_target="tpu_custom_call" | custom-call | flops 402653184 | bytes 1441792 | tf_op jit(solution)/shard_map/attend/pallas_call | solution.py:137
  196.2 3.1 fusion.141
  201.7 3.2 collective-permute-start.20
  209.8 5.0 collective-permute-done.21.refs_3_
  225.5 5.0 collective-permute-done.23.refs_2_
  235.0 15.2 %ffn_both.1 = (f32[64,1536]{1,0:T(8,128)S(1)}, bf16[64,1536]{1,0:T(8,128)(2,1)S(1)}, bf16[64,1536]{1,0:T(8,128)(2,1)S(1)}, bf16[64,1536]{1,0:T(8,128)(2,1)S(1)},...) custom-call(s32[1]{0:T(128)} %bitcast.core_ref, ...), custom_call_target="tpu_custom_call" | custom-call | flops 8455716864 | bytes 22413312 | tf_op jit(solution)/shard_map/ffn_both/pallas_call | solution.py:329
  253.8 3.3 collective-permute-start.26
  257.0 3.4 collective-permute-done.25.refs_1_
  262.1 4.5 collective-permute-done.27.refs_3_
  277.1 10.4 %weight_gradient.4 = bf16[1536,2688]{1,0:T(8,128)(2,1)} custom-call(bf16[256,5760]{1,0:T(8,128)(2,1)S(1)} %copy-done, bf16[256,5760]{1,0:T(8,128)(2,1)} %copy-done.50, bf16[256,5760]{1,0:T(8,128)(2,1)S(1)} %copy-done, bf16[256,5760]{1,0:T(8,128)(2,1)} %copy-done.50, bf16[256,2688]{1,0:T(8,128)(2,1)S(1)} %get-tuple-element.137.refs_4_, ...), custom_call_target="tpu_custom_call" | custom-call | flops 4227858432 | bytes 8257536 | tf_op jit(solution)/shard_map/weight_gradient/pallas_call | solution.py:398
  293.4 7.8 %attend_backward.1 = (bf16[256,384]{1,0:T(8,128)(2,1)S(1)}, f32[512,256]{1,0:T(8,128)S(1)}, bf16[512,256]{1,0:T(8,128)(2,1)S(1)}, f32[1,64]{1,0:T(1,128)S(1)}) custom-call(bf16[256,384]{1,0:T(8,128)(2,1)S(1)} %copy-done.48, bf16[256,384]{1,0:T(8,128)(2,1)S(1)} %convolution_convert_fusion.5.do_ref, bf16[1024,256]{1,0:T(8,128)(2,1)S(1)} %copy-done.24, ...), custom_call_target="tpu_custom_call" | custom-call | flops 1006632960 | bytes 3146240 | tf_op jit(solution)/shard_map/attend_backward/pallas_call | solution.py:137
  304.3 7.0 %collective-permute-done.33.far_ref = bf16[256,256]{1,0:T(8,128)(2,1)S(1)} collective-permute-done((bf16[256,256]{1,0:T(8,128)(2,1)S(1)}, bf16[256,256]{1,0:T(8,128)(2,1)S(1)}, u32[]{:S(2)}, u32[]{:S(2)}) %collective-permute-start.33) | collective-permute-done | bytes 131104 | tf_op jit(solution)/shard_map/ppermute | solution.py:68
  319.8 4.5 collective-permute-start.43
  330.5 3.7 weight_gradient.5.refs_6_
  334.2 3.6 collective-permute-done.38.refs_6_
  339.0 14.1 %ffn_backward.1 = (f32[64,1536]{1,0:T(8,128)S(1)}, bf16[64,1536]{1,0:T(8,128)(2,1)}, bf16[64,1536]{1,0:T(8,128)(2,1)}, bf16[64,1536]{1,0:T(8,128)(2,1)S(1)}, bf1...) custom-call(s32[1]{0:T(128)} %bitcast.core_ref, bf16[64,1536]{1,0:T(8,128)(2,1)S(1)} %get-tuple-element.118.refs_0_, ...), custom_call_target="tpu_custom_call" | custom-call | flops 7046430720 | bytes 19267584 | tf_op jit(solution)/shard_map/ffn_backward/pallas_call | solution.py:329
  354.9 3.7 collective-permute-done.44.refs_3_
  362.4 8.7 %weight_gradient.6 = bf16[1536,3200]{1,0:T(8,128)(2,1)} custom-call(bf16[256,1536]{1,0:T(8,128)(2,1)S(1)} %constant_dynamic-update-slice_fusion.10.refs_0_, bf16[256,1536]{1,0:T(8,128)(2,1)S(1)} %collective-permute-done.43.refs_1_, bf16[256,1536]{1,0:T(8,128)(2,1)S(1)} %constant_dynamic-update-slice_fusion.14.refs_2_, ...), custom_call_target="tpu_custom_call", output_to_operand_aliasing={{}: (6, {})} | custom-call | flops 4227858432 | bytes 8257536 | tf_op jit(solution)/shard_map/weight_gradient/pallas_call | solution.py:398
  384.0 7.0 %collective-permute-start.54 = (bf16[64,1536]{1,0:T(8,128)(2,1)}, bf16[64,1536]{1,0:T(8,128)(2,1)}, u32[]{:S(2)}, u32[]{:S(2)}) collective-permute-start(bf16[64,1536]{1,0:T(8,128)(2,1)} %copy-done.45), channel_id=1, source_target_pairs={{0,2},{1,3},{2,0},{3,1},{4,6},{5,7},{6,4},{7,5},{8,10},{9,11},{10,... | collective-permute-start | bytes 589832 | tf_op jit(solution)/shard_map/ppermute | solution.py:77
  393.4 3.0 multiply_reduce_fusion.3
  397.5 3.4 collective-permute-start.52
  404.1 4.8 fusion.143
  417.6 5.3 %collective-permute-done.58.refs_3_ = bf16[64,1536]{1,0:T(8,128)(2,1)S(1)} collective-permute-done((bf16[64,1536]{1,0:T(8,128)(2,1)S(1)}, bf16[64,1536]{1,0:T(8,128)(2,1)S(1)}, u32[]{:S(2)}, u32[]{:S(2)}) %collective-permute-start.58) | collective-permute-done | bytes 196640 | tf_op jit(solution)/shard_map/ppermute | solution.py:77
  428.1 7.7 %all-to-all-start.2 = ((bf16[32,8,1536]{2,1,0:T(8,128)(2,1)}), bf16[32,8,1536]{2,1,0:T(8,128)(2,1)}, u32[]{:S(2)}, u32[]{:S(2)}) async-start(bf16[32,8,1536]{2,1,0:T(8,128)(2,1)} %fusion.4), calls=%async_computation.3 | async-start | bytes 1572864 | tf_op jit(solution)/shard_map/all_to_all | solution.py:1004
  438.6 3.3 weight_gradient.7
  443.0 5.5 %all-to-all-done.2 = bf16[32,8,1536]{2,1,0:T(8,128)(2,1)} async-done(((bf16[32,8,1536]{2,1,0:T(8,128)(2,1)}), bf16[32,8,1536]{2,1,0:T(8,128)(2,1)}, u32[]{:S(2)}, u32[]{:S(2)}) %all-to-all-start.2) | async-done | bytes 786464 | tf_op jit(solution)/shard_map/all_to_all | solution.py:1004
  454.0 6.6 %all-to-all-start.3 = ((bf16[32,48,768]{2,1,0:T(8,128)(2,1)}), bf16[32,48,768]{2,1,0:T(8,128)(2,1)S(1)}, u32[]{:S(2)}, u32[]{:S(2)}) async-start(bf16[32,48,768]{2,1,0:T(8,128)(2,1)} %bitcast.101), calls=%async_computation.5 | async-start | bytes 4718592 | tf_op jit(solution)/shard_map/all_to_all | solution.py:1029
  462.4 8.9 %collective-permute-done.64 = bf16[136,1536]{1,0:T(8,128)(2,1)S(1)} collective-permute-done((bf16[136,1536]{1,0:T(8,128)(2,1)}, bf16[136,1536]{1,0:T(8,128)(2,1)S(1)}, u32[]{:S(2)}, u32[]{:S(2)}) %collective-permute-start.64) | collective-permute-done | bytes 417824 | tf_op jit(solution)/shard_map/ppermute | solution.py:77
  478.6 13.4 %reduce-scatter.3.cloned.1.call-done.sum_ref = bf16[96,3200]{1,0:T(8,128)(2,1)} async-done(((bf16[1536,3200]{1,0:T(8,128)(2,1)}), bf16[96,3200]{1,0:T(8,128)(2,1)}) %reduce-scatter.3.cloned.1.call-update) | async-done | bytes 614416 | tf_op jit(solution)/shard_map/reduce_scatter | solution.py:544
  493.1 4.7 collective-permute-start.66
  (581 shorter events, 196.7 us)
Async XLA Ops:
  14.3 20.9 %all-to-all-start = ((bf16[32,5,1536]{2,1,0:T(8,128)(2,1)}), bf16[32,5,1536]{2,1,0:T(8,128)(2,1)S(1)}, u32[]{:S(2)}, u32[]{:S(2)}) async-start(bf16[32,5,1536]{2,1,0:T(8,128)(2,1)} %pad_maximum_fusion), calls=%async_computation | async-start | bytes 1572864 | tf_op jit(solution)/shard_map/all_to_all | solution.py:698
  23.2 114.5 %all-gather.3.cloned.1.call-start = ((), (), s32[]{:S(2)}) async-start(), calls=%async_computation.6 | async-start | bytes 20275200 | tf_op jit(solution)/shard_map/all_gather | solution.py:700
  35.3 188.4 %all-gather.5.cloned.1.call-start = ((), (), s32[]{:S(2)}) async-start(), calls=%async_computation.7 | async-start | bytes 17031168 | tf_op jit(solution)/shard_map/all_gather | solution.py:701
  45.9 44.5 %all-to-all-start.1 = ((bf16[16,48,1536]{2,1,0:T(8,128)(2,1)}), bf16[16,48,1536]{2,1,0:T(8,128)(2,1)S(1)}, u32[]{:S(2)}, u32[]{:S(2)}) async-start(bf16[16,48,1536]{2,1,0:T(8,128)(2,1)} %broadcast_in_dim.85), calls=%async_computation.1 | async-start | bytes 4718592 | tf_op jit(solution)/shard_map/all_to_all | solution.py:550
  51.7 384.1 %reduce-scatter.5.cloned.1.call-start = ((), (), s32[]{:S(2)}) async-start(), calls=%async_computation.9 | async-start | bytes 8773632 | tf_op jit(solution)/shard_map/reduce_scatter | solution.py:544
  54.7 10.7 %collective-permute-start.2 = (bf16[128,1536]{1,0:T(8,128)(2,1)}, bf16[128,1536]{1,0:T(8,128)(2,1)}, u32[]{:S(2)}, u32[]{:S(2)}) collective-permute-start(bf16[128,1536]{1,0:T(8,128)(2,1)} %get-tuple-element.331), channel_id=1, source_target_pairs={{0,3},{1,0},{2,1},{3,2},{4,7},{5,4},{6,5},{7,6},{8,11},{9,8},{10,9... | collective-permute-start | bytes 1179656 | tf_op jit(solution)/shard_map/ppermute | solution.py:77
  55.4 35.6 %collective-permute-start.1 = (bf16[128,1536]{1,0:T(8,128)(2,1)}, bf16[128,1536]{1,0:T(8,128)(2,1)}, u32[]{:S(2)}, u32[]{:S(2)}) collective-permute-start(bf16[128,1536]{1,0:T(8,128)(2,1)} %get-tuple-element.331), channel_id=1, source_target_pairs={{0,2},{1,3},{2,0},{3,1},{4,6},{5,7},{6,4},{7,5},{8,10},{9,11},{10,... | collective-permute-start | bytes 1179656 | tf_op jit(solution)/shard_map/ppermute | solution.py:77
  58.1 34.7 %collective-permute-start = (bf16[128,1536]{1,0:T(8,128)(2,1)}, bf16[128,1536]{1,0:T(8,128)(2,1)S(1)}, u32[]{:S(2)}, u32[]{:S(2)}) collective-permute-start(bf16[128,1536]{1,0:T(8,128)(2,1)} %get-tuple-element.331), channel_id=1, source_target_pairs={{0,1},{1,2},{2,3},{3,0},{4,5},{5,6},{6,7},{7,4},{8,9},{9,10},{10,1... | collective-permute-start | bytes 1179656 | tf_op jit(solution)/shard_map/ppermute | solution.py:77
  107.4 10.5 %collective-permute-start.7 = (bf16[64,1536]{1,0:T(8,128)(2,1)}, bf16[64,1536]{1,0:T(8,128)(2,1)S(1)}, u32[]{:S(2)}, u32[]{:S(2)}) collective-permute-start(bf16[64,1536]{1,0:T(8,128)(2,1)} %get-tuple-element.301), channel_id=1, source_target_pairs={{0,1},{1,2},{2,3},{3,0},{4,5},{5,6},{6,7},{7,4},{8,9},{9,10},{10,1... | collective-permute-start | bytes 589832 | tf_op jit(solution)/shard_map/ppermute | solution.py:77
  119.6 11.0 %collective-permute-start.9 = (bf16[64,1536]{1,0:T(8,128)(2,1)S(1)}, bf16[64,1536]{1,0:T(8,128)(2,1)S(1)}, u32[]{:S(2)}, u32[]{:S(2)}) collective-permute-start(bf16[64,1536]{1,0:T(8,128)(2,1)S(1)} %get-tuple-element.118.refs_0_), channel_id=1, source_target_pairs={{0,2},{1,3},{2,0},{3,1},{4,6},{5,7},{6,4},{7,5},{8,10},{9,11},{10,... | collective-permute-start | bytes 589832 | tf_op jit(solution)/shard_map/ppermute | solution.py:77
  151.5 10.4 %collective-permute-start.13 = (bf16[64,1536]{1,0:T(8,128)(2,1)}, bf16[64,1536]{1,0:T(8,128)(2,1)S(1)}, u32[]{:S(2)}, u32[]{:S(2)}) collective-permute-start(bf16[64,1536]{1,0:T(8,128)(2,1)} %get-tuple-element.123), channel_id=1, source_target_pairs={{0,1},{1,2},{2,3},{3,0},{4,5},{5,6},{6,7},{7,4},{8,9},{9,10},{10,1... | collective-permute-start | bytes 589832 | tf_op jit(solution)/shard_map/ppermute | solution.py:77
  162.2 11.4 %collective-permute-start.15 = (bf16[64,1536]{1,0:T(8,128)(2,1)S(1)}, bf16[64,1536]{1,0:T(8,128)(2,1)S(1)}, u32[]{:S(2)}, u32[]{:S(2)}) collective-permute-start(bf16[64,1536]{1,0:T(8,128)(2,1)S(1)} %get-tuple-element.125), channel_id=1, source_target_pairs={{0,2},{1,3},{2,0},{3,1},{4,6},{5,7},{6,4},{7,5},{8,10},{9,11},{10,... | collective-permute-start | bytes 589832 | tf_op jit(solution)/shard_map/ppermute | solution.py:77
  164.6 9.4 %collective-permute-start.16 = (bf16[64,1536]{1,0:T(8,128)(2,1)S(1)}, bf16[64,1536]{1,0:T(8,128)(2,1)S(1)}, u32[]{:S(2)}, u32[]{:S(2)}) collective-permute-start(bf16[64,1536]{1,0:T(8,128)(2,1)S(1)} %get-tuple-element.125), channel_id=1, source_target_pairs={{0,3},{1,0},{2,1},{3,2},{4,7},{5,4},{6,5},{7,6},{8,11},{9,8},{10,9... | collective-permute-start | bytes 589832 | tf_op jit(solution)/shard_map/ppermute | solution.py:77
  200.1 8.3 %collective-permute-start.19 = (bf16[64,1536]{1,0:T(8,128)(2,1)}, bf16[64,1536]{1,0:T(8,128)(2,1)}, u32[]{:S(2)}, u32[]{:S(2)}) collective-permute-start(bf16[64,1536]{1,0:T(8,128)(2,1)} %get-tuple-element.300), channel_id=1, source_target_pairs={{0,3},{1,0},{2,1},{3,2},{4,7},{5,4},{6,5},{7,6},{8,11},{9,8},{10,9... | collective-permute-start | bytes 589832 | tf_op jit(solution)/shard_map/ppermute | solution.py:77
  204.9 9.9 %collective-permute-start.21 = (bf16[64,1536]{1,0:T(8,128)(2,1)}, bf16[64,1536]{1,0:T(8,128)(2,1)}, u32[]{:S(2)}, u32[]{:S(2)}) collective-permute-start(bf16[64,1536]{1,0:T(8,128)(2,1)} %get-tuple-element.298), channel_id=1, source_target_pairs={{0,1},{1,2},{2,3},{3,0},{4,5},{5,6},{6,7},{7,4},{8,9},{9,10},{10,1... | collective-permute-start | bytes 589832 | tf_op jit(solution)/shard_map/ppermute | solution.py:77
  219.8 10.8 %collective-permute-start.23 = (bf16[64,1536]{1,0:T(8,128)(2,1)}, bf16[64,1536]{1,0:T(8,128)(2,1)}, u32[]{:S(2)}, u32[]{:S(2)}) collective-permute-start(bf16[64,1536]{1,0:T(8,128)(2,1)} %get-tuple-element.129.refs_0_), channel_id=1, source_target_pairs={{0,2},{1,3},{2,0},{3,1},{4,6},{5,7},{6,4},{7,5},{8,10},{9,11},{10,... | collective-permute-start | bytes 589832 | tf_op jit(solution)/shard_map/ppermute | solution.py:77
  221.6 9.7 %collective-permute-start.24 = (bf16[64,1536]{1,0:T(8,128)(2,1)}, bf16[64,1536]{1,0:T(8,128)(2,1)}, u32[]{:S(2)}, u32[]{:S(2)}) collective-permute-start(bf16[64,1536]{1,0:T(8,128)(2,1)} %get-tuple-element.129.refs_0_), channel_id=1, source_target_pairs={{0,3},{1,0},{2,1},{3,2},{4,7},{5,4},{6,5},{7,6},{8,11},{9,8},{10,9... | collective-permute-start | bytes 589832 | tf_op jit(solution)/shard_map/ppermute | solution.py:77
  251.0 22.6 %collective-permute-start.31 = (bf16[256,5760]{1,0:T(8,128)(2,1)}, bf16[256,5760]{1,0:T(8,128)(2,1)S(1)}, u32[]{:S(2)}, u32[]{:S(2)}) collective-permute-start(bf16[256,5760]{1,0:T(8,128)(2,1)} %get-tuple-element.136.refs_0_.refs_2_), channel_id=1, source_target_pairs={{0,4},{4,0},{1,5},{5,1},{2,6},{6,2},{3,7},{7,3},{8,12},{12,8},{9,1... | collective-permute-start | bytes 8847368 | tf_op jit(solution)/shard_map/ppermute | solution.py:72
  253.8 8.3 %collective-permute-start.26 = (bf16[64,1536]{1,0:T(8,128)(2,1)S(1)}, bf16[64,1536]{1,0:T(8,128)(2,1)S(1)}, u32[]{:S(2)}, u32[]{:S(2)}) collective-permute-start(bf16[64,1536]{1,0:T(8,128)(2,1)S(1)} %get-tuple-element.132), channel_id=1, source_target_pairs={{0,2},{1,3},{2,0},{3,1},{4,6},{5,7},{6,4},{7,5},{8,10},{9,11},{10,... | collective-permute-start | bytes 589832 | tf_op jit(solution)/shard_map/ppermute | solution.py:77
  257.0 9.6 %collective-permute-start.27 = (bf16[64,1536]{1,0:T(8,128)(2,1)S(1)}, bf16[64,1536]{1,0:T(8,128)(2,1)S(1)}, u32[]{:S(2)}, u32[]{:S(2)}) collective-permute-start(bf16[64,1536]{1,0:T(8,128)(2,1)S(1)} %get-tuple-element.133), channel_id=1, source_target_pairs={{0,1},{1,2},{2,3},{3,0},{4,5},{5,6},{6,7},{7,4},{8,9},{9,10},{10,1... | collective-permute-start | bytes 589832 | tf_op jit(solution)/shard_map/ppermute | solution.py:77
  269.0 18.5 %collective-permute-start.28 = (bf16[64,1536]{1,0:T(8,128)(2,1)}, bf16[64,1536]{1,0:T(8,128)(2,1)}, u32[]{:S(2)}, u32[]{:S(2)}) collective-permute-start(bf16[64,1536]{1,0:T(8,128)(2,1)} %get-tuple-element.138), channel_id=1, source_target_pairs={{0,1},{1,2},{2,3},{3,0},{4,5},{5,6},{6,7},{7,4},{8,9},{9,10},{10,1... | collective-permute-start | bytes 589832 | tf_op jit(solution)/shard_map/ppermute | solution.py:77
  269.8 17.7 %collective-permute-start.29 = (bf16[64,1536]{1,0:T(8,128)(2,1)}, bf16[64,1536]{1,0:T(8,128)(2,1)}, u32[]{:S(2)}, u32[]{:S(2)}) collective-permute-start(bf16[64,1536]{1,0:T(8,128)(2,1)} %get-tuple-element.138), channel_id=1, source_target_pairs={{0,2},{1,3},{2,0},{3,1},{4,6},{5,7},{6,4},{7,5},{8,10},{9,11},{10,... | collective-permute-start | bytes 589832 | tf_op jit(solution)/shard_map/ppermute | solution.py:77
  271.6 15.9 %collective-permute-start.30 = (bf16[64,1536]{1,0:T(8,128)(2,1)}, bf16[64,1536]{1,0:T(8,128)(2,1)}, u32[]{:S(2)}, u32[]{:S(2)}) collective-permute-start(bf16[64,1536]{1,0:T(8,128)(2,1)} %get-tuple-element.138), channel_id=1, source_target_pairs={{0,3},{1,0},{2,1},{3,2},{4,7},{5,4},{6,5},{7,6},{8,11},{9,8},{10,9... | collective-permute-start | bytes 589832 | tf_op jit(solution)/shard_map/ppermute | solution.py:77
  287.5 204.5 %reduce-scatter.3.cloned.1.call-start = ((), (), s32[]{:S(2)}) async-start(), calls=%async_computation.8 | async-start | bytes 10444800 | tf_op jit(solution)/shard_map/reduce_scatter | solution.py:544
  302.9 25.1 %collective-permute-start.40 = (bf16[256,1536]{1,0:T(8,128)(2,1)S(1)}, bf16[256,1536]{1,0:T(8,128)(2,1)S(1)}, u32[]{:S(2)}, u32[]{:S(2)}) collective-permute-start(bf16[256,1536]{1,0:T(8,128)(2,1)S(1)} %constant_dynamic-update-slice_fusion.2.refs_0_), channel_id=1, source_target_pairs={{0,4},{4,0},{1,5},{5,1},{2,6},{6,2},{3,7},{7,3},{8,12},{12,8},{9,1... | collective-permute-start | bytes 2359304 | tf_op jit(solution)/shard_map/ppermute | solution.py:72
  303.2 26.0 %collective-permute-start.41 = (bf16[256,1536]{1,0:T(8,128)(2,1)S(1)}, bf16[256,1536]{1,0:T(8,128)(2,1)S(1)}, u32[]{:S(2)}, u32[]{:S(2)}) collective-permute-start(bf16[256,1536]{1,0:T(8,128)(2,1)S(1)} %constant_dynamic-update-slice_fusion.6), channel_id=1, source_target_pairs={{0,4},{4,0},{1,5},{5,1},{2,6},{6,2},{3,7},{7,3},{8,12},{12,8},{9,1... | collective-permute-start | bytes 2359304 | tf_op jit(solution)/shard_map/ppermute | solution.py:72
  314.9 9.4 %collective-permute-start.35 = (bf16[64,1536]{1,0:T(8,128)(2,1)S(1)}, bf16[64,1536]{1,0:T(8,128)(2,1)S(1)}, u32[]{:S(2)}, u32[]{:S(2)}) collective-permute-start(bf16[64,1536]{1,0:T(8,128)(2,1)S(1)} %get-tuple-element.296), channel_id=1, source_target_pairs={{0,2},{1,3},{2,0},{3,1},{4,6},{5,7},{6,4},{7,5},{8,10},{9,11},{10,... | collective-permute-start | bytes 589832 | tf_op jit(solution)/shard_map/ppermute | solution.py:77
  316.1 10.7 %collective-permute-start.36 = (bf16[64,1536]{1,0:T(8,128)(2,1)S(1)}, bf16[64,1536]{1,0:T(8,128)(2,1)S(1)}, u32[]{:S(2)}, u32[]{:S(2)}) collective-permute-start(bf16[64,1536]{1,0:T(8,128)(2,1)S(1)} %get-tuple-element.295), channel_id=1, source_target_pairs={{0,1},{1,2},{2,3},{3,0},{4,5},{5,6},{6,7},{7,4},{8,9},{9,10},{10,1... | collective-permute-start | bytes 589832 | tf_op jit(solution)/shard_map/ppermute | solution.py:77
  319.8 35.1 %collective-permute-start.43 = (bf16[256,1536]{1,0:T(8,128)(2,1)S(1)}, bf16[256,1536]{1,0:T(8,128)(2,1)S(1)}, u32[]{:S(2)}, u32[]{:S(2)}) collective-permute-start(bf16[256,1536]{1,0:T(8,128)(2,1)S(1)} %constant_dynamic-update-slice_fusion.10.refs_0_), channel_id=1, source_target_pairs={{0,4},{4,0},{1,5},{5,1},{2,6},{6,2},{3,7},{7,3},{8,12},{12,8},{9,1... | collective-permute-start | bytes 2359304 | tf_op jit(solution)/shard_map/ppermute | solution.py:72
  328.0 9.8 %collective-permute-start.38 = (bf16[64,1536]{1,0:T(8,128)(2,1)S(1)}, bf16[64,1536]{1,0:T(8,128)(2,1)S(1)}, u32[]{:S(2)}, u32[]{:S(2)}) collective-permute-start(bf16[64,1536]{1,0:T(8,128)(2,1)S(1)} %get-tuple-element.148.refs_4_), channel_id=1, source_target_pairs={{0,2},{1,3},{2,0},{3,1},{4,6},{5,7},{6,4},{7,5},{8,10},{9,11},{10,... | collective-permute-start | bytes 589832 | tf_op jit(solution)/shard_map/ppermute | solution.py:77
  329.3 9.7 %collective-permute-start.39 = (bf16[64,1536]{1,0:T(8,128)(2,1)S(1)}, bf16[64,1536]{1,0:T(8,128)(2,1)S(1)}, u32[]{:S(2)}, u32[]{:S(2)}) collective-permute-start(bf16[64,1536]{1,0:T(8,128)(2,1)S(1)} %get-tuple-element.148.refs_4_), channel_id=1, source_target_pairs={{0,3},{1,0},{2,1},{3,2},{4,7},{5,4},{6,5},{7,6},{8,11},{9,8},{10,9... | collective-permute-start | bytes 589832 | tf_op jit(solution)/shard_map/ppermute | solution.py:77
  358.6 12.6 %collective-permute-start.46 = (bf16[64,1536]{1,0:T(8,128)(2,1)}, bf16[64,1536]{1,0:T(8,128)(2,1)S(1)}, u32[]{:S(2)}, u32[]{:S(2)}) collective-permute-start(bf16[64,1536]{1,0:T(8,128)(2,1)} %get-tuple-element.162), channel_id=1, source_target_pairs={{0,3},{1,0},{2,1},{3,2},{4,7},{5,4},{6,5},{7,6},{8,11},{9,8},{10,9... | collective-permute-start | bytes 589832 | tf_op jit(solution)/shard_map/ppermute | solution.py:77
  359.7 11.4 %collective-permute-start.47 = (bf16[64,1536]{1,0:T(8,128)(2,1)}, bf16[64,1536]{1,0:T(8,128)(2,1)S(1)}, u32[]{:S(2)}, u32[]{:S(2)}) collective-permute-start(bf16[64,1536]{1,0:T(8,128)(2,1)} %get-tuple-element.163), channel_id=1, source_target_pairs={{0,2},{1,3},{2,0},{3,1},{4,6},{5,7},{6,4},{7,5},{8,10},{9,11},{10,... | collective-permute-start | bytes 589832 | tf_op jit(solution)/shard_map/ppermute | solution.py:77
  362.0 10.5 %collective-permute-start.48 = (bf16[64,1536]{1,0:T(8,128)(2,1)S(1)}, bf16[64,1536]{1,0:T(8,128)(2,1)S(1)}, u32[]{:S(2)}, u32[]{:S(2)}) collective-permute-start(bf16[64,1536]{1,0:T(8,128)(2,1)S(1)} %get-tuple-element.164), channel_id=1, source_target_pairs={{0,1},{1,2},{2,3},{3,0},{4,5},{5,6},{6,7},{7,4},{8,9},{9,10},{10,1... | collective-permute-start | bytes 589832 | tf_op jit(solution)/shard_map/ppermute | solution.py:77
  377.6 13.4 %collective-permute-start.50 = (bf16[64,1536]{1,0:T(8,128)(2,1)}, bf16[64,1536]{1,0:T(8,128)(2,1)S(1)}, u32[]{:S(2)}, u32[]{:S(2)}) collective-permute-start(bf16[64,1536]{1,0:T(8,128)(2,1)} %get-tuple-element.176), channel_id=1, source_target_pairs={{0,2},{1,3},{2,0},{3,1},{4,6},{5,7},{6,4},{7,5},{8,10},{9,11},{10,... | collective-permute-start | bytes 589832 | tf_op jit(solution)/shard_map/ppermute | solution.py:77
  379.3 12.4 %collective-permute-start.51 = (bf16[64,1536]{1,0:T(8,128)(2,1)}, bf16[64,1536]{1,0:T(8,128)(2,1)}, u32[]{:S(2)}, u32[]{:S(2)}) collective-permute-start(bf16[64,1536]{1,0:T(8,128)(2,1)} %get-tuple-element.176), channel_id=1, source_target_pairs={{0,3},{1,0},{2,1},{3,2},{4,7},{5,4},{6,5},{7,6},{8,11},{9,8},{10,9... | collective-permute-start | bytes 589832 | tf_op jit(solution)/shard_map/ppermute | solution.py:77
  382.0 55.4 %collective-permute-start.59 = (bf16[256,1536]{1,0:T(8,128)(2,1)S(1)}, bf16[256,1536]{1,0:T(8,128)(2,1)S(1)}, u32[]{:S(2)}, u32[]{:S(2)}) collective-permute-start(bf16[256,1536]{1,0:T(8,128)(2,1)S(1)} %multiply_convert_fusion.refs_0_), channel_id=1, source_target_pairs={{0,4},{4,0},{1,5},{5,1},{2,6},{6,2},{3,7},{7,3},{8,12},{12,8},{9,1... | collective-permute-start | bytes 2359304 | tf_op jit(solution)/shard_map/ppermute | solution.py:72
  383.4 19.9 %collective-permute-start.53 = (bf16[64,1536]{1,0:T(8,128)(2,1)}, bf16[64,1536]{1,0:T(8,128)(2,1)}, u32[]{:S(2)}, u32[]{:S(2)}) collective-permute-start(bf16[64,1536]{1,0:T(8,128)(2,1)} %copy-done.46), channel_id=1, source_target_pairs={{0,3},{1,0},{2,1},{3,2},{4,7},{5,4},{6,5},{7,6},{8,11},{9,8},{10,9... | collective-permute-start | bytes 589832 | tf_op jit(solution)/shard_map/ppermute | solution.py:77
  384.0 19.3 %collective-permute-start.54 = (bf16[64,1536]{1,0:T(8,128)(2,1)}, bf16[64,1536]{1,0:T(8,128)(2,1)}, u32[]{:S(2)}, u32[]{:S(2)}) collective-permute-start(bf16[64,1536]{1,0:T(8,128)(2,1)} %copy-done.45), channel_id=1, source_target_pairs={{0,2},{1,3},{2,0},{3,1},{4,6},{5,7},{6,4},{7,5},{8,10},{9,11},{10,... | collective-permute-start | bytes 589832 | tf_op jit(solution)/shard_map/ppermute | solution.py:77
  391.1 12.3 %collective-permute-start.55 = (bf16[64,1536]{1,0:T(8,128)(2,1)S(1)}, bf16[64,1536]{1,0:T(8,128)(2,1)}, u32[]{:S(2)}, u32[]{:S(2)}) collective-permute-start(bf16[64,1536]{1,0:T(8,128)(2,1)S(1)} %copy-done.44), channel_id=1, source_target_pairs={{0,1},{1,2},{2,3},{3,0},{4,5},{5,6},{6,7},{7,4},{8,9},{9,10},{10,1... | collective-permute-start | bytes 589832 | tf_op jit(solution)/shard_map/ppermute | solution.py:77
  403.0 34.3 %collective-permute-start.60 = (bf16[256,1536]{1,0:T(8,128)(2,1)}, bf16[256,1536]{1,0:T(8,128)(2,1)}, u32[]{:S(2)}, u32[]{:S(2)}) collective-permute-start(bf16[256,1536]{1,0:T(8,128)(2,1)} %copy-done.119), channel_id=1, source_target_pairs={{0,4},{4,0},{1,5},{5,1},{2,6},{6,2},{3,7},{7,3},{8,12},{12,8},{9,1... | collective-permute-start | bytes 2359304 | tf_op jit(solution)/shard_map/ppermute | solution.py:72
  411.8 11.1 %collective-permute-start.58 = (bf16[64,1536]{1,0:T(8,128)(2,1)S(1)}, bf16[64,1536]{1,0:T(8,128)(2,1)S(1)}, u32[]{:S(2)}, u32[]{:S(2)}) collective-permute-start(bf16[64,1536]{1,0:T(8,128)(2,1)S(1)} %get-tuple-element.292), channel_id=1, source_target_pairs={{0,1},{1,2},{2,3},{3,0},{4,5},{5,6},{6,7},{7,4},{8,9},{9,10},{10,1... | collective-permute-start | bytes 589832 | tf_op jit(solution)/shard_map/ppermute | solution.py:77
  416.1 22.4 %collective-permute-start.61 = (bf16[256,768]{1,0:T(8,128)(2,1)}, bf16[256,768]{1,0:T(8,128)(2,1)S(1)}, u32[]{:S(2)}, u32[]{:S(2)}) collective-permute-start(bf16[256,768]{1,0:T(8,128)(2,1)} %get-tuple-element.290), channel_id=1, source_target_pairs={{0,4},{4,0},{1,5},{5,1},{2,6},{6,2},{3,7},{7,3},{8,12},{12,8},{9,1... | collective-permute-start | bytes 1179656 | tf_op jit(solution)/shard_map/ppermute | solution.py:72
  428.1 20.4 %all-to-all-start.2 = ((bf16[32,8,1536]{2,1,0:T(8,128)(2,1)}), bf16[32,8,1536]{2,1,0:T(8,128)(2,1)}, u32[]{:S(2)}, u32[]{:S(2)}) async-start(bf16[32,8,1536]{2,1,0:T(8,128)(2,1)} %fusion.4), calls=%async_computation.3 | async-start | bytes 1572864 | tf_op jit(solution)/shard_map/all_to_all | solution.py:1004
  450.8 11.6 %collective-permute-start.63 = (bf16[136,1536]{1,0:T(8,128)(2,1)}, bf16[136,1536]{1,0:T(8,128)(2,1)}, u32[]{:S(2)}, u32[]{:S(2)}) collective-permute-start(bf16[136,1536]{1,0:T(8,128)(2,1)} %fusion.19), channel_id=1, source_target_pairs={{0,1},{1,2},{2,3},{3,0},{4,5},{5,6},{6,7},{7,4},{8,9},{9,10},{10,1... | collective-permute-start | bytes 1253384 | tf_op jit(solution)/shard_map/ppermute | solution.py:77
  451.2 20.1 %collective-permute-start.64 = (bf16[136,1536]{1,0:T(8,128)(2,1)}, bf16[136,1536]{1,0:T(8,128)(2,1)S(1)}, u32[]{:S(2)}, u32[]{:S(2)}) collective-permute-start(bf16[136,1536]{1,0:T(8,128)(2,1)} %fusion.19), channel_id=1, source_target_pairs={{0,2},{1,3},{2,0},{3,1},{4,6},{5,7},{6,4},{7,5},{8,10},{9,11},{10,... | collective-permute-start | bytes 1253384 | tf_op jit(solution)/shard_map/ppermute | solution.py:77
  452.3 20.4 %collective-permute-start.65 = (bf16[136,1536]{1,0:T(8,128)(2,1)}, bf16[136,1536]{1,0:T(8,128)(2,1)S(1)}, u32[]{:S(2)}, u32[]{:S(2)}) collective-permute-start(bf16[136,1536]{1,0:T(8,128)(2,1)} %fusion.19), channel_id=1, source_target_pairs={{0,3},{1,0},{2,1},{3,2},{4,7},{5,4},{6,5},{7,6},{8,11},{9,8},{10,9... | collective-permute-start | bytes 1253384 | tf_op jit(solution)/shard_map/ppermute | solution.py:77
  454.0 47.2 %all-to-all-start.3 = ((bf16[32,48,768]{2,1,0:T(8,128)(2,1)}), bf16[32,48,768]{2,1,0:T(8,128)(2,1)S(1)}, u32[]{:S(2)}, u32[]{:S(2)}) async-start(bf16[32,48,768]{2,1,0:T(8,128)(2,1)} %bitcast.101), calls=%async_computation.5 | async-start | bytes 4718592 | tf_op jit(solution)/shard_map/all_to_all | solution.py:1029
  (156 other events, 1088.3 us)
Sparse Core Ops, SparseCore 0:
  35.4 102.1 all-gather.2
  140.4 72.6 all-gather.4
  287.6 85.3 reduce-scatter.4
  376.4 115.6 reduce-scatter.2
where the time goes:
time: 521 us; the launch traced here: 511 us
  waiting for transfers between devices  163 us (31%)
  starting transfers between devices  121 us (23%)
  Pallas kernels  91.4 us (18%)
  local copies, waits for them, and re-layouts  60 us (12%)
  matrix products  30 us (6%)
  other arithmetic  28.5 us (5%)
  between operations  16.9 us (3%)
    ppermute x48, waiting for transfers between devices, shift_tp(): lax.ppermute(block, 'tp', [(i, (i + distance) % members) for i in range(m...  83.9 us
    ppermute x48, starting transfers between devices, shift_tp(): lax.ppermute(block, 'tp', [(i, (i + distance) % members) for i in range(m...  62.5 us
    pallas_call x2, Pallas kernels, ffn_backward(): pl.pallas_call(functools.partial(ffn_backward_kernel, count, forward), gr...  29.4 us
    pallas_call x4, Pallas kernels, gradient(): pl.pallas_call(functools.partial(gradient_kernel, edge, cut), grid=(steps...  26 us
    all_to_all x1, waiting for transfers between devices, gather_pack(): lax.all_to_all(jnp.broadcast_to(pack, (chips,) + pack.shape), CHIP_AXES,...  23.2 us
    ppermute x15, starting transfers between devices, swap_core(): return lax.ppermute(block, 'core', [(0, 1), (1, 0)])  23.1 us
    pallas_call x11, Pallas kernels, one_step(): pl.pallas_call(kernel, grid=(1,), in_specs=[whole(v.shape) for v in opera...  22.5 us
    unnamed x269, local copies, waits for them, and re-layouts  22.3 us
  transfers between devices with their start and end apart: 75, of which 43 were waited for; matrix products, arithmetic and copies ran while one was open for 18% of the time, Pallas kernels for 15%

commit v1 on v0

--- a/solution.py
+++ b/solution.py
@@ -253,10 +253,11 @@
     )(*chunks, pack, pack)
 
 
-def ffn_backward_kernel(count, forward, core_ref, *refs):
-    x_refs, b_refs = refs[:count], refs[count : 2 * count]
-    gu_ref, dn_ref = refs[2 * count : 2 * count + 2]
-    place = 2 * count + 2
+def ffn_backward_kernel(count, back_count, forward, core_ref, *refs):
+    x_refs, b_refs = refs[:count], refs[count : count + back_count]
+    place = count + back_count
+    gu_ref, dn_ref = refs[place : place + 2]
+    place += 2
     back_outs = refs[place : place + count]
     place += count
     if forward:
@@ -327,10 +328,10 @@
     ways = 2 if forward else 1
     side_width = (2 * width if forward else 0) + steps * block
     results = pl.pallas_call(
-        functools.partial(ffn_backward_kernel, count, forward),
+        functools.partial(ffn_backward_kernel, count, len(back_chunks), forward),
         grid=(steps,),
         in_specs=[pl.BlockSpec(memory_space=pltpu.SMEM)]
-        + [whole((rows, width))] * (2 * count)
+        + [whole(v.shape) for v in (*chunks, *back_chunks)]
         + weight_specs(width, steps),
         out_specs=[whole((rows, width))] * (ways * count)
         + [whole((tokens, steps * block)), whole((tokens, side_width))],
@@ -718,7 +719,7 @@
     stream0 = own_tokens.astype(F32)
     upstream = own_back.astype(F32)
     both = tp_gather(jnp.concatenate([own_tokens, own_back]))
-    back_s_chunks = [slot[chunk:] for slot in both]
+    back_s = jnp.concatenate([slot[chunk:] for slot in both])
 
     gathered = jnp.arange(row_count)
     member_of = (own - gathered // chunk) % members
@@ -812,7 +813,7 @@
 
     normed_s = tp_gather(normed)
     d_chunks, out_chunks, keep, side = ffn_backward(
-        core_ref, normed_s, back_s_chunks, second_all, steps, True
+        core_ref, normed_s, [back_s], second_all, steps, True
     )
     d_stream3, back_b, gain_s_grad = norm_backward(
         tp_scatter(d_chunks), stream3, gain_s, upstream
@@ -1008,8 +1009,15 @@
         concat_axis=0,
         tiled=True,
     )
+    mixer_home = lax.all_to_all(
+        partial.reshape(shards, depth, mixer_cols),
+        TOKEN_AXES,
+        split_axis=0,
+        concat_axis=0,
+        tiled=True,
+    )
     second_grads = finish(second_sums, steps, hidden)
-    home, partial, second_grads = lax.optimization_barrier((home, partial, second_grads))
+    home, mixer_home, second_grads = lax.optimization_barrier((home, mixer_home, second_grads))
     place = jnp.arange(2 * chunk + 8)
     small_line = (place == 2 * chunk) | (place == 2 * chunk + 1)
     wanted = (
@@ -1026,13 +1034,6 @@
     rounded = payload.astype(BF16).astype(F32)
     payload = jnp.where((place == 2 * chunk + 1)[:, None], payload - rounded, payload)
     last = tp_gather(payload.astype(BF16))
-    mixer_home = lax.all_to_all(
-        partial.reshape(shards, depth, mixer_cols),
-        TOKEN_AXES,
-        split_axis=0,
-        concat_axis=0,
-        tiled=True,
-    )
     home_rows = (
         jnp.repeat(jnp.tile(send_piece, members), part_rows) * piece_rows
         + member_of * part_rows

time: 521 us -> 545 us (1.046)
  the two profiles are of different devices: /device:TPU:23 before, /device:TPU:1 now
where the time goes in v1:
time: 545 us; the launch traced here: 535 us
  waiting for transfers between devices  208 us (38%)
  starting transfers between devices  103 us (19%)
  Pallas kernels  90.7 us (17%)
  local copies, waits for them, and re-layouts  60.8 us (11%)
  matrix products  31.3 us (6%)
  other arithmetic  24.5 us (4%)
  between operations  16.8 us (3%)
    ppermute x48, waiting for transfers between devices, shift_tp(): lax.ppermute(block, 'tp', [(i, (i + distance) % members) for i in range(m...  114 us
    ppermute x48, starting transfers between devices, shift_tp(): lax.ppermute(block, 'tp', [(i, (i + distance) % members) for i in range(m...  51.5 us
    all_to_all x1, waiting for transfers between devices, body(): lax.all_to_all(partial.reshape(shards, depth, mixer_cols), TOKEN_AXES, sp...  35 us
    pallas_call x2, Pallas kernels, ffn_backward(): pl.pallas_call(functools.partial(ffn_backward_kernel, count, len(back_chu...  29.6 us
    pallas_call x4, Pallas kernels, gradient(): pl.pallas_call(functools.partial(gradient_kernel, edge, cut), grid=(steps...  26 us
    pallas_call x11, Pallas kernels, one_step(): pl.pallas_call(kernel, grid=(1,), in_specs=[whole(v.shape) for v in opera...  21.6 us
    unnamed x275, local copies, waits for them, and re-layouts  21.3 us
    ppermute x15, starting transfers between devices, swap_core(): return lax.ppermute(block, 'core', [(0, 1), (1, 0)])  19.3 us
  transfers between devices with their start and end apart: 75, of which 41 were waited for; matrix products, arithmetic and copies ran while one was open for 16% of the time, Pallas kernels for 14%

profile of v1, /device:TPU:1, one launch (start us, length us, event | category | flops | bytes accessed | tf_op | source)
XLA Modules:
  0.0 535.4 jit_solution(12720827844938091711)
XLA Ops:
  14.3 9.4 %all-to-all-start = ((bf16[32,5,1536]{2,1,0:T(8,128)(2,1)}), bf16[32,5,1536]{2,1,0:T(8,128)(2,1)S(1)}, u32[]{:S(2)}, u32[]{:S(2)}) async-start(bf16[32,5,1536]{2,1,0:T(8,128)(2,1)} %pad_maximum_fusion), calls=%async_computation | async-start | bytes 1572864 | tf_op jit(solution)/shard_map/all_to_all | solution.py:699
  25.9 12.1 %all-to-all-done = bf16[32,5,1536]{2,1,0:T(8,128)(2,1)S(1)} async-done(((bf16[32,5,1536]{2,1,0:T(8,128)(2,1)}), bf16[32,5,1536]{2,1,0:T(8,128)(2,1)S(1)}, u32[]{:S(2)}, u32[]{:S(2)}) %all-to-all-start) | async-done | bytes 491552 | tf_op jit(solution)/shard_map/all_to_all | solution.py:699
  48.6 3.9 all-to-all-start.1
  63.3 2.6 collective-permute-start.1
  69.9 3.9 collective-permute-done
  75.6 13.8 %all-to-all-done.1 = bf16[16,48,1536]{2,1,0:T(8,128)(2,1)S(1)} async-done(((bf16[16,48,1536]{2,1,0:T(8,128)(2,1)}), bf16[16,48,1536]{2,1,0:T(8,128)(2,1)S(1)}, u32[]{:S(2)}, u32[]{:S(2)}) %all-to-all-start.1) | async-done | bytes 2359328 | tf_op jit(solution)/shard_map/all_to_all | solution.py:551
  95.1 3.8 collective-permute-start.3
  104.3 3.3 fusion.140
  107.7 4.9 collective-permute-start.5
  115.2 3.7 collective-permute-done.5.refs_1_
  125.4 4.0 collective-permute-done.10.refs_3_
  129.3 5.2 collective-permute-done.8.refs_1_
  134.6 4.0 all-gather.3.cloned.1.call-done.refs_4_.refs_5_.refs_8_.refs_9_
  138.6 11.1 %ffn_forward.1 = (f32[64,1536]{1,0:T(8,128)S(1)}, bf16[64,1536]{1,0:T(8,128)(2,1)S(1)}, bf16[64,1536]{1,0:T(8,128)(2,1)}, bf16[64,1536]{1,0:T(8,128)(2,1)}) custom-call(bf16[64,1536]{1,0:T(8,128)(2,1)S(1)} %get-tuple-element.118.refs_0_, bf16[64,1536]{1,0:T(8,128)(2,1)S(1)} %collective-permute-done.8.refs_1_, ...), custom_call_target="tpu_custom_call" | custom-call | flops 4227858432 | bytes 16515072 | tf_op jit(solution)/shard_map/ffn_forward/pallas_call | solution.py:239
  154.2 6.9 %collective-permute-done.11.refs_1_ = bf16[64,1536]{1,0:T(8,128)(2,1)S(1)} collective-permute-done((bf16[64,1536]{1,0:T(8,128)(2,1)S(1)}, bf16[64,1536]{1,0:T(8,128)(2,1)S(1)}, u32[]{:S(2)}, u32[]{:S(2)}) %collective-permute-start.11) | collective-permute-done | bytes 196640 | tf_op jit(solution)/shard_map/ppermute | solution.py:77
  161.1 4.7 collective-permute-done.13.refs_3_
  169.8 9.2 %collective-permute-done.14 = bf16[64,1536]{1,0:T(8,128)(2,1)S(1)} collective-permute-done((bf16[64,1536]{1,0:T(8,128)(2,1)S(1)}, bf16[64,1536]{1,0:T(8,128)(2,1)S(1)}, u32[]{:S(2)}, u32[]{:S(2)}) %collective-permute-start.14) | collective-permute-done | bytes 196640 | tf_op jit(solution)/shard_map/ppermute | solution.py:77
  184.7 7.1 %collective-permute-done.17 = bf16[256,256]{1,0:T(8,128)(2,1)S(1)} collective-permute-done((bf16[256,256]{1,0:T(8,128)(2,1)S(1)}, bf16[256,256]{1,0:T(8,128)(2,1)S(1)}, u32[]{:S(2)}, u32[]{:S(2)}) %collective-permute-start.17) | collective-permute-done | bytes 131104 | tf_op jit(solution)/shard_map/ppermute | solution.py:68
  191.9 2.7 collective-permute-start.18
  195.9 5.3 attend.1
  201.1 3.2 fusion.141
  210.6 5.4 %collective-permute-done.19.refs_1_ = bf16[64,1536]{1,0:T(8,128)(2,1)S(1)} collective-permute-done((bf16[64,1536]{1,0:T(8,128)(2,1)}, bf16[64,1536]{1,0:T(8,128)(2,1)S(1)}, u32[]{:S(2)}, u32[]{:S(2)}) %collective-permute-start.19) | collective-permute-done | bytes 196640 | tf_op jit(solution)/shard_map/ppermute | solution.py:77
  215.9 3.8 collective-permute-done.21.refs_3_
  225.8 8.8 %collective-permute-done.22.refs_1_ = bf16[64,1536]{1,0:T(8,128)(2,1)} collective-permute-done((bf16[64,1536]{1,0:T(8,128)(2,1)}, bf16[64,1536]{1,0:T(8,128)(2,1)}, u32[]{:S(2)}, u32[]{:S(2)}) %collective-permute-start.22) | collective-permute-done | bytes 196640 | tf_op jit(solution)/shard_map/ppermute | solution.py:77
  234.7 15.4 %ffn_both.1 = (f32[64,1536]{1,0:T(8,128)S(1)}, bf16[64,1536]{1,0:T(8,128)(2,1)S(1)}, bf16[64,1536]{1,0:T(8,128)(2,1)S(1)}, bf16[64,1536]{1,0:T(8,128)(2,1)S(1)},...) custom-call(s32[1]{0:T(128)} %bitcast.core_ref, ...), custom_call_target="tpu_custom_call" | custom-call | flops 8455716864 | bytes 22413312 | tf_op jit(solution)/shard_map/ffn_both/pallas_call | solution.py:330
  255.5 7.8 %collective-permute-done.25.refs_1_ = bf16[64,1536]{1,0:T(8,128)(2,1)S(1)} collective-permute-done((bf16[64,1536]{1,0:T(8,128)(2,1)S(1)}, bf16[64,1536]{1,0:T(8,128)(2,1)S(1)}, u32[]{:S(2)}, u32[]{:S(2)}) %collective-permute-start.25) | collective-permute-done | bytes 196640 | tf_op jit(solution)/shard_map/ppermute | solution.py:77
  263.3 3.6 collective-permute-done.27.refs_3_
  275.0 10.4 %weight_gradient.4 = bf16[1536,2688]{1,0:T(8,128)(2,1)} custom-call(bf16[256,5760]{1,0:T(8,128)(2,1)S(1)} %copy-done, bf16[256,5760]{1,0:T(8,128)(2,1)} %copy-done.51, bf16[256,5760]{1,0:T(8,128)(2,1)S(1)} %copy-done, bf16[256,5760]{1,0:T(8,128)(2,1)} %copy-done.51, bf16[256,2688]{1,0:T(8,128)(2,1)S(1)} %get-tuple-element.137.refs_4_, ...), custom_call_target="tpu_custom_call" | custom-call | flops 4227858432 | bytes 8257536 | tf_op jit(solution)/shard_map/weight_gradient/pallas_call | solution.py:399
  292.3 7.7 %attend_backward.1 = (bf16[256,384]{1,0:T(8,128)(2,1)S(1)}, f32[512,256]{1,0:T(8,128)S(1)}, bf16[512,256]{1,0:T(8,128)(2,1)S(1)}, f32[1,64]{1,0:T(1,128)S(1)}) custom-call(bf16[256,384]{1,0:T(8,128)(2,1)S(1)} %copy-done.50, bf16[256,384]{1,0:T(8,128)(2,1)S(1)} %convolution_convert_fusion.5.do_ref, bf16[1024,256]{1,0:T(8,128)(2,1)S(1)} %copy-done.26, ...), custom_call_target="tpu_custom_call" | custom-call | flops 1006632960 | bytes 3146240 | tf_op jit(solution)/shard_map/attend_backward/pallas_call | solution.py:137
  303.2 6.4 %collective-permute-done.33.far_ref = bf16[256,256]{1,0:T(8,128)(2,1)S(1)} collective-permute-done((bf16[256,256]{1,0:T(8,128)(2,1)S(1)}, bf16[256,256]{1,0:T(8,128)(2,1)S(1)}, u32[]{:S(2)}, u32[]{:S(2)}) %collective-permute-start.33) | collective-permute-done | bytes 131104 | tf_op jit(solution)/shard_map/ppermute | solution.py:68
  319.2 5.2 collective-permute-start.43
  332.2 3.6 weight_gradient.5.refs_6_
  336.1 3.2 collective-permute-done.38.refs_6_
  340.7 14.2 %ffn_backward.1 = (f32[64,1536]{1,0:T(8,128)S(1)}, bf16[64,1536]{1,0:T(8,128)(2,1)}, bf16[64,1536]{1,0:T(8,128)(2,1)}, bf16[64,1536]{1,0:T(8,128)(2,1)}, bf16[25...) custom-call(s32[1]{0:T(128)} %bitcast.core_ref, bf16[64,1536]{1,0:T(8,128)(2,1)S(1)} %copy-done.2, ...), custom_call_target="tpu_custom_call" | custom-call | flops 7046430720 | bytes 19267584 | tf_op jit(solution)/shard_map/ffn_backward/pallas_call | solution.py:330
  356.6 3.7 collective-permute-done.44.refs_3_
  363.6 8.7 %weight_gradient.6 = bf16[1536,3200]{1,0:T(8,128)(2,1)} custom-call(bf16[256,1536]{1,0:T(8,128)(2,1)S(1)} %constant_dynamic-update-slice_fusion.10.refs_0_, bf16[256,1536]{1,0:T(8,128)(2,1)S(1)} %collective-permute-done.43.refs_1_, bf16[256,1536]{1,0:T(8,128)(2,1)S(1)} %constant_dynamic-update-slice_fusion.14.refs_2_, ...), custom_call_target="tpu_custom_call", output_to_operand_aliasing={{}: (6, {})} | custom-call | flops 4227858432 | bytes 8257536 | tf_op jit(solution)/shard_map/weight_gradient/pallas_call | solution.py:399
  372.4 3.1 collective-permute-done.48.refs_3_
  382.4 5.7 %collective-permute-done.49 = bf16[64,1536]{1,0:T(8,128)(2,1)S(1)} collective-permute-done((bf16[64,1536]{1,0:T(8,128)(2,1)S(1)}, bf16[64,1536]{1,0:T(8,128)(2,1)S(1)}, u32[]{:S(2)}, u32[]{:S(2)}) %collective-permute-start.49) | collective-permute-done | bytes 196640 | tf_op jit(solution)/shard_map/ppermute | solution.py:77
  390.5 3.0 multiply_reduce_fusion.3
  394.5 4.3 collective-permute-start.52
  402.1 5.1 fusion.143
  417.1 5.4 %collective-permute-done.58.refs_3_ = bf16[64,1536]{1,0:T(8,128)(2,1)S(1)} collective-permute-done((bf16[64,1536]{1,0:T(8,128)(2,1)S(1)}, bf16[64,1536]{1,0:T(8,128)(2,1)S(1)}, u32[]{:S(2)}, u32[]{:S(2)}) %collective-permute-start.58) | collective-permute-done | bytes 196640 | tf_op jit(solution)/shard_map/ppermute | solution.py:77
  426.1 5.7 %all-to-all-start.2 = ((bf16[32,8,1536]{2,1,0:T(8,128)(2,1)}), bf16[32,8,1536]{2,1,0:T(8,128)(2,1)}, u32[]{:S(2)}, u32[]{:S(2)}) async-start(bf16[32,8,1536]{2,1,0:T(8,128)(2,1)} %fusion.4), calls=%async_computation.3 | async-start | bytes 1572864 | tf_op jit(solution)/shard_map/all_to_all | solution.py:1005
  434.9 3.3 weight_gradient.7
  438.2 8.6 %all-to-all-done.2 = bf16[32,8,1536]{2,1,0:T(8,128)(2,1)} async-done(((bf16[32,8,1536]{2,1,0:T(8,128)(2,1)}), bf16[32,8,1536]{2,1,0:T(8,128)(2,1)}, u32[]{:S(2)}, u32[]{:S(2)}) %all-to-all-start.2) | async-done | bytes 786464 | tf_op jit(solution)/shard_map/all_to_all | solution.py:1005
  446.8 4.2 all-to-all-start.3
  455.9 35.0 %all-to-all-done.3 = bf16[32,48,768]{2,1,0:T(8,128)(2,1)S(1)} async-done(((bf16[32,48,768]{2,1,0:T(8,128)(2,1)}), bf16[32,48,768]{2,1,0:T(8,128)(2,1)S(1)}, u32[]{:S(2)}, u32[]{:S(2)}) %all-to-all-start.3) | async-done | bytes 2359328 | tf_op jit(solution)/shard_map/all_to_all | solution.py:1012
  495.9 17.7 %collective-permute-done.63 = bf16[136,1536]{1,0:T(8,128)(2,1)S(1)} collective-permute-done((bf16[136,1536]{1,0:T(8,128)(2,1)S(1)}, bf16[136,1536]{1,0:T(8,128)(2,1)S(1)}, u32[]{:S(2)}, u32[]{:S(2)}) %collective-permute-start.63) | collective-permute-done | bytes 417824 | tf_op jit(solution)/shard_map/ppermute | solution.py:77
  (588 shorter events, 184.6 us)
Async XLA Ops:
  14.3 23.7 %all-to-all-start = ((bf16[32,5,1536]{2,1,0:T(8,128)(2,1)}), bf16[32,5,1536]{2,1,0:T(8,128)(2,1)S(1)}, u32[]{:S(2)}, u32[]{:S(2)}) async-start(bf16[32,5,1536]{2,1,0:T(8,128)(2,1)} %pad_maximum_fusion), calls=%async_computation | async-start | bytes 1572864 | tf_op jit(solution)/shard_map/all_to_all | solution.py:699
  23.8 114.8 %all-gather.3.cloned.1.call-start = ((), (), s32[]{:S(2)}) async-start(), calls=%async_computation.6 | async-start | bytes 20275200 | tf_op jit(solution)/shard_map/all_gather | solution.py:701
  38.0 187.7 %all-gather.5.cloned.1.call-start = ((), (), s32[]{:S(2)}) async-start(), calls=%async_computation.7 | async-start | bytes 17031168 | tf_op jit(solution)/shard_map/all_gather | solution.py:702
  48.6 40.8 %all-to-all-start.1 = ((bf16[16,48,1536]{2,1,0:T(8,128)(2,1)}), bf16[16,48,1536]{2,1,0:T(8,128)(2,1)S(1)}, u32[]{:S(2)}, u32[]{:S(2)}) async-start(bf16[16,48,1536]{2,1,0:T(8,128)(2,1)} %broadcast_in_dim.85), calls=%async_computation.1 | async-start | bytes 4718592 | tf_op jit(solution)/shard_map/all_to_all | solution.py:551
  52.5 398.6 %reduce-scatter.5.cloned.1.call-start = ((), (), s32[]{:S(2)}) async-start(), calls=%async_computation.9 | async-start | bytes 8773632 | tf_op jit(solution)/shard_map/reduce_scatter | solution.py:545
  61.5 12.4 %collective-permute-start = (bf16[128,1536]{1,0:T(8,128)(2,1)}, bf16[128,1536]{1,0:T(8,128)(2,1)}, u32[]{:S(2)}, u32[]{:S(2)}) collective-permute-start(bf16[128,1536]{1,0:T(8,128)(2,1)} %get-tuple-element.331), channel_id=1, source_target_pairs={{0,1},{1,2},{2,3},{3,0},{4,5},{5,6},{6,7},{7,4},{8,9},{9,10},{10,1... | collective-permute-start | bytes 1179656 | tf_op jit(solution)/shard_map/ppermute | solution.py:77
  63.3 27.0 %collective-permute-start.1 = (bf16[128,1536]{1,0:T(8,128)(2,1)}, bf16[128,1536]{1,0:T(8,128)(2,1)}, u32[]{:S(2)}, u32[]{:S(2)}) collective-permute-start(bf16[128,1536]{1,0:T(8,128)(2,1)} %get-tuple-element.331), channel_id=1, source_target_pairs={{0,2},{1,3},{2,0},{3,1},{4,6},{5,7},{6,4},{7,5},{8,10},{9,11},{10,... | collective-permute-start | bytes 1179656 | tf_op jit(solution)/shard_map/ppermute | solution.py:77
  65.9 26.1 %collective-permute-start.2 = (bf16[128,1536]{1,0:T(8,128)(2,1)}, bf16[128,1536]{1,0:T(8,128)(2,1)}, u32[]{:S(2)}, u32[]{:S(2)}) collective-permute-start(bf16[128,1536]{1,0:T(8,128)(2,1)} %get-tuple-element.331), channel_id=1, source_target_pairs={{0,3},{1,0},{2,1},{3,2},{4,7},{5,4},{6,5},{7,6},{8,11},{9,8},{10,9... | collective-permute-start | bytes 1179656 | tf_op jit(solution)/shard_map/ppermute | solution.py:77
  107.7 11.3 %collective-permute-start.5 = (bf16[64,1536]{1,0:T(8,128)(2,1)S(1)}, bf16[64,1536]{1,0:T(8,128)(2,1)S(1)}, u32[]{:S(2)}, u32[]{:S(2)}) collective-permute-start(bf16[64,1536]{1,0:T(8,128)(2,1)S(1)} %get-tuple-element.303), channel_id=1, source_target_pairs={{0,3},{1,0},{2,1},{3,2},{4,7},{5,4},{6,5},{7,6},{8,11},{9,8},{10,9... | collective-permute-start | bytes 589832 | tf_op jit(solution)/shard_map/ppermute | solution.py:77
  122.8 11.8 %collective-permute-start.8 = (bf16[64,1536]{1,0:T(8,128)(2,1)S(1)}, bf16[64,1536]{1,0:T(8,128)(2,1)S(1)}, u32[]{:S(2)}, u32[]{:S(2)}) collective-permute-start(bf16[64,1536]{1,0:T(8,128)(2,1)S(1)} %get-tuple-element.118.refs_0_), channel_id=1, source_target_pairs={{0,1},{1,2},{2,3},{3,0},{4,5},{5,6},{6,7},{7,4},{8,9},{9,10},{10,1... | collective-permute-start | bytes 589832 | tf_op jit(solution)/shard_map/ppermute | solution.py:77
  123.9 10.7 %collective-permute-start.9 = (bf16[64,1536]{1,0:T(8,128)(2,1)S(1)}, bf16[64,1536]{1,0:T(8,128)(2,1)S(1)}, u32[]{:S(2)}, u32[]{:S(2)}) collective-permute-start(bf16[64,1536]{1,0:T(8,128)(2,1)S(1)} %get-tuple-element.118.refs_0_), channel_id=1, source_target_pairs={{0,2},{1,3},{2,0},{3,1},{4,6},{5,7},{6,4},{7,5},{8,10},{9,11},{10,... | collective-permute-start | bytes 589832 | tf_op jit(solution)/shard_map/ppermute | solution.py:77
  150.5 10.6 %collective-permute-start.11 = (bf16[64,1536]{1,0:T(8,128)(2,1)S(1)}, bf16[64,1536]{1,0:T(8,128)(2,1)S(1)}, u32[]{:S(2)}, u32[]{:S(2)}) collective-permute-start(bf16[64,1536]{1,0:T(8,128)(2,1)S(1)} %get-tuple-element.121), channel_id=1, source_target_pairs={{0,3},{1,0},{2,1},{3,2},{4,7},{5,4},{6,5},{7,6},{8,11},{9,8},{10,9... | collective-permute-start | bytes 589832 | tf_op jit(solution)/shard_map/ppermute | solution.py:77
  153.5 12.3 %collective-permute-start.13 = (bf16[64,1536]{1,0:T(8,128)(2,1)}, bf16[64,1536]{1,0:T(8,128)(2,1)S(1)}, u32[]{:S(2)}, u32[]{:S(2)}) collective-permute-start(bf16[64,1536]{1,0:T(8,128)(2,1)} %get-tuple-element.123), channel_id=1, source_target_pairs={{0,1},{1,2},{2,3},{3,0},{4,5},{5,6},{6,7},{7,4},{8,9},{9,10},{10,1... | collective-permute-start | bytes 589832 | tf_op jit(solution)/shard_map/ppermute | solution.py:77
  167.0 11.9 %collective-permute-start.14 = (bf16[64,1536]{1,0:T(8,128)(2,1)S(1)}, bf16[64,1536]{1,0:T(8,128)(2,1)S(1)}, u32[]{:S(2)}, u32[]{:S(2)}) collective-permute-start(bf16[64,1536]{1,0:T(8,128)(2,1)S(1)} %get-tuple-element.125), channel_id=1, source_target_pairs={{0,1},{1,2},{2,3},{3,0},{4,5},{5,6},{6,7},{7,4},{8,9},{9,10},{10,1... | collective-permute-start | bytes 589832 | tf_op jit(solution)/shard_map/ppermute | solution.py:77
  167.1 11.9 %collective-permute-start.15 = (bf16[64,1536]{1,0:T(8,128)(2,1)S(1)}, bf16[64,1536]{1,0:T(8,128)(2,1)S(1)}, u32[]{:S(2)}, u32[]{:S(2)}) collective-permute-start(bf16[64,1536]{1,0:T(8,128)(2,1)S(1)} %get-tuple-element.125), channel_id=1, source_target_pairs={{0,2},{1,3},{2,0},{3,1},{4,6},{5,7},{6,4},{7,5},{8,10},{9,11},{10,... | collective-permute-start | bytes 589832 | tf_op jit(solution)/shard_map/ppermute | solution.py:77
  167.7 11.3 %collective-permute-start.16 = (bf16[64,1536]{1,0:T(8,128)(2,1)S(1)}, bf16[64,1536]{1,0:T(8,128)(2,1)S(1)}, u32[]{:S(2)}, u32[]{:S(2)}) collective-permute-start(bf16[64,1536]{1,0:T(8,128)(2,1)S(1)} %get-tuple-element.125), channel_id=1, source_target_pairs={{0,3},{1,0},{2,1},{3,2},{4,7},{5,4},{6,5},{7,6},{8,11},{9,8},{10,9... | collective-permute-start | bytes 589832 | tf_op jit(solution)/shard_map/ppermute | solution.py:77
  205.1 10.8 %collective-permute-start.19 = (bf16[64,1536]{1,0:T(8,128)(2,1)}, bf16[64,1536]{1,0:T(8,128)(2,1)S(1)}, u32[]{:S(2)}, u32[]{:S(2)}) collective-permute-start(bf16[64,1536]{1,0:T(8,128)(2,1)} %get-tuple-element.300), channel_id=1, source_target_pairs={{0,3},{1,0},{2,1},{3,2},{4,7},{5,4},{6,5},{7,6},{8,11},{9,8},{10,9... | collective-permute-start | bytes 589832 | tf_op jit(solution)/shard_map/ppermute | solution.py:77
  207.5 12.3 %collective-permute-start.21 = (bf16[64,1536]{1,0:T(8,128)(2,1)}, bf16[64,1536]{1,0:T(8,128)(2,1)}, u32[]{:S(2)}, u32[]{:S(2)}) collective-permute-start(bf16[64,1536]{1,0:T(8,128)(2,1)} %get-tuple-element.298), channel_id=1, source_target_pairs={{0,1},{1,2},{2,3},{3,0},{4,5},{5,6},{6,7},{7,4},{8,9},{9,10},{10,1... | collective-permute-start | bytes 589832 | tf_op jit(solution)/shard_map/ppermute | solution.py:77
  223.0 11.5 %collective-permute-start.22 = (bf16[64,1536]{1,0:T(8,128)(2,1)}, bf16[64,1536]{1,0:T(8,128)(2,1)}, u32[]{:S(2)}, u32[]{:S(2)}) collective-permute-start(bf16[64,1536]{1,0:T(8,128)(2,1)} %get-tuple-element.129.refs_0_), channel_id=1, source_target_pairs={{0,1},{1,2},{2,3},{3,0},{4,5},{5,6},{6,7},{7,4},{8,9},{9,10},{10,1... | collective-permute-start | bytes 589832 | tf_op jit(solution)/shard_map/ppermute | solution.py:77
  223.0 11.5 %collective-permute-start.23 = (bf16[64,1536]{1,0:T(8,128)(2,1)}, bf16[64,1536]{1,0:T(8,128)(2,1)}, u32[]{:S(2)}, u32[]{:S(2)}) collective-permute-start(bf16[64,1536]{1,0:T(8,128)(2,1)} %get-tuple-element.129.refs_0_), channel_id=1, source_target_pairs={{0,2},{1,3},{2,0},{3,1},{4,6},{5,7},{6,4},{7,5},{8,10},{9,11},{10,... | collective-permute-start | bytes 589832 | tf_op jit(solution)/shard_map/ppermute | solution.py:77
  224.2 10.5 %collective-permute-start.24 = (bf16[64,1536]{1,0:T(8,128)(2,1)}, bf16[64,1536]{1,0:T(8,128)(2,1)}, u32[]{:S(2)}, u32[]{:S(2)}) collective-permute-start(bf16[64,1536]{1,0:T(8,128)(2,1)} %get-tuple-element.129.refs_0_), channel_id=1, source_target_pairs={{0,3},{1,0},{2,1},{3,2},{4,7},{5,4},{6,5},{7,6},{8,11},{9,8},{10,9... | collective-permute-start | bytes 589832 | tf_op jit(solution)/shard_map/ppermute | solution.py:77
  250.9 20.5 %collective-permute-start.31 = (bf16[256,5760]{1,0:T(8,128)(2,1)}, bf16[256,5760]{1,0:T(8,128)(2,1)S(1)}, u32[]{:S(2)}, u32[]{:S(2)}) collective-permute-start(bf16[256,5760]{1,0:T(8,128)(2,1)} %get-tuple-element.136.refs_0_.refs_2_), channel_id=1, source_target_pairs={{0,4},{4,0},{1,5},{5,1},{2,6},{6,2},{3,7},{7,3},{8,12},{12,8},{9,1... | collective-permute-start | bytes 8847368 | tf_op jit(solution)/shard_map/ppermute | solution.py:72
  254.9 12.0 %collective-permute-start.27 = (bf16[64,1536]{1,0:T(8,128)(2,1)S(1)}, bf16[64,1536]{1,0:T(8,128)(2,1)S(1)}, u32[]{:S(2)}, u32[]{:S(2)}) collective-permute-start(bf16[64,1536]{1,0:T(8,128)(2,1)S(1)} %get-tuple-element.133), channel_id=1, source_target_pairs={{0,1},{1,2},{2,3},{3,0},{4,5},{5,6},{6,7},{7,4},{8,9},{9,10},{10,1... | collective-permute-start | bytes 589832 | tf_op jit(solution)/shard_map/ppermute | solution.py:77
  268.6 16.8 %collective-permute-start.28 = (bf16[64,1536]{1,0:T(8,128)(2,1)}, bf16[64,1536]{1,0:T(8,128)(2,1)}, u32[]{:S(2)}, u32[]{:S(2)}) collective-permute-start(bf16[64,1536]{1,0:T(8,128)(2,1)} %get-tuple-element.138), channel_id=1, source_target_pairs={{0,1},{1,2},{2,3},{3,0},{4,5},{5,6},{6,7},{7,4},{8,9},{9,10},{10,1... | collective-permute-start | bytes 589832 | tf_op jit(solution)/shard_map/ppermute | solution.py:77
  268.6 16.8 %collective-permute-start.29 = (bf16[64,1536]{1,0:T(8,128)(2,1)}, bf16[64,1536]{1,0:T(8,128)(2,1)}, u32[]{:S(2)}, u32[]{:S(2)}) collective-permute-start(bf16[64,1536]{1,0:T(8,128)(2,1)} %get-tuple-element.138), channel_id=1, source_target_pairs={{0,2},{1,3},{2,0},{3,1},{4,6},{5,7},{6,4},{7,5},{8,10},{9,11},{10,... | collective-permute-start | bytes 589832 | tf_op jit(solution)/shard_map/ppermute | solution.py:77
  270.2 15.2 %collective-permute-start.30 = (bf16[64,1536]{1,0:T(8,128)(2,1)}, bf16[64,1536]{1,0:T(8,128)(2,1)}, u32[]{:S(2)}, u32[]{:S(2)}) collective-permute-start(bf16[64,1536]{1,0:T(8,128)(2,1)} %get-tuple-element.138), channel_id=1, source_target_pairs={{0,3},{1,0},{2,1},{3,2},{4,7},{5,4},{6,5},{7,6},{8,11},{9,8},{10,9... | collective-permute-start | bytes 589832 | tf_op jit(solution)/shard_map/ppermute | solution.py:77
  285.4 234.8 %reduce-scatter.3.cloned.1.call-start = ((), (), s32[]{:S(2)}) async-start(), calls=%async_computation.8 | async-start | bytes 10444800 | tf_op jit(solution)/shard_map/reduce_scatter | solution.py:545
  301.5 27.4 %collective-permute-start.40 = (bf16[256,1536]{1,0:T(8,128)(2,1)S(1)}, bf16[256,1536]{1,0:T(8,128)(2,1)S(1)}, u32[]{:S(2)}, u32[]{:S(2)}) collective-permute-start(bf16[256,1536]{1,0:T(8,128)(2,1)S(1)} %constant_dynamic-update-slice_fusion.2.refs_0_), channel_id=1, source_target_pairs={{0,4},{4,0},{1,5},{5,1},{2,6},{6,2},{3,7},{7,3},{8,12},{12,8},{9,1... | collective-permute-start | bytes 2359304 | tf_op jit(solution)/shard_map/ppermute | solution.py:72
  301.8 28.9 %collective-permute-start.41 = (bf16[256,1536]{1,0:T(8,128)(2,1)S(1)}, bf16[256,1536]{1,0:T(8,128)(2,1)S(1)}, u32[]{:S(2)}, u32[]{:S(2)}) collective-permute-start(bf16[256,1536]{1,0:T(8,128)(2,1)S(1)} %constant_dynamic-update-slice_fusion.6), channel_id=1, source_target_pairs={{0,4},{4,0},{1,5},{5,1},{2,6},{6,2},{3,7},{7,3},{8,12},{12,8},{9,1... | collective-permute-start | bytes 2359304 | tf_op jit(solution)/shard_map/ppermute | solution.py:72
  316.0 11.2 %collective-permute-start.36 = (bf16[64,1536]{1,0:T(8,128)(2,1)S(1)}, bf16[64,1536]{1,0:T(8,128)(2,1)S(1)}, u32[]{:S(2)}, u32[]{:S(2)}) collective-permute-start(bf16[64,1536]{1,0:T(8,128)(2,1)S(1)} %get-tuple-element.295), channel_id=1, source_target_pairs={{0,1},{1,2},{2,3},{3,0},{4,5},{5,6},{6,7},{7,4},{8,9},{9,10},{10,1... | collective-permute-start | bytes 589832 | tf_op jit(solution)/shard_map/ppermute | solution.py:77
  319.2 37.4 %collective-permute-start.43 = (bf16[256,1536]{1,0:T(8,128)(2,1)S(1)}, bf16[256,1536]{1,0:T(8,128)(2,1)S(1)}, u32[]{:S(2)}, u32[]{:S(2)}) collective-permute-start(bf16[256,1536]{1,0:T(8,128)(2,1)S(1)} %constant_dynamic-update-slice_fusion.10.refs_0_), channel_id=1, source_target_pairs={{0,4},{4,0},{1,5},{5,1},{2,6},{6,2},{3,7},{7,3},{8,12},{12,8},{9,1... | collective-permute-start | bytes 2359304 | tf_op jit(solution)/shard_map/ppermute | solution.py:72
  328.9 10.5 %collective-permute-start.38 = (bf16[64,1536]{1,0:T(8,128)(2,1)S(1)}, bf16[64,1536]{1,0:T(8,128)(2,1)S(1)}, u32[]{:S(2)}, u32[]{:S(2)}) collective-permute-start(bf16[64,1536]{1,0:T(8,128)(2,1)S(1)} %get-tuple-element.148.refs_4_), channel_id=1, source_target_pairs={{0,2},{1,3},{2,0},{3,1},{4,6},{5,7},{6,4},{7,5},{8,10},{9,11},{10,... | collective-permute-start | bytes 589832 | tf_op jit(solution)/shard_map/ppermute | solution.py:77
  360.3 12.1 %collective-permute-start.46 = (bf16[64,1536]{1,0:T(8,128)(2,1)}, bf16[64,1536]{1,0:T(8,128)(2,1)S(1)}, u32[]{:S(2)}, u32[]{:S(2)}) collective-permute-start(bf16[64,1536]{1,0:T(8,128)(2,1)} %get-tuple-element.162), channel_id=1, source_target_pairs={{0,3},{1,0},{2,1},{3,2},{4,7},{5,4},{6,5},{7,6},{8,11},{9,8},{10,9... | collective-permute-start | bytes 589832 | tf_op jit(solution)/shard_map/ppermute | solution.py:77
  362.7 12.7 %collective-permute-start.48 = (bf16[64,1536]{1,0:T(8,128)(2,1)}, bf16[64,1536]{1,0:T(8,128)(2,1)S(1)}, u32[]{:S(2)}, u32[]{:S(2)}) collective-permute-start(bf16[64,1536]{1,0:T(8,128)(2,1)} %get-tuple-element.164), channel_id=1, source_target_pairs={{0,1},{1,2},{2,3},{3,0},{4,5},{5,6},{6,7},{7,4},{8,9},{9,10},{10,1... | collective-permute-start | bytes 589832 | tf_op jit(solution)/shard_map/ppermute | solution.py:77
  376.6 11.5 %collective-permute-start.49 = (bf16[64,1536]{1,0:T(8,128)(2,1)S(1)}, bf16[64,1536]{1,0:T(8,128)(2,1)S(1)}, u32[]{:S(2)}, u32[]{:S(2)}) collective-permute-start(bf16[64,1536]{1,0:T(8,128)(2,1)S(1)} %get-tuple-element.176), channel_id=1, source_target_pairs={{0,1},{1,2},{2,3},{3,0},{4,5},{5,6},{6,7},{7,4},{8,9},{9,10},{10,1... | collective-permute-start | bytes 589832 | tf_op jit(solution)/shard_map/ppermute | solution.py:77
  376.6 11.5 %collective-permute-start.50 = (bf16[64,1536]{1,0:T(8,128)(2,1)S(1)}, bf16[64,1536]{1,0:T(8,128)(2,1)S(1)}, u32[]{:S(2)}, u32[]{:S(2)}) collective-permute-start(bf16[64,1536]{1,0:T(8,128)(2,1)S(1)} %get-tuple-element.176), channel_id=1, source_target_pairs={{0,2},{1,3},{2,0},{3,1},{4,6},{5,7},{6,4},{7,5},{8,10},{9,11},{10,... | collective-permute-start | bytes 589832 | tf_op jit(solution)/shard_map/ppermute | solution.py:77
  377.8 11.0 %collective-permute-start.51 = (bf16[64,1536]{1,0:T(8,128)(2,1)S(1)}, bf16[64,1536]{1,0:T(8,128)(2,1)}, u32[]{:S(2)}, u32[]{:S(2)}) collective-permute-start(bf16[64,1536]{1,0:T(8,128)(2,1)S(1)} %get-tuple-element.176), channel_id=1, source_target_pairs={{0,3},{1,0},{2,1},{3,2},{4,7},{5,4},{6,5},{7,6},{8,11},{9,8},{10,9... | collective-permute-start | bytes 589832 | tf_op jit(solution)/shard_map/ppermute | solution.py:77
  379.4 54.1 %collective-permute-start.59 = (bf16[256,1536]{1,0:T(8,128)(2,1)S(1)}, bf16[256,1536]{1,0:T(8,128)(2,1)S(1)}, u32[]{:S(2)}, u32[]{:S(2)}) collective-permute-start(bf16[256,1536]{1,0:T(8,128)(2,1)S(1)} %multiply_convert_fusion.refs_0_), channel_id=1, source_target_pairs={{0,4},{4,0},{1,5},{5,1},{2,6},{6,2},{3,7},{7,3},{8,12},{12,8},{9,1... | collective-permute-start | bytes 2359304 | tf_op jit(solution)/shard_map/ppermute | solution.py:72
  380.9 21.2 %collective-permute-start.53 = (bf16[64,1536]{1,0:T(8,128)(2,1)}, bf16[64,1536]{1,0:T(8,128)(2,1)}, u32[]{:S(2)}, u32[]{:S(2)}) collective-permute-start(bf16[64,1536]{1,0:T(8,128)(2,1)} %get-tuple-element.177), channel_id=1, source_target_pairs={{0,3},{1,0},{2,1},{3,2},{4,7},{5,4},{6,5},{7,6},{8,11},{9,8},{10,9... | collective-permute-start | bytes 589832 | tf_op jit(solution)/shard_map/ppermute | solution.py:77
  388.1 13.9 %collective-permute-start.54 = (bf16[64,1536]{1,0:T(8,128)(2,1)}, bf16[64,1536]{1,0:T(8,128)(2,1)}, u32[]{:S(2)}, u32[]{:S(2)}) collective-permute-start(bf16[64,1536]{1,0:T(8,128)(2,1)} %get-tuple-element.178), channel_id=1, source_target_pairs={{0,2},{1,3},{2,0},{3,1},{4,6},{5,7},{6,4},{7,5},{8,10},{9,11},{10,... | collective-permute-start | bytes 589832 | tf_op jit(solution)/shard_map/ppermute | solution.py:77
  388.2 13.9 %collective-permute-start.55 = (bf16[64,1536]{1,0:T(8,128)(2,1)}, bf16[64,1536]{1,0:T(8,128)(2,1)}, u32[]{:S(2)}, u32[]{:S(2)}) collective-permute-start(bf16[64,1536]{1,0:T(8,128)(2,1)} %get-tuple-element.179), channel_id=1, source_target_pairs={{0,1},{1,2},{2,3},{3,0},{4,5},{5,6},{6,7},{7,4},{8,9},{9,10},{10,1... | collective-permute-start | bytes 589832 | tf_op jit(solution)/shard_map/ppermute | solution.py:77
  401.0 32.5 %collective-permute-start.60 = (bf16[256,1536]{1,0:T(8,128)(2,1)}, bf16[256,1536]{1,0:T(8,128)(2,1)}, u32[]{:S(2)}, u32[]{:S(2)}) collective-permute-start(bf16[256,1536]{1,0:T(8,128)(2,1)} %copy-done.127), channel_id=1, source_target_pairs={{0,4},{4,0},{1,5},{5,1},{2,6},{6,2},{3,7},{7,3},{8,12},{12,8},{9,1... | collective-permute-start | bytes 2359304 | tf_op jit(solution)/shard_map/ppermute | solution.py:72
  411.7 10.8 %collective-permute-start.58 = (bf16[64,1536]{1,0:T(8,128)(2,1)S(1)}, bf16[64,1536]{1,0:T(8,128)(2,1)S(1)}, u32[]{:S(2)}, u32[]{:S(2)}) collective-permute-start(bf16[64,1536]{1,0:T(8,128)(2,1)S(1)} %get-tuple-element.292), channel_id=1, source_target_pairs={{0,1},{1,2},{2,3},{3,0},{4,5},{5,6},{6,7},{7,4},{8,9},{9,10},{10,1... | collective-permute-start | bytes 589832 | tf_op jit(solution)/shard_map/ppermute | solution.py:77
  426.1 20.8 %all-to-all-start.2 = ((bf16[32,8,1536]{2,1,0:T(8,128)(2,1)}), bf16[32,8,1536]{2,1,0:T(8,128)(2,1)}, u32[]{:S(2)}, u32[]{:S(2)}) async-start(bf16[32,8,1536]{2,1,0:T(8,128)(2,1)} %fusion.4), calls=%async_computation.3 | async-start | bytes 1572864 | tf_op jit(solution)/shard_map/all_to_all | solution.py:1005
  446.8 44.0 %all-to-all-start.3 = ((bf16[32,48,768]{2,1,0:T(8,128)(2,1)}), bf16[32,48,768]{2,1,0:T(8,128)(2,1)S(1)}, u32[]{:S(2)}, u32[]{:S(2)}) async-start(bf16[32,48,768]{2,1,0:T(8,128)(2,1)} %bitcast.101), calls=%async_computation.4 | async-start | bytes 4718592 | tf_op jit(solution)/shard_map/all_to_all | solution.py:1012
  492.3 21.3 %collective-permute-start.63 = (bf16[136,1536]{1,0:T(8,128)(2,1)S(1)}, bf16[136,1536]{1,0:T(8,128)(2,1)S(1)}, u32[]{:S(2)}, u32[]{:S(2)}) collective-permute-start(bf16[136,1536]{1,0:T(8,128)(2,1)S(1)} %fusion.19), channel_id=1, source_target_pairs={{0,1},{1,2},{2,3},{3,0},{4,5},{5,6},{6,7},{7,4},{8,9},{9,10},{10,1... | collective-permute-start | bytes 1253384 | tf_op jit(solution)/shard_map/ppermute | solution.py:77
  493.4 20.2 %collective-permute-start.64 = (bf16[136,1536]{1,0:T(8,128)(2,1)S(1)}, bf16[136,1536]{1,0:T(8,128)(2,1)S(1)}, u32[]{:S(2)}, u32[]{:S(2)}) collective-permute-start(bf16[136,1536]{1,0:T(8,128)(2,1)S(1)} %fusion.19), channel_id=1, source_target_pairs={{0,2},{1,3},{2,0},{3,1},{4,6},{5,7},{6,4},{7,5},{8,10},{9,11},{10,... | collective-permute-start | bytes 1253384 | tf_op jit(solution)/shard_map/ppermute | solution.py:77
  494.0 20.0 %collective-permute-start.65 = (bf16[136,1536]{1,0:T(8,128)(2,1)S(1)}, bf16[136,1536]{1,0:T(8,128)(2,1)S(1)}, u32[]{:S(2)}, u32[]{:S(2)}) collective-permute-start(bf16[136,1536]{1,0:T(8,128)(2,1)S(1)} %fusion.19), channel_id=1, source_target_pairs={{0,3},{1,0},{2,1},{3,2},{4,7},{5,4},{6,5},{7,6},{8,11},{9,8},{10,9... | collective-permute-start | bytes 1253384 | tf_op jit(solution)/shard_map/ppermute | solution.py:77
  (159 other events, 1389.5 us)
Sparse Core Ops, SparseCore 0:
  38.2 100.4 all-gather.2
  141.5 72.6 all-gather.4
  285.6 85.0 reduce-scatter.4
  375.6 115.4 reduce-scatter.2

commit v2 on v1

--- a/solution.py
+++ b/solution.py
@@ -545,21 +545,19 @@
     return lax.psum_scatter(partial, CHIP_AXES, scatter_dimension=0, tiled=True)
 
 
-def gather_pack(pack):
-    chips = lax.axis_size(CHIP_AXES)
+def spread_pack(pack):
+    return jnp.broadcast_to(pack, (lax.axis_size(CHIP_AXES),) + pack.shape)
+
+
+def gather_pack(spread):
+    chips, rows, columns = spread.shape
     core = lax.axis_index("core")
-    plane = lax.all_to_all(
-        jnp.broadcast_to(pack, (chips,) + pack.shape),
-        CHIP_AXES,
-        split_axis=0,
-        concat_axis=0,
-        tiled=True,
-    )
+    plane = lax.all_to_all(spread, CHIP_AXES, split_axis=0, concat_axis=0, tiled=True)
     other = swap_core(plane)
-    both = jnp.zeros((chips, CORES) + pack.shape, BF16)
+    both = jnp.zeros((chips, CORES, rows, columns), BF16)
     both = lax.dynamic_update_slice(both, plane[:, None], (0, core, 0, 0))
     both = lax.dynamic_update_slice(both, other[:, None], (0, 1 - core, 0, 0))
-    return both.reshape(-1, pack.shape[1])
+    return both.reshape(-1, columns)
 
 
 def finish_kernel(steps, core_ref, sum_ref, other_ref, gateup_ref, down_ref, *rest):
@@ -665,16 +663,6 @@
     ffn_width = 3 * padded
     block = TILE + TILE // 2
 
-    def pack_ffn(gateup, down):
-        wide = jnp.pad(gateup, ((0, 0), (0, 0), (0, padded - hidden)))
-        wide = wide.reshape(depth, 2, steps, TILE).transpose(0, 2, 1, 3).reshape(depth, -1)
-        return [wide, jnp.pad(down.T, ((0, 0), (0, padded - hidden)))]
-
-    mixer_pack = jnp.concatenate([mixer_project.reshape(depth, -1), mixer_output.T], axis=1)
-    first_pack = jnp.concatenate(
-        pack_ffn(first_gateup, first_down) + [attend_project, attend_output.T], axis=1
-    )
-    second_pack = jnp.concatenate(pack_ffn(second_gateup, second_down), axis=1)
     piece_table = deal_order.reshape(shards, shards, piece_rows)[:, :, 0]
     anchor = piece_table // row_count
     anchor_piece = piece_table % row_count // piece_rows
@@ -696,8 +684,37 @@
         ],
         axis=1,
     )
+    outgoing, weights = lax.optimization_barrier(
+        (
+            outgoing,
+            (
+                mixer_project,
+                mixer_output,
+                first_gateup,
+                first_down,
+                attend_project,
+                attend_output,
+                second_gateup,
+                second_down,
+            ),
+        )
+    )
+    mixer_project, mixer_output, first_gateup, first_down = weights[:4]
+    attend_project, attend_output, second_gateup, second_down = weights[4:]
     arrived = lax.all_to_all(outgoing, TOKEN_AXES, split_axis=0, concat_axis=0, tiled=True)
-    arrived, mixer_pack, first_pack = lax.optimization_barrier((arrived, mixer_pack, first_pack))
+
+    def pack_ffn(gateup, down):
+        wide = jnp.pad(gateup, ((0, 0), (0, 0), (0, padded - hidden)))
+        wide = wide.reshape(depth, 2, steps, TILE).transpose(0, 2, 1, 3).reshape(depth, -1)
+        return [wide, jnp.pad(down.T, ((0, 0), (0, padded - hidden)))]
+
+    mixer_pack = jnp.concatenate([mixer_project.reshape(depth, -1), mixer_output.T], axis=1)
+    first_pack = jnp.concatenate(
+        pack_ffn(first_gateup, first_down) + [attend_project, attend_output.T], axis=1
+    )
+    second_pack = jnp.concatenate(pack_ffn(second_gateup, second_down), axis=1)
+    mixer_pack = spread_pack(mixer_pack)
+    arrived, mixer_pack = lax.optimization_barrier((arrived, mixer_pack))
     first_all = lax.all_gather(first_pack, TOKEN_AXES, axis=0, tiled=True)
     second_all = lax.all_gather(second_pack, TOKEN_AXES, axis=0, tiled=True)
     project_b = first_all[:, ffn_width : ffn_width + attend_project.shape[1]]
@@ -1009,15 +1026,8 @@
         concat_axis=0,
         tiled=True,
     )
-    mixer_home = lax.all_to_all(
-        partial.reshape(shards, depth, mixer_cols),
-        TOKEN_AXES,
-        split_axis=0,
-        concat_axis=0,
-        tiled=True,
-    )
     second_grads = finish(second_sums, steps, hidden)
-    home, mixer_home, second_grads = lax.optimization_barrier((home, mixer_home, second_grads))
+    home, partial, second_grads = lax.optimization_barrier((home, partial, second_grads))
     place = jnp.arange(2 * chunk + 8)
     small_line = (place == 2 * chunk) | (place == 2 * chunk + 1)
     wanted = (
@@ -1034,6 +1044,13 @@
     rounded = payload.astype(BF16).astype(F32)
     payload = jnp.where((place == 2 * chunk + 1)[:, None], payload - rounded, payload)
     last = tp_gather(payload.astype(BF16))
+    mixer_home = lax.all_to_all(
+        partial.reshape(shards, depth, mixer_cols),
+        TOKEN_AXES,
+        split_axis=0,
+        concat_axis=0,
+        tiled=True,
+    )
     home_rows = (
         jnp.repeat(jnp.tile(send_piece, members), part_rows) * piece_rows
         + member_of * part_rows

time: 545 us -> 523 us (0.960)
  the two profiles are of different devices: /device:TPU:1 before, /device:TPU:27 now
where the time goes in v2:
time: 523 us; the launch traced here: 513 us
  waiting for transfers between devices  167 us (32%)
  starting transfers between devices  120 us (23%)
  Pallas kernels  90.1 us (17%)
  local copies, waits for them, and re-layouts  58.5 us (11%)
  matrix products  31.5 us (6%)
  other arithmetic  28.7 us (5%)
  between operations  16.9 us (3%)
    ppermute x48, waiting for transfers between devices, shift_tp(): lax.ppermute(block, 'tp', [(i, (i + distance) % members) for i in range(m...  88.9 us
    ppermute x48, starting transfers between devices, shift_tp(): lax.ppermute(block, 'tp', [(i, (i + distance) % members) for i in range(m...  59.2 us
    pallas_call x2, Pallas kernels, ffn_backward(): pl.pallas_call(functools.partial(ffn_backward_kernel, count, len(back_chu...  29.6 us
    all_to_all x1, waiting for transfers between devices, gather_pack(): lax.all_to_all(spread, CHIP_AXES, split_axis=0, concat_axis=0, tiled=True)  26.3 us
    ppermute x15, starting transfers between devices, swap_core(): return lax.ppermute(block, 'core', [(0, 1), (1, 0)])  26.2 us
    pallas_call x4, Pallas kernels, gradient(): pl.pallas_call(functools.partial(gradient_kernel, edge, cut), grid=(steps...  26 us
    pallas_call x11, Pallas kernels, one_step(): pl.pallas_call(kernel, grid=(1,), in_specs=[whole(v.shape) for v in opera...  21 us
    dot_general x10, matrix products, times(): lax.dot_general(left, right, (((1,), (0,)), ((), ())), preferred_element_...  18 us
  transfers between devices with their start and end apart: 75, of which 38 were waited for; matrix products, arithmetic and copies ran while one was open for 18% of the time, Pallas kernels for 15%

profile of v2, /device:TPU:27, one launch (start us, length us, event | category | flops | bytes accessed | tf_op | source)
XLA Modules:
  0.0 512.7 jit_solution(2224212593615912018)
XLA Ops:
  18.4 8.8 %all-to-all-start = ((bf16[32,5,1536]{2,1,0:T(8,128)(2,1)}), bf16[32,5,1536]{2,1,0:T(8,128)(2,1)S(1)}, u32[]{:S(2)}, u32[]{:S(2)}) async-start(bf16[32,5,1536]{2,1,0:T(8,128)(2,1)} %pad_maximum_fusion), calls=%async_computation | async-start | bytes 1572864 | tf_op jit(solution)/shard_map/all_to_all | solution.py:704
  34.3 10.4 %all-to-all-done = bf16[32,5,1536]{2,1,0:T(8,128)(2,1)S(1)} async-done(((bf16[32,5,1536]{2,1,0:T(8,128)(2,1)}), bf16[32,5,1536]{2,1,0:T(8,128)(2,1)S(1)}, u32[]{:S(2)}, u32[]{:S(2)}) %all-to-all-start) | async-done | bytes 491552 | tf_op jit(solution)/shard_map/all_to_all | solution.py:704
  46.5 5.8 %all-to-all-start.1 = ((bf16[16,48,1536]{2,1,0:T(8,128)(2,1)}), bf16[16,48,1536]{2,1,0:T(8,128)(2,1)S(1)}, u32[]{:S(2)}, u32[]{:S(2)}) async-start(bf16[16,48,1536]{2,1,0:T(8,128)(2,1)} %broadcast_in_dim.84), calls=%async_computation.1 | async-start | bytes 4718592 | tf_op jit(solution)/shard_map/all_to_all | solution.py:555
  66.4 4.0 collective-permute-done
  72.1 26.3 %all-to-all-done.1 = bf16[16,48,1536]{2,1,0:T(8,128)(2,1)S(1)} async-done(((bf16[16,48,1536]{2,1,0:T(8,128)(2,1)}), bf16[16,48,1536]{2,1,0:T(8,128)(2,1)S(1)}, u32[]{:S(2)}, u32[]{:S(2)}) %all-to-all-start.1) | async-done | bytes 2359328 | tf_op jit(solution)/shard_map/all_to_all | solution.py:555
  98.4 5.4 %collective-permute-start.4 = (bf16[16,48,1536]{2,1,0:T(8,128)(2,1)S(1)}, bf16[16,48,1536]{2,1,0:T(8,128)(2,1)S(1)}, u32[]{:S(2)}, u32[]{:S(2)}) collective-permute-start(bf16[16,48,1536]{2,1,0:T(8,128)(2,1)S(1)} %all-to-all-done.1), channel_id=1, source_target_pairs={{0,4},{4,0},{1,5},{5,1},{2,6},{6,2},{3,7},{7,3},{8,12},{12,8},{9,1... | collective-permute-start | bytes 7077896 | tf_op jit(solution)/shard_map/ppermute | solution.py:72
  116.2 3.0 fusion.140
  125.2 7.6 %collective-permute-done.5.refs_1_ = bf16[64,1536]{1,0:T(8,128)(2,1)S(1)} collective-permute-done((bf16[64,1536]{1,0:T(8,128)(2,1)}, bf16[64,1536]{1,0:T(8,128)(2,1)S(1)}, u32[]{:S(2)}, u32[]{:S(2)}) %collective-permute-start.5) | collective-permute-done | bytes 196640 | tf_op jit(solution)/shard_map/ppermute | solution.py:77
  140.2 4.9 collective-permute-done.9.refs_2_
  145.1 11.2 %ffn_forward.1 = (f32[64,1536]{1,0:T(8,128)S(1)}, bf16[64,1536]{1,0:T(8,128)(2,1)}, bf16[64,1536]{1,0:T(8,128)(2,1)}, bf16[64,1536]{1,0:T(8,128)(2,1)S(1)}) custom-call(bf16[64,1536]{1,0:T(8,128)(2,1)S(1)} %get-tuple-element.129.refs_0_, bf16[64,1536]{1,0:T(8,128)(2,1)S(1)} %collective-permute-done.8.refs_1_, ...), custom_call_target="tpu_custom_call" | custom-call | flops 4227858432 | bytes 16515072 | tf_op jit(solution)/shard_map/ffn_forward/pallas_call | solution.py:239
  159.7 3.0 collective-permute-done.11.refs_1_
  162.7 3.2 collective-permute-done.12.refs_2_
  167.8 3.7 collective-permute-start.14
  172.2 7.1 %collective-permute-done.14 = bf16[64,1536]{1,0:T(8,128)(2,1)S(1)} collective-permute-done((bf16[64,1536]{1,0:T(8,128)(2,1)S(1)}, bf16[64,1536]{1,0:T(8,128)(2,1)S(1)}, u32[]{:S(2)}, u32[]{:S(2)}) %collective-permute-start.14) | collective-permute-done | bytes 196640 | tf_op jit(solution)/shard_map/ppermute | solution.py:77
  179.4 4.2 collective-permute-done.16
  186.0 2.5 heads.1
  188.8 7.6 %collective-permute-done.17 = bf16[256,256]{1,0:T(8,128)(2,1)S(1)} collective-permute-done((bf16[256,256]{1,0:T(8,128)(2,1)S(1)}, bf16[256,256]{1,0:T(8,128)(2,1)S(1)}, u32[]{:S(2)}, u32[]{:S(2)}) %collective-permute-start.17) | collective-permute-done | bytes 131104 | tf_op jit(solution)/shard_map/ppermute | solution.py:68
  198.9 5.3 %attend.1 = bf16[256,384]{1,0:T(8,128)(2,1)S(1)} custom-call(bf16[256,384]{1,0:T(8,128)(2,1)S(1)} %get-tuple-element.140.q_ref, bf16[1024,256]{1,0:T(8,128)(2,1)S(1)} %pad_maximum_fusion.3.kv_ref, bf16[1024,256]{1,0:T(8,128)(2,1)S(1)} %select_convert_fusion.barred_ref), custom_call_target="tpu_custom_call" | custom-call | flops 402653184 | bytes 1441792 | tf_op jit(solution)/shard_map/attend/pallas_call | solution.py:137
  204.2 3.1 fusion.141
  214.0 5.9 %collective-permute-done.19.refs_1_ = bf16[64,1536]{1,0:T(8,128)(2,1)S(1)} collective-permute-done((bf16[64,1536]{1,0:T(8,128)(2,1)}, bf16[64,1536]{1,0:T(8,128)(2,1)S(1)}, u32[]{:S(2)}, u32[]{:S(2)}) %collective-permute-start.19) | collective-permute-done | bytes 196640 | tf_op jit(solution)/shard_map/ppermute | solution.py:77
  223.6 3.4 collective-permute-start.22
  227.6 7.8 %collective-permute-done.22.refs_1_ = bf16[64,1536]{1,0:T(8,128)(2,1)} collective-permute-done((bf16[64,1536]{1,0:T(8,128)(2,1)}, bf16[64,1536]{1,0:T(8,128)(2,1)}, u32[]{:S(2)}, u32[]{:S(2)}) %collective-permute-start.22) | collective-permute-done | bytes 196640 | tf_op jit(solution)/shard_map/ppermute | solution.py:77
  235.4 3.9 collective-permute-done.24.refs_3_
  239.3 15.4 %ffn_both.1 = (f32[64,1536]{1,0:T(8,128)S(1)}, bf16[64,1536]{1,0:T(8,128)(2,1)S(1)}, bf16[64,1536]{1,0:T(8,128)(2,1)S(1)}, bf16[64,1536]{1,0:T(8,128)(2,1)S(1)},...) custom-call(s32[1]{0:T(128)} %bitcast.core_ref, ...), custom_call_target="tpu_custom_call" | custom-call | flops 8455716864 | bytes 22413312 | tf_op jit(solution)/shard_map/ffn_both/pallas_call | solution.py:330
  258.9 9.3 %collective-permute-done.25.refs_1_ = bf16[64,1536]{1,0:T(8,128)(2,1)S(1)} collective-permute-done((bf16[64,1536]{1,0:T(8,128)(2,1)S(1)}, bf16[64,1536]{1,0:T(8,128)(2,1)S(1)}, u32[]{:S(2)}, u32[]{:S(2)}) %collective-permute-start.25) | collective-permute-done | bytes 196640 | tf_op jit(solution)/shard_map/ppermute | solution.py:77
  276.9 10.4 %weight_gradient.4 = bf16[1536,2688]{1,0:T(8,128)(2,1)} custom-call(bf16[256,5760]{1,0:T(8,128)(2,1)S(1)} %copy-done, bf16[256,5760]{1,0:T(8,128)(2,1)} %copy-done.51, bf16[256,5760]{1,0:T(8,128)(2,1)S(1)} %copy-done, bf16[256,5760]{1,0:T(8,128)(2,1)} %copy-done.51, bf16[256,2688]{1,0:T(8,128)(2,1)S(1)} %get-tuple-element.153.refs_4_, ...), custom_call_target="tpu_custom_call" | custom-call | flops 4227858432 | bytes 8257536 | tf_op jit(solution)/shard_map/weight_gradient/pallas_call | solution.py:399
  292.3 7.7 %attend_backward.1 = (bf16[256,384]{1,0:T(8,128)(2,1)S(1)}, f32[512,256]{1,0:T(8,128)S(1)}, bf16[512,256]{1,0:T(8,128)(2,1)S(1)}, f32[1,64]{1,0:T(1,128)S(1)}) custom-call(bf16[256,384]{1,0:T(8,128)(2,1)S(1)} %copy-done.48, bf16[256,384]{1,0:T(8,128)(2,1)S(1)} %convolution_convert_fusion.5.do_ref, bf16[1024,256]{1,0:T(8,128)(2,1)S(1)} %copy-done.26, ...), custom_call_target="tpu_custom_call" | custom-call | flops 1006632960 | bytes 3146240 | tf_op jit(solution)/shard_map/attend_backward/pallas_call | solution.py:137
  303.1 6.7 %collective-permute-done.33.far_ref = bf16[256,256]{1,0:T(8,128)(2,1)S(1)} collective-permute-done((bf16[256,256]{1,0:T(8,128)(2,1)S(1)}, bf16[256,256]{1,0:T(8,128)(2,1)S(1)}, u32[]{:S(2)}, u32[]{:S(2)}) %collective-permute-start.33) | collective-permute-done | bytes 131104 | tf_op jit(solution)/shard_map/ppermute | solution.py:68
  313.3 3.1 collective-permute-start.34
  319.7 3.3 collective-permute-start.43
  322.9 2.7 collective-permute-done.35.refs_2_
  330.9 3.6 weight_gradient.5.refs_6_
  334.8 5.8 %collective-permute-done.39.refs_7_ = bf16[64,1536]{1,0:T(8,128)(2,1)S(1)} collective-permute-done((bf16[64,1536]{1,0:T(8,128)(2,1)S(1)}, bf16[64,1536]{1,0:T(8,128)(2,1)S(1)}, u32[]{:S(2)}, u32[]{:S(2)}) %collective-permute-start.39) | collective-permute-done | bytes 196640 | tf_op jit(solution)/shard_map/ppermute | solution.py:77
  340.6 14.2 %ffn_backward.1 = (f32[64,1536]{1,0:T(8,128)S(1)}, bf16[64,1536]{1,0:T(8,128)(2,1)}, bf16[64,1536]{1,0:T(8,128)(2,1)}, bf16[64,1536]{1,0:T(8,128)(2,1)S(1)}, bf1...) custom-call(s32[1]{0:T(128)} %bitcast.core_ref, bf16[64,1536]{1,0:T(8,128)(2,1)S(1)} %copy-done.2, ...), custom_call_target="tpu_custom_call" | custom-call | flops 7046430720 | bytes 19267584 | tf_op jit(solution)/shard_map/ffn_backward/pallas_call | solution.py:330
  356.1 3.7 collective-permute-done.44.refs_3_
  363.7 8.7 %weight_gradient.6 = bf16[1536,3200]{1,0:T(8,128)(2,1)} custom-call(bf16[256,1536]{1,0:T(8,128)(2,1)S(1)} %constant_dynamic-update-slice_fusion.10.refs_0_, bf16[256,1536]{1,0:T(8,128)(2,1)S(1)} %collective-permute-done.43.refs_1_, bf16[256,1536]{1,0:T(8,128)(2,1)S(1)} %constant_dynamic-update-slice_fusion.14.refs_2_, ...), custom_call_target="tpu_custom_call", output_to_operand_aliasing={{}: (6, {})} | custom-call | flops 4227858432 | bytes 8257536 | tf_op jit(solution)/shard_map/weight_gradient/pallas_call | solution.py:399
  386.2 4.3 collective-permute-start.55
  393.1 3.0 multiply_reduce_fusion.3
  397.2 2.5 collective-permute-start.52
  403.5 5.1 fusion.143
  418.0 4.7 collective-permute-start.61
  428.0 7.6 %all-to-all-start.2 = ((bf16[32,8,1536]{2,1,0:T(8,128)(2,1)}), bf16[32,8,1536]{2,1,0:T(8,128)(2,1)}, u32[]{:S(2)}, u32[]{:S(2)}) async-start(bf16[32,8,1536]{2,1,0:T(8,128)(2,1)} %fusion.4), calls=%async_computation.3 | async-start | bytes 1572864 | tf_op jit(solution)/shard_map/all_to_all | solution.py:1022
  438.3 3.3 weight_gradient.7
  442.8 6.7 %all-to-all-done.2 = bf16[32,8,1536]{2,1,0:T(8,128)(2,1)} async-done(((bf16[32,8,1536]{2,1,0:T(8,128)(2,1)}), bf16[32,8,1536]{2,1,0:T(8,128)(2,1)}, u32[]{:S(2)}, u32[]{:S(2)}) %all-to-all-start.2) | async-done | bytes 786464 | tf_op jit(solution)/shard_map/all_to_all | solution.py:1022
  454.5 7.1 %all-to-all-start.3 = ((bf16[32,48,768]{2,1,0:T(8,128)(2,1)}), bf16[32,48,768]{2,1,0:T(8,128)(2,1)S(1)}, u32[]{:S(2)}, u32[]{:S(2)}) async-start(bf16[32,48,768]{2,1,0:T(8,128)(2,1)} %bitcast.101), calls=%async_computation.5 | async-start | bytes 4718592 | tf_op jit(solution)/shard_map/all_to_all | solution.py:1047
  465.7 9.8 %collective-permute-done.65 = bf16[136,1536]{1,0:T(8,128)(2,1)S(1)} collective-permute-done((bf16[136,1536]{1,0:T(8,128)(2,1)}, bf16[136,1536]{1,0:T(8,128)(2,1)S(1)}, u32[]{:S(2)}, u32[]{:S(2)}) %collective-permute-start.65) | collective-permute-done | bytes 417824 | tf_op jit(solution)/shard_map/ppermute | solution.py:77
  481.4 13.5 %reduce-scatter.3.cloned.1.call-done.sum_ref = bf16[96,3200]{1,0:T(8,128)(2,1)} async-done(((bf16[1536,3200]{1,0:T(8,128)(2,1)}), bf16[96,3200]{1,0:T(8,128)(2,1)}) %reduce-scatter.3.cloned.1.call-update) | async-done | bytes 614416 | tf_op jit(solution)/shard_map/reduce_scatter | solution.py:545
  495.9 3.6 collective-permute-start.66
  (587 shorter events, 181.9 us)
Async XLA Ops:
  7.2 137.8 %all-gather.3.cloned.1.call-start = ((), (), s32[]{:S(2)}) async-start(), calls=%async_computation.6 | async-start | bytes 20275200 | tf_op jit(solution)/shard_map/all_gather | solution.py:718
  16.4 211.2 %all-gather.5.cloned.1.call-start = ((), (), s32[]{:S(2)}) async-start(), calls=%async_computation.7 | async-start | bytes 17031168 | tf_op jit(solution)/shard_map/all_gather | solution.py:719
  18.4 26.4 %all-to-all-start = ((bf16[32,5,1536]{2,1,0:T(8,128)(2,1)}), bf16[32,5,1536]{2,1,0:T(8,128)(2,1)S(1)}, u32[]{:S(2)}, u32[]{:S(2)}) async-start(bf16[32,5,1536]{2,1,0:T(8,128)(2,1)} %pad_maximum_fusion), calls=%async_computation | async-start | bytes 1572864 | tf_op jit(solution)/shard_map/all_to_all | solution.py:704
  46.5 51.9 %all-to-all-start.1 = ((bf16[16,48,1536]{2,1,0:T(8,128)(2,1)}), bf16[16,48,1536]{2,1,0:T(8,128)(2,1)S(1)}, u32[]{:S(2)}, u32[]{:S(2)}) async-start(bf16[16,48,1536]{2,1,0:T(8,128)(2,1)} %broadcast_in_dim.84), calls=%async_computation.1 | async-start | bytes 4718592 | tf_op jit(solution)/shard_map/all_to_all | solution.py:555
  52.4 383.2 %reduce-scatter.5.cloned.1.call-start = ((), (), s32[]{:S(2)}) async-start(), calls=%async_computation.9 | async-start | bytes 8773632 | tf_op jit(solution)/shard_map/reduce_scatter | solution.py:545
  61.3 42.6 %collective-permute-start.1 = (bf16[128,1536]{1,0:T(8,128)(2,1)}, bf16[128,1536]{1,0:T(8,128)(2,1)}, u32[]{:S(2)}, u32[]{:S(2)}) collective-permute-start(bf16[128,1536]{1,0:T(8,128)(2,1)} %get-tuple-element.347), channel_id=1, source_target_pairs={{0,2},{1,3},{2,0},{3,1},{4,6},{5,7},{6,4},{7,5},{8,10},{9,11},{10,... | collective-permute-start | bytes 1179656 | tf_op jit(solution)/shard_map/ppermute | solution.py:77
  63.4 42.1 %collective-permute-start.2 = (bf16[128,1536]{1,0:T(8,128)(2,1)}, bf16[128,1536]{1,0:T(8,128)(2,1)}, u32[]{:S(2)}, u32[]{:S(2)}) collective-permute-start(bf16[128,1536]{1,0:T(8,128)(2,1)} %get-tuple-element.347), channel_id=1, source_target_pairs={{0,3},{1,0},{2,1},{3,2},{4,7},{5,4},{6,5},{7,6},{8,11},{9,8},{10,9... | collective-permute-start | bytes 1179656 | tf_op jit(solution)/shard_map/ppermute | solution.py:77
  98.4 13.3 %collective-permute-start.4 = (bf16[16,48,1536]{2,1,0:T(8,128)(2,1)S(1)}, bf16[16,48,1536]{2,1,0:T(8,128)(2,1)S(1)}, u32[]{:S(2)}, u32[]{:S(2)}) collective-permute-start(bf16[16,48,1536]{2,1,0:T(8,128)(2,1)S(1)} %all-to-all-done.1), channel_id=1, source_target_pairs={{0,4},{4,0},{1,5},{5,1},{2,6},{6,2},{3,7},{7,3},{8,12},{12,8},{9,1... | collective-permute-start | bytes 7077896 | tf_op jit(solution)/shard_map/ppermute | solution.py:72
  121.1 11.7 %collective-permute-start.5 = (bf16[64,1536]{1,0:T(8,128)(2,1)}, bf16[64,1536]{1,0:T(8,128)(2,1)S(1)}, u32[]{:S(2)}, u32[]{:S(2)}) collective-permute-start(bf16[64,1536]{1,0:T(8,128)(2,1)} %get-tuple-element.319), channel_id=1, source_target_pairs={{0,3},{1,0},{2,1},{3,2},{4,7},{5,4},{6,5},{7,6},{8,11},{9,8},{10,9... | collective-permute-start | bytes 589832 | tf_op jit(solution)/shard_map/ppermute | solution.py:77
  121.3 11.5 %collective-permute-start.6 = (bf16[64,1536]{1,0:T(8,128)(2,1)}, bf16[64,1536]{1,0:T(8,128)(2,1)S(1)}, u32[]{:S(2)}, u32[]{:S(2)}) collective-permute-start(bf16[64,1536]{1,0:T(8,128)(2,1)} %get-tuple-element.318), channel_id=1, source_target_pairs={{0,2},{1,3},{2,0},{3,1},{4,6},{5,7},{6,4},{7,5},{8,10},{9,11},{10,... | collective-permute-start | bytes 589832 | tf_op jit(solution)/shard_map/ppermute | solution.py:77
  121.6 11.5 %collective-permute-start.7 = (bf16[64,1536]{1,0:T(8,128)(2,1)S(1)}, bf16[64,1536]{1,0:T(8,128)(2,1)S(1)}, u32[]{:S(2)}, u32[]{:S(2)}) collective-permute-start(bf16[64,1536]{1,0:T(8,128)(2,1)S(1)} %get-tuple-element.317), channel_id=1, source_target_pairs={{0,1},{1,2},{2,3},{3,0},{4,5},{5,6},{6,7},{7,4},{8,9},{9,10},{10,1... | collective-permute-start | bytes 589832 | tf_op jit(solution)/shard_map/ppermute | solution.py:77
  167.8 11.5 %collective-permute-start.14 = (bf16[64,1536]{1,0:T(8,128)(2,1)S(1)}, bf16[64,1536]{1,0:T(8,128)(2,1)S(1)}, u32[]{:S(2)}, u32[]{:S(2)}) collective-permute-start(bf16[64,1536]{1,0:T(8,128)(2,1)S(1)} %get-tuple-element.139), channel_id=1, source_target_pairs={{0,1},{1,2},{2,3},{3,0},{4,5},{5,6},{6,7},{7,4},{8,9},{9,10},{10,1... | collective-permute-start | bytes 589832 | tf_op jit(solution)/shard_map/ppermute | solution.py:77
  171.5 12.0 %collective-permute-start.16 = (bf16[64,1536]{1,0:T(8,128)(2,1)S(1)}, bf16[64,1536]{1,0:T(8,128)(2,1)S(1)}, u32[]{:S(2)}, u32[]{:S(2)}) collective-permute-start(bf16[64,1536]{1,0:T(8,128)(2,1)S(1)} %get-tuple-element.139), channel_id=1, source_target_pairs={{0,3},{1,0},{2,1},{3,2},{4,7},{5,4},{6,5},{7,6},{8,11},{9,8},{10,9... | collective-permute-start | bytes 589832 | tf_op jit(solution)/shard_map/ppermute | solution.py:77
  208.1 11.8 %collective-permute-start.19 = (bf16[64,1536]{1,0:T(8,128)(2,1)}, bf16[64,1536]{1,0:T(8,128)(2,1)S(1)}, u32[]{:S(2)}, u32[]{:S(2)}) collective-permute-start(bf16[64,1536]{1,0:T(8,128)(2,1)} %get-tuple-element.316), channel_id=1, source_target_pairs={{0,3},{1,0},{2,1},{3,2},{4,7},{5,4},{6,5},{7,6},{8,11},{9,8},{10,9... | collective-permute-start | bytes 589832 | tf_op jit(solution)/shard_map/ppermute | solution.py:77
  208.1 11.8 %collective-permute-start.20 = (bf16[64,1536]{1,0:T(8,128)(2,1)}, bf16[64,1536]{1,0:T(8,128)(2,1)S(1)}, u32[]{:S(2)}, u32[]{:S(2)}) collective-permute-start(bf16[64,1536]{1,0:T(8,128)(2,1)} %get-tuple-element.315), channel_id=1, source_target_pairs={{0,2},{1,3},{2,0},{3,1},{4,6},{5,7},{6,4},{7,5},{8,10},{9,11},{10,... | collective-permute-start | bytes 589832 | tf_op jit(solution)/shard_map/ppermute | solution.py:77
  209.5 10.8 %collective-permute-start.21 = (bf16[64,1536]{1,0:T(8,128)(2,1)}, bf16[64,1536]{1,0:T(8,128)(2,1)}, u32[]{:S(2)}, u32[]{:S(2)}) collective-permute-start(bf16[64,1536]{1,0:T(8,128)(2,1)} %get-tuple-element.314), channel_id=1, source_target_pairs={{0,1},{1,2},{2,3},{3,0},{4,5},{5,6},{6,7},{7,4},{8,9},{9,10},{10,1... | collective-permute-start | bytes 589832 | tf_op jit(solution)/shard_map/ppermute | solution.py:77
  223.6 11.8 %collective-permute-start.22 = (bf16[64,1536]{1,0:T(8,128)(2,1)}, bf16[64,1536]{1,0:T(8,128)(2,1)}, u32[]{:S(2)}, u32[]{:S(2)}) collective-permute-start(bf16[64,1536]{1,0:T(8,128)(2,1)} %get-tuple-element.143.refs_0_), channel_id=1, source_target_pairs={{0,1},{1,2},{2,3},{3,0},{4,5},{5,6},{6,7},{7,4},{8,9},{9,10},{10,1... | collective-permute-start | bytes 589832 | tf_op jit(solution)/shard_map/ppermute | solution.py:77
  227.0 12.3 %collective-permute-start.24 = (bf16[64,1536]{1,0:T(8,128)(2,1)}, bf16[64,1536]{1,0:T(8,128)(2,1)}, u32[]{:S(2)}, u32[]{:S(2)}) collective-permute-start(bf16[64,1536]{1,0:T(8,128)(2,1)} %get-tuple-element.143.refs_0_), channel_id=1, source_target_pairs={{0,3},{1,0},{2,1},{3,2},{4,7},{5,4},{6,5},{7,6},{8,11},{9,8},{10,9... | collective-permute-start | bytes 589832 | tf_op jit(solution)/shard_map/ppermute | solution.py:77
  255.6 17.8 %collective-permute-start.31 = (bf16[256,5760]{1,0:T(8,128)(2,1)}, bf16[256,5760]{1,0:T(8,128)(2,1)S(1)}, u32[]{:S(2)}, u32[]{:S(2)}) collective-permute-start(bf16[256,5760]{1,0:T(8,128)(2,1)} %get-tuple-element.152.refs_0_.refs_2_), channel_id=1, source_target_pairs={{0,4},{4,0},{1,5},{5,1},{2,6},{6,2},{3,7},{7,3},{8,12},{12,8},{9,1... | collective-permute-start | bytes 8847368 | tf_op jit(solution)/shard_map/ppermute | solution.py:72
  256.3 12.0 %collective-permute-start.25 = (bf16[64,1536]{1,0:T(8,128)(2,1)S(1)}, bf16[64,1536]{1,0:T(8,128)(2,1)S(1)}, u32[]{:S(2)}, u32[]{:S(2)}) collective-permute-start(bf16[64,1536]{1,0:T(8,128)(2,1)S(1)} %get-tuple-element.147), channel_id=1, source_target_pairs={{0,3},{1,0},{2,1},{3,2},{4,7},{5,4},{6,5},{7,6},{8,11},{9,8},{10,9... | collective-permute-start | bytes 589832 | tf_op jit(solution)/shard_map/ppermute | solution.py:77
  256.3 12.0 %collective-permute-start.26 = (bf16[64,1536]{1,0:T(8,128)(2,1)S(1)}, bf16[64,1536]{1,0:T(8,128)(2,1)S(1)}, u32[]{:S(2)}, u32[]{:S(2)}) collective-permute-start(bf16[64,1536]{1,0:T(8,128)(2,1)S(1)} %get-tuple-element.148), channel_id=1, source_target_pairs={{0,2},{1,3},{2,0},{3,1},{4,6},{5,7},{6,4},{7,5},{8,10},{9,11},{10,... | collective-permute-start | bytes 589832 | tf_op jit(solution)/shard_map/ppermute | solution.py:77
  258.0 10.5 %collective-permute-start.27 = (bf16[64,1536]{1,0:T(8,128)(2,1)S(1)}, bf16[64,1536]{1,0:T(8,128)(2,1)S(1)}, u32[]{:S(2)}, u32[]{:S(2)}) collective-permute-start(bf16[64,1536]{1,0:T(8,128)(2,1)S(1)} %get-tuple-element.149), channel_id=1, source_target_pairs={{0,1},{1,2},{2,3},{3,0},{4,5},{5,6},{6,7},{7,4},{8,9},{9,10},{10,1... | collective-permute-start | bytes 589832 | tf_op jit(solution)/shard_map/ppermute | solution.py:77
  270.2 17.0 %collective-permute-start.28 = (bf16[64,1536]{1,0:T(8,128)(2,1)S(1)}, bf16[64,1536]{1,0:T(8,128)(2,1)S(1)}, u32[]{:S(2)}, u32[]{:S(2)}) collective-permute-start(bf16[64,1536]{1,0:T(8,128)(2,1)S(1)} %get-tuple-element.154), channel_id=1, source_target_pairs={{0,1},{1,2},{2,3},{3,0},{4,5},{5,6},{6,7},{7,4},{8,9},{9,10},{10,1... | collective-permute-start | bytes 589832 | tf_op jit(solution)/shard_map/ppermute | solution.py:77
  272.7 14.6 %collective-permute-start.29 = (bf16[64,1536]{1,0:T(8,128)(2,1)S(1)}, bf16[64,1536]{1,0:T(8,128)(2,1)}, u32[]{:S(2)}, u32[]{:S(2)}) collective-permute-start(bf16[64,1536]{1,0:T(8,128)(2,1)S(1)} %get-tuple-element.154), channel_id=1, source_target_pairs={{0,2},{1,3},{2,0},{3,1},{4,6},{5,7},{6,4},{7,5},{8,10},{9,11},{10,... | collective-permute-start | bytes 589832 | tf_op jit(solution)/shard_map/ppermute | solution.py:77
  272.8 14.5 %collective-permute-start.30 = (bf16[64,1536]{1,0:T(8,128)(2,1)S(1)}, bf16[64,1536]{1,0:T(8,128)(2,1)}, u32[]{:S(2)}, u32[]{:S(2)}) collective-permute-start(bf16[64,1536]{1,0:T(8,128)(2,1)S(1)} %get-tuple-element.154), channel_id=1, source_target_pairs={{0,3},{1,0},{2,1},{3,2},{4,7},{5,4},{6,5},{7,6},{8,11},{9,8},{10,9... | collective-permute-start | bytes 589832 | tf_op jit(solution)/shard_map/ppermute | solution.py:77
  287.3 207.5 %reduce-scatter.3.cloned.1.call-start = ((), (), s32[]{:S(2)}) async-start(), calls=%async_computation.8 | async-start | bytes 10444800 | tf_op jit(solution)/shard_map/reduce_scatter | solution.py:545
  301.5 27.2 %collective-permute-start.40 = (bf16[256,1536]{1,0:T(8,128)(2,1)S(1)}, bf16[256,1536]{1,0:T(8,128)(2,1)S(1)}, u32[]{:S(2)}, u32[]{:S(2)}) collective-permute-start(bf16[256,1536]{1,0:T(8,128)(2,1)S(1)} %constant_dynamic-update-slice_fusion.2.refs_0_), channel_id=1, source_target_pairs={{0,4},{4,0},{1,5},{5,1},{2,6},{6,2},{3,7},{7,3},{8,12},{12,8},{9,1... | collective-permute-start | bytes 2359304 | tf_op jit(solution)/shard_map/ppermute | solution.py:72
  301.8 28.4 %collective-permute-start.41 = (bf16[256,1536]{1,0:T(8,128)(2,1)S(1)}, bf16[256,1536]{1,0:T(8,128)(2,1)S(1)}, u32[]{:S(2)}, u32[]{:S(2)}) collective-permute-start(bf16[256,1536]{1,0:T(8,128)(2,1)S(1)} %constant_dynamic-update-slice_fusion.6), channel_id=1, source_target_pairs={{0,4},{4,0},{1,5},{5,1},{2,6},{6,2},{3,7},{7,3},{8,12},{12,8},{9,1... | collective-permute-start | bytes 2359304 | tf_op jit(solution)/shard_map/ppermute | solution.py:72
  317.4 10.1 %collective-permute-start.36 = (bf16[64,1536]{1,0:T(8,128)(2,1)S(1)}, bf16[64,1536]{1,0:T(8,128)(2,1)S(1)}, u32[]{:S(2)}, u32[]{:S(2)}) collective-permute-start(bf16[64,1536]{1,0:T(8,128)(2,1)S(1)} %get-tuple-element.311), channel_id=1, source_target_pairs={{0,1},{1,2},{2,3},{3,0},{4,5},{5,6},{6,7},{7,4},{8,9},{9,10},{10,1... | collective-permute-start | bytes 589832 | tf_op jit(solution)/shard_map/ppermute | solution.py:77
  319.7 36.4 %collective-permute-start.43 = (bf16[256,1536]{1,0:T(8,128)(2,1)S(1)}, bf16[256,1536]{1,0:T(8,128)(2,1)S(1)}, u32[]{:S(2)}, u32[]{:S(2)}) collective-permute-start(bf16[256,1536]{1,0:T(8,128)(2,1)S(1)} %constant_dynamic-update-slice_fusion.10.refs_0_), channel_id=1, source_target_pairs={{0,4},{4,0},{1,5},{5,1},{2,6},{6,2},{3,7},{7,3},{8,12},{12,8},{9,1... | collective-permute-start | bytes 2359304 | tf_op jit(solution)/shard_map/ppermute | solution.py:72
  330.2 10.4 %collective-permute-start.39 = (bf16[64,1536]{1,0:T(8,128)(2,1)S(1)}, bf16[64,1536]{1,0:T(8,128)(2,1)S(1)}, u32[]{:S(2)}, u32[]{:S(2)}) collective-permute-start(bf16[64,1536]{1,0:T(8,128)(2,1)S(1)} %get-tuple-element.164.refs_4_), channel_id=1, source_target_pairs={{0,3},{1,0},{2,1},{3,2},{4,7},{5,4},{6,5},{7,6},{8,11},{9,8},{10,9... | collective-permute-start | bytes 589832 | tf_op jit(solution)/shard_map/ppermute | solution.py:77
  359.8 12.6 %collective-permute-start.46 = (bf16[64,1536]{1,0:T(8,128)(2,1)}, bf16[64,1536]{1,0:T(8,128)(2,1)S(1)}, u32[]{:S(2)}, u32[]{:S(2)}) collective-permute-start(bf16[64,1536]{1,0:T(8,128)(2,1)} %get-tuple-element.178), channel_id=1, source_target_pairs={{0,3},{1,0},{2,1},{3,2},{4,7},{5,4},{6,5},{7,6},{8,11},{9,8},{10,9... | collective-permute-start | bytes 589832 | tf_op jit(solution)/shard_map/ppermute | solution.py:77
  359.9 12.6 %collective-permute-start.47 = (bf16[64,1536]{1,0:T(8,128)(2,1)}, bf16[64,1536]{1,0:T(8,128)(2,1)S(1)}, u32[]{:S(2)}, u32[]{:S(2)}) collective-permute-start(bf16[64,1536]{1,0:T(8,128)(2,1)} %get-tuple-element.179), channel_id=1, source_target_pairs={{0,2},{1,3},{2,0},{3,1},{4,6},{5,7},{6,4},{7,5},{8,10},{9,11},{10,... | collective-permute-start | bytes 589832 | tf_op jit(solution)/shard_map/ppermute | solution.py:77
  361.3 11.2 %collective-permute-start.48 = (bf16[64,1536]{1,0:T(8,128)(2,1)S(1)}, bf16[64,1536]{1,0:T(8,128)(2,1)S(1)}, u32[]{:S(2)}, u32[]{:S(2)}) collective-permute-start(bf16[64,1536]{1,0:T(8,128)(2,1)S(1)} %get-tuple-element.180), channel_id=1, source_target_pairs={{0,1},{1,2},{2,3},{3,0},{4,5},{5,6},{6,7},{7,4},{8,9},{9,10},{10,1... | collective-permute-start | bytes 589832 | tf_op jit(solution)/shard_map/ppermute | solution.py:77
  379.3 12.3 %collective-permute-start.51 = (bf16[64,1536]{1,0:T(8,128)(2,1)S(1)}, bf16[64,1536]{1,0:T(8,128)(2,1)}, u32[]{:S(2)}, u32[]{:S(2)}) collective-permute-start(bf16[64,1536]{1,0:T(8,128)(2,1)S(1)} %get-tuple-element.192), channel_id=1, source_target_pairs={{0,3},{1,0},{2,1},{3,2},{4,7},{5,4},{6,5},{7,6},{8,11},{9,8},{10,9... | collective-permute-start | bytes 589832 | tf_op jit(solution)/shard_map/ppermute | solution.py:77
  380.2 56.8 %collective-permute-start.59 = (bf16[256,1536]{1,0:T(8,128)(2,1)S(1)}, bf16[256,1536]{1,0:T(8,128)(2,1)S(1)}, u32[]{:S(2)}, u32[]{:S(2)}) collective-permute-start(bf16[256,1536]{1,0:T(8,128)(2,1)S(1)} %multiply_convert_fusion.refs_0_), channel_id=1, source_target_pairs={{0,4},{4,0},{1,5},{5,1},{2,6},{6,2},{3,7},{7,3},{8,12},{12,8},{9,1... | collective-permute-start | bytes 2359304 | tf_op jit(solution)/shard_map/ppermute | solution.py:72
  381.8 20.9 %collective-permute-start.53 = (bf16[64,1536]{1,0:T(8,128)(2,1)}, bf16[64,1536]{1,0:T(8,128)(2,1)}, u32[]{:S(2)}, u32[]{:S(2)}) collective-permute-start(bf16[64,1536]{1,0:T(8,128)(2,1)} %get-tuple-element.193), channel_id=1, source_target_pairs={{0,3},{1,0},{2,1},{3,2},{4,7},{5,4},{6,5},{7,6},{8,11},{9,8},{10,9... | collective-permute-start | bytes 589832 | tf_op jit(solution)/shard_map/ppermute | solution.py:77
  384.7 18.0 %collective-permute-start.54 = (bf16[64,1536]{1,0:T(8,128)(2,1)}, bf16[64,1536]{1,0:T(8,128)(2,1)}, u32[]{:S(2)}, u32[]{:S(2)}) collective-permute-start(bf16[64,1536]{1,0:T(8,128)(2,1)} %get-tuple-element.194), channel_id=1, source_target_pairs={{0,2},{1,3},{2,0},{3,1},{4,6},{5,7},{6,4},{7,5},{8,10},{9,11},{10,... | collective-permute-start | bytes 589832 | tf_op jit(solution)/shard_map/ppermute | solution.py:77
  386.2 16.5 %collective-permute-start.55 = (bf16[64,1536]{1,0:T(8,128)(2,1)}, bf16[64,1536]{1,0:T(8,128)(2,1)}, u32[]{:S(2)}, u32[]{:S(2)}) collective-permute-start(bf16[64,1536]{1,0:T(8,128)(2,1)} %get-tuple-element.195), channel_id=1, source_target_pairs={{0,1},{1,2},{2,3},{3,0},{4,5},{5,6},{6,7},{7,4},{8,9},{9,10},{10,1... | collective-permute-start | bytes 589832 | tf_op jit(solution)/shard_map/ppermute | solution.py:77
  402.5 34.5 %collective-permute-start.60 = (bf16[256,1536]{1,0:T(8,128)(2,1)}, bf16[256,1536]{1,0:T(8,128)(2,1)}, u32[]{:S(2)}, u32[]{:S(2)}) collective-permute-start(bf16[256,1536]{1,0:T(8,128)(2,1)} %copy-done.124), channel_id=1, source_target_pairs={{0,4},{4,0},{1,5},{5,1},{2,6},{6,2},{3,7},{7,3},{8,12},{12,8},{9,1... | collective-permute-start | bytes 2359304 | tf_op jit(solution)/shard_map/ppermute | solution.py:72
  410.1 12.7 %collective-permute-start.57 = (bf16[64,1536]{1,0:T(8,128)(2,1)S(1)}, bf16[64,1536]{1,0:T(8,128)(2,1)S(1)}, u32[]{:S(2)}, u32[]{:S(2)}) collective-permute-start(bf16[64,1536]{1,0:T(8,128)(2,1)S(1)} %get-tuple-element.309), channel_id=1, source_target_pairs={{0,2},{1,3},{2,0},{3,1},{4,6},{5,7},{6,4},{7,5},{8,10},{9,11},{10,... | collective-permute-start | bytes 589832 | tf_op jit(solution)/shard_map/ppermute | solution.py:77
  412.1 10.6 %collective-permute-start.58 = (bf16[64,1536]{1,0:T(8,128)(2,1)S(1)}, bf16[64,1536]{1,0:T(8,128)(2,1)S(1)}, u32[]{:S(2)}, u32[]{:S(2)}) collective-permute-start(bf16[64,1536]{1,0:T(8,128)(2,1)S(1)} %get-tuple-element.308), channel_id=1, source_target_pairs={{0,1},{1,2},{2,3},{3,0},{4,5},{5,6},{6,7},{7,4},{8,9},{9,10},{10,1... | collective-permute-start | bytes 589832 | tf_op jit(solution)/shard_map/ppermute | solution.py:77
  418.0 20.2 %collective-permute-start.61 = (bf16[256,768]{1,0:T(8,128)(2,1)}, bf16[256,768]{1,0:T(8,128)(2,1)S(1)}, u32[]{:S(2)}, u32[]{:S(2)}) collective-permute-start(bf16[256,768]{1,0:T(8,128)(2,1)} %get-tuple-element.306), channel_id=1, source_target_pairs={{0,4},{4,0},{1,5},{5,1},{2,6},{6,2},{3,7},{7,3},{8,12},{12,8},{9,1... | collective-permute-start | bytes 1179656 | tf_op jit(solution)/shard_map/ppermute | solution.py:72
  428.0 21.4 %all-to-all-start.2 = ((bf16[32,8,1536]{2,1,0:T(8,128)(2,1)}), bf16[32,8,1536]{2,1,0:T(8,128)(2,1)}, u32[]{:S(2)}, u32[]{:S(2)}) async-start(bf16[32,8,1536]{2,1,0:T(8,128)(2,1)} %fusion.4), calls=%async_computation.3 | async-start | bytes 1572864 | tf_op jit(solution)/shard_map/all_to_all | solution.py:1022
  451.7 11.6 %collective-permute-start.63 = (bf16[136,1536]{1,0:T(8,128)(2,1)}, bf16[136,1536]{1,0:T(8,128)(2,1)}, u32[]{:S(2)}, u32[]{:S(2)}) collective-permute-start(bf16[136,1536]{1,0:T(8,128)(2,1)} %fusion.19), channel_id=1, source_target_pairs={{0,1},{1,2},{2,3},{3,0},{4,5},{5,6},{6,7},{7,4},{8,9},{9,10},{10,1... | collective-permute-start | bytes 1253384 | tf_op jit(solution)/shard_map/ppermute | solution.py:77
  453.1 12.5 %collective-permute-start.64 = (bf16[136,1536]{1,0:T(8,128)(2,1)}, bf16[136,1536]{1,0:T(8,128)(2,1)S(1)}, u32[]{:S(2)}, u32[]{:S(2)}) collective-permute-start(bf16[136,1536]{1,0:T(8,128)(2,1)} %fusion.19), channel_id=1, source_target_pairs={{0,2},{1,3},{2,0},{3,1},{4,6},{5,7},{6,4},{7,5},{8,10},{9,11},{10,... | collective-permute-start | bytes 1253384 | tf_op jit(solution)/shard_map/ppermute | solution.py:77
  454.5 21.0 %collective-permute-start.65 = (bf16[136,1536]{1,0:T(8,128)(2,1)}, bf16[136,1536]{1,0:T(8,128)(2,1)S(1)}, u32[]{:S(2)}, u32[]{:S(2)}) collective-permute-start(bf16[136,1536]{1,0:T(8,128)(2,1)} %fusion.19), channel_id=1, source_target_pairs={{0,3},{1,0},{2,1},{3,2},{4,7},{5,4},{6,5},{7,6},{8,11},{9,8},{10,9... | collective-permute-start | bytes 1253384 | tf_op jit(solution)/shard_map/ppermute | solution.py:77
  454.5 48.4 %all-to-all-start.3 = ((bf16[32,48,768]{2,1,0:T(8,128)(2,1)}), bf16[32,48,768]{2,1,0:T(8,128)(2,1)S(1)}, u32[]{:S(2)}, u32[]{:S(2)}) async-start(bf16[32,48,768]{2,1,0:T(8,128)(2,1)} %bitcast.101), calls=%async_computation.5 | async-start | bytes 4718592 | tf_op jit(solution)/shard_map/all_to_all | solution.py:1047
  (158 other events, 1503.2 us)
Sparse Core Ops, SparseCore 0:
  16.5 106.9 all-gather.2
  126.3 72.3 all-gather.4
  287.4 87.6 reduce-scatter.4
  378.5 116.3 reduce-scatter.2

commit v3 on v1

--- a/solution.py
+++ b/solution.py
@@ -471,7 +471,7 @@
 
 
 def attend_backward_kernel(
-    scale, q_ref, do_ref, kv_ref, barred_ref, raw_ref, cos_ref, sin_ref, gain_ref,
+    scale, first_ref, second_ref, third_ref, fourth_ref, weight_ref, q_ref, kv_ref, barred_ref, raw_ref, cos_ref, sin_ref, gain_ref,
     dq_ref, near_ref, cross_ref, gain_grad_ref,
 ):
     size = gain_ref.shape[1]
@@ -480,6 +480,10 @@
     rows = kv_ref.shape[0] // 4
     cosine, sine, gain = cos_ref[...], sin_ref[...], gain_ref[...]
     barred = barred_ref[...].astype(F32)
+    back = jnp.concatenate(
+        [ref[...] for ref in (first_ref, second_ref, third_ref, fourth_ref)], axis=0
+    )
+    d_attended = times(back, weight_ref[...]).astype(BF16)
     gain_grad = jnp.zeros_like(gain)
     for group in range(kv_heads):
         columns = slice(group * size, (group + 1) * size)
@@ -489,7 +493,7 @@
         for member in range(groups):
             head = group * groups + member
             head_columns = slice(head * size, (head + 1) * size)
-            query, d_out = q_ref[:, head_columns], do_ref[:, head_columns]
+            query, d_out = q_ref[:, head_columns], d_attended[:, head_columns]
             probs = head_probs(key, query, scale, barred)
             d_probs = times_t(value, d_out)
             inner = jnp.sum(probs * d_probs, axis=0, keepdims=True)
@@ -830,14 +834,11 @@
     back_b = tp_gather(back_b)
     back_b, partial = lax.optimization_barrier((back_b, partial))
     second_sums = sum_chips(partial)
-    back_b = jnp.concatenate(back_b)
-    back_b_other = swap_core(back_b)
     attend_in_other = swap_core(attend_in)
-    d_attended_b = times(back_b, output_b_t).astype(BF16)
     pair_rows = 2 * row_count
     d_query, near, cross, qgain_grad = one_step(
         functools.partial(attend_backward_kernel, score_scale),
-        [query_b, d_attended_b, key_value_all, barred, proj_b, cosine, sine, qgain_f],
+        [*back_b, output_b_t, query_b, key_value_all, barred, proj_b, cosine, sine, qgain_f],
         [
             jax.ShapeDtypeStruct(query_b.shape, BF16),
             jax.ShapeDtypeStruct((pair_rows, kv_width), F32),
@@ -848,6 +849,8 @@
         "attend_backward",
         5 * attend_flops,
     )
+    back_b = jnp.concatenate(back_b)
+    back_b_other = swap_core(back_b)
     cross = swap_core(cross)
     far = (near[row_count:] + cross[row_count:].astype(F32)).astype(BF16)
     d_proj_b, kgain_grad = one_step(
@@ -1009,15 +1012,8 @@
         concat_axis=0,
         tiled=True,
     )
-    mixer_home = lax.all_to_all(
-        partial.reshape(shards, depth, mixer_cols),
-        TOKEN_AXES,
-        split_axis=0,
-        concat_axis=0,
-        tiled=True,
-    )
     second_grads = finish(second_sums, steps, hidden)
-    home, mixer_home, second_grads = lax.optimization_barrier((home, mixer_home, second_grads))
+    home, partial, second_grads = lax.optimization_barrier((home, partial, second_grads))
     place = jnp.arange(2 * chunk + 8)
     small_line = (place == 2 * chunk) | (place == 2 * chunk + 1)
     wanted = (
@@ -1034,6 +1030,13 @@
     rounded = payload.astype(BF16).astype(F32)
     payload = jnp.where((place == 2 * chunk + 1)[:, None], payload - rounded, payload)
     last = tp_gather(payload.astype(BF16))
+    mixer_home = lax.all_to_all(
+        partial.reshape(shards, depth, mixer_cols),
+        TOKEN_AXES,
+        split_axis=0,
+        concat_axis=0,
+        tiled=True,
+    )
     home_rows = (
         jnp.repeat(jnp.tile(send_piece, members), part_rows) * piece_rows
         + member_of * part_rows

time: 545 us -> 523 us (0.960)
  waiting for transfers between devices: 208 us -> 173 us
  other arithmetic: 24.5 us -> 31.7 us
    all_to_all x1, waiting for transfers between devices: 35 us -> 6.42 us  [body(): lax.all_to_all(partial.reshape(shards, depth, mixer_cols), TOKEN_AXES, sp...]
    ppermute x48, waiting for transfers between devices: 114 us -> 103 us  [shift_tp(): lax.ppermute(block, 'tp', [(i, (i + distance) % members) for i in range(m...]
    unnamed x275 -> x289, local copies, waits for them, and re-layouts: 21.3 us -> 19.4 us
    dot_general x10 -> x9, matrix products: 17.3 us -> 16.3 us  [times(): lax.dot_general(left, right, (((1,), (0,)), ((), ())), preferred_element_...]
  transfers between devices with their start and end apart: 75 -> 75, of which waited for: 41 -> 39; matrix products, arithmetic and copies ran while one was open for 16% -> 20% of each run, Pallas kernels for 14% -> 15%
where the time goes in v3:
time: 523 us; the launch traced here: 513 us
  waiting for transfers between devices  173 us (33%)
  starting transfers between devices  104 us (20%)
  Pallas kernels  92.7 us (18%)
  local copies, waits for them, and re-layouts  65.8 us (13%)
  other arithmetic  31.7 us (6%)
  matrix products  29 us (6%)
  between operations  16.9 us (3%)
    ppermute x48, waiting for transfers between devices, shift_tp(): lax.ppermute(block, 'tp', [(i, (i + distance) % members) for i in range(m...  103 us
    ppermute x48, starting transfers between devices, shift_tp(): lax.ppermute(block, 'tp', [(i, (i + distance) % members) for i in range(m...  51 us
    pallas_call x2, Pallas kernels, ffn_backward(): pl.pallas_call(functools.partial(ffn_backward_kernel, count, len(back_chu...  29.3 us
    pallas_call x4, Pallas kernels, gradient(): pl.pallas_call(functools.partial(gradient_kernel, edge, cut), grid=(steps...  26.1 us
    pallas_call x11, Pallas kernels, one_step(): pl.pallas_call(kernel, grid=(1,), in_specs=[whole(v.shape) for v in opera...  23.9 us
    unnamed x289, local copies, waits for them, and re-layouts  19.4 us
    ppermute x15, starting transfers between devices, swap_core(): return lax.ppermute(block, 'core', [(0, 1), (1, 0)])  17.2 us
    dot_general x9, matrix products, times(): lax.dot_general(left, right, (((1,), (0,)), ((), ())), preferred_element_...  16.3 us
  transfers between devices with their start and end apart: 75, of which 39 were waited for; matrix products, arithmetic and copies ran while one was open for 20% of the time, Pallas kernels for 15%

profile of v3, /device:TPU:1, one launch (start us, length us, event | category | flops | bytes accessed | tf_op | source)
XLA Modules:
  0.0 513.0 jit_solution(10653698818011615789)
XLA Ops:
  14.3 9.4 %all-to-all-start = ((bf16[32,5,1536]{2,1,0:T(8,128)(2,1)}), bf16[32,5,1536]{2,1,0:T(8,128)(2,1)S(1)}, u32[]{:S(2)}, u32[]{:S(2)}) async-start(bf16[32,5,1536]{2,1,0:T(8,128)(2,1)} %pad_maximum_fusion), calls=%async_computation | async-start | bytes 1572864 | tf_op jit(solution)/shard_map/all_to_all | solution.py:703
  25.9 12.1 %all-to-all-done = bf16[32,5,1536]{2,1,0:T(8,128)(2,1)S(1)} async-done(((bf16[32,5,1536]{2,1,0:T(8,128)(2,1)}), bf16[32,5,1536]{2,1,0:T(8,128)(2,1)S(1)}, u32[]{:S(2)}, u32[]{:S(2)}) %all-to-all-start) | async-done | bytes 491552 | tf_op jit(solution)/shard_map/all_to_all | solution.py:703
  48.6 3.9 all-to-all-start.1
  63.3 2.6 collective-permute-start.1
  69.9 3.9 collective-permute-done
  75.6 13.8 %all-to-all-done.1 = bf16[16,48,1536]{2,1,0:T(8,128)(2,1)S(1)} async-done(((bf16[16,48,1536]{2,1,0:T(8,128)(2,1)}), bf16[16,48,1536]{2,1,0:T(8,128)(2,1)S(1)}, u32[]{:S(2)}, u32[]{:S(2)}) %all-to-all-start.1) | async-done | bytes 2359328 | tf_op jit(solution)/shard_map/all_to_all | solution.py:555
  95.1 3.7 collective-permute-start.3
  107.2 4.8 collective-permute-start.5
  115.0 3.7 collective-permute-done.5.refs_1_
  125.1 4.1 collective-permute-done.10.refs_3_
  129.1 5.3 %collective-permute-done.8.refs_1_ = bf16[64,1536]{1,0:T(8,128)(2,1)S(1)} collective-permute-done((bf16[64,1536]{1,0:T(8,128)(2,1)S(1)}, bf16[64,1536]{1,0:T(8,128)(2,1)S(1)}, u32[]{:S(2)}, u32[]{:S(2)}) %collective-permute-start.8) | collective-permute-done | bytes 196640 | tf_op jit(solution)/shard_map/ppermute | solution.py:77
  134.4 4.2 all-gather.3.cloned.1.call-done.refs_4_.refs_5_.refs_8_.refs_9_
  138.6 11.0 %ffn_forward.1 = (f32[64,1536]{1,0:T(8,128)S(1)}, bf16[64,1536]{1,0:T(8,128)(2,1)S(1)}, bf16[64,1536]{1,0:T(8,128)(2,1)}, bf16[64,1536]{1,0:T(8,128)(2,1)S(1)}) custom-call(bf16[64,1536]{1,0:T(8,128)(2,1)S(1)} %get-tuple-element.118.refs_0_, bf16[64,1536]{1,0:T(8,128)(2,1)S(1)} %collective-permute-done.8.refs_1_, ...), custom_call_target="tpu_custom_call" | custom-call | flops 4227858432 | bytes 16515072 | tf_op jit(solution)/shard_map/ffn_forward/pallas_call | solution.py:239
  149.7 2.5 collective-permute-start.11
  153.5 6.9 %collective-permute-done.11.refs_1_ = bf16[64,1536]{1,0:T(8,128)(2,1)S(1)} collective-permute-done((bf16[64,1536]{1,0:T(8,128)(2,1)S(1)}, bf16[64,1536]{1,0:T(8,128)(2,1)S(1)}, u32[]{:S(2)}, u32[]{:S(2)}) %collective-permute-start.11) | collective-permute-done | bytes 196640 | tf_op jit(solution)/shard_map/ppermute | solution.py:77
  160.3 4.7 collective-permute-done.13.refs_3_
  168.0 9.1 %collective-permute-done.14 = bf16[64,1536]{1,0:T(8,128)(2,1)S(1)} collective-permute-done((bf16[64,1536]{1,0:T(8,128)(2,1)S(1)}, bf16[64,1536]{1,0:T(8,128)(2,1)S(1)}, u32[]{:S(2)}, u32[]{:S(2)}) %collective-permute-start.14) | collective-permute-done | bytes 196640 | tf_op jit(solution)/shard_map/ppermute | solution.py:77
  183.1 7.0 %collective-permute-done.17 = bf16[256,256]{1,0:T(8,128)(2,1)S(1)} collective-permute-done((bf16[256,256]{1,0:T(8,128)(2,1)S(1)}, bf16[256,256]{1,0:T(8,128)(2,1)S(1)}, u32[]{:S(2)}, u32[]{:S(2)}) %collective-permute-start.17) | collective-permute-done | bytes 131104 | tf_op jit(solution)/shard_map/ppermute | solution.py:68
  190.2 2.6 collective-permute-start.18
  194.4 5.3 %attend.1 = bf16[256,384]{1,0:T(8,128)(2,1)S(1)} custom-call(bf16[256,384]{1,0:T(8,128)(2,1)S(1)} %get-tuple-element.126.q_ref, bf16[1024,256]{1,0:T(8,128)(2,1)S(1)} %pad_maximum_fusion.3.kv_ref, bf16[1024,256]{1,0:T(8,128)(2,1)S(1)} %select_convert_fusion.barred_ref), custom_call_target="tpu_custom_call" | custom-call | flops 402653184 | bytes 1441792 | tf_op jit(solution)/shard_map/attend/pallas_call | solution.py:137
  199.7 3.1 fusion.140
  210.1 3.1 collective-permute-done.20.refs_2_
  213.1 4.6 collective-permute-done.21.refs_3_
  223.8 8.8 %collective-permute-done.22.refs_1_ = bf16[64,1536]{1,0:T(8,128)(2,1)} collective-permute-done((bf16[64,1536]{1,0:T(8,128)(2,1)}, bf16[64,1536]{1,0:T(8,128)(2,1)}, u32[]{:S(2)}, u32[]{:S(2)}) %collective-permute-start.22) | collective-permute-done | bytes 196640 | tf_op jit(solution)/shard_map/ppermute | solution.py:77
  232.7 15.2 %ffn_both.1 = (f32[64,1536]{1,0:T(8,128)S(1)}, bf16[64,1536]{1,0:T(8,128)(2,1)S(1)}, bf16[64,1536]{1,0:T(8,128)(2,1)S(1)}, bf16[64,1536]{1,0:T(8,128)(2,1)S(1)},...) custom-call(s32[1]{0:T(128)} %bitcast.core_ref, ...), custom_call_target="tpu_custom_call" | custom-call | flops 8455716864 | bytes 22413312 | tf_op jit(solution)/shard_map/ffn_both/pallas_call | solution.py:330
  253.3 4.0 collective-permute-done.25.refs_1_
  257.3 3.1 collective-permute-done.26.refs_2_
  260.5 4.3 collective-permute-done.27.refs_3_
  273.6 10.4 %weight_gradient.4 = bf16[1536,2688]{1,0:T(8,128)(2,1)} custom-call(bf16[256,5760]{1,0:T(8,128)(2,1)S(1)} %copy-done, bf16[256,5760]{1,0:T(8,128)(2,1)} %copy-done.57, bf16[256,5760]{1,0:T(8,128)(2,1)S(1)} %copy-done, bf16[256,5760]{1,0:T(8,128)(2,1)} %copy-done.57, bf16[256,2688]{1,0:T(8,128)(2,1)S(1)} %get-tuple-element.137.refs_4_, ...), custom_call_target="tpu_custom_call" | custom-call | flops 4227858432 | bytes 8257536 | tf_op jit(solution)/shard_map/weight_gradient/pallas_call | solution.py:399
  288.1 9.4 %attend_backward.1 = (bf16[256,384]{1,0:T(8,128)(2,1)S(1)}, f32[512,256]{1,0:T(8,128)S(1)}, bf16[512,256]{1,0:T(8,128)(2,1)S(1)}, f32[1,64]{1,0:T(1,128)S(1)}) custom-call(bf16[64,1536]{1,0:T(8,128)(2,1)} %get-tuple-element.138.first_ref, bf16[64,1536]{1,0:T(8,128)(2,1)} %collective-permute-done.28.second_ref, ...), custom_call_target="tpu_custom_call" | custom-call | flops 1006632960 | bytes 4915712 | tf_op jit(solution)/shard_map/attend_backward/pallas_call | solution.py:137
  303.3 7.2 %collective-permute-done.33.far_ref = bf16[256,256]{1,0:T(8,128)(2,1)S(1)} collective-permute-done((bf16[256,256]{1,0:T(8,128)(2,1)S(1)}, bf16[256,256]{1,0:T(8,128)(2,1)S(1)}, u32[]{:S(2)}, u32[]{:S(2)}) %collective-permute-start.33) | collective-permute-done | bytes 131104 | tf_op jit(solution)/shard_map/ppermute | solution.py:68
  332.3 3.6 weight_gradient.5.refs_6_
  335.9 4.3 collective-permute-done.38.refs_6_
  340.2 14.1 %ffn_backward.1 = (f32[64,1536]{1,0:T(8,128)S(1)}, bf16[64,1536]{1,0:T(8,128)(2,1)}, bf16[64,1536]{1,0:T(8,128)(2,1)S(1)}, bf16[64,1536]{1,0:T(8,128)(2,1)S(1)},...) custom-call(s32[1]{0:T(128)} %bitcast.core_ref, bf16[64,1536]{1,0:T(8,128)(2,1)S(1)} %copy-done.8, ...), custom_call_target="tpu_custom_call" | custom-call | flops 7046430720 | bytes 19267584 | tf_op jit(solution)/shard_map/ffn_backward/pallas_call | solution.py:330
  355.7 3.7 collective-permute-done.44.refs_3_
  362.9 8.8 %weight_gradient.6 = bf16[1536,3200]{1,0:T(8,128)(2,1)} custom-call(bf16[256,1536]{1,0:T(8,128)(2,1)S(1)} %constant_dynamic-update-slice_fusion.10.refs_0_, bf16[256,1536]{1,0:T(8,128)(2,1)S(1)} %collective-permute-done.43.refs_1_, bf16[256,1536]{1,0:T(8,128)(2,1)S(1)} %constant_dynamic-update-slice_fusion.14.refs_2_, ...), custom_call_target="tpu_custom_call", output_to_operand_aliasing={{}: (6, {})} | custom-call | flops 4227858432 | bytes 8257536 | tf_op jit(solution)/shard_map/weight_gradient/pallas_call | solution.py:399
  371.7 2.6 collective-permute-done.48.refs_3_
  385.5 2.5 collective-permute-done.49
  392.5 3.0 multiply_reduce_fusion.3
  397.0 4.7 collective-permute-start.52
  410.4 5.1 fusion.142
  425.3 5.2 %collective-permute-done.58.refs_3_ = bf16[64,1536]{1,0:T(8,128)(2,1)S(1)} collective-permute-done((bf16[64,1536]{1,0:T(8,128)(2,1)S(1)}, bf16[64,1536]{1,0:T(8,128)(2,1)S(1)}, u32[]{:S(2)}, u32[]{:S(2)}) %collective-permute-start.58) | collective-permute-done | bytes 196640 | tf_op jit(solution)/shard_map/ppermute | solution.py:77
  435.7 6.6 %all-to-all-start.2 = ((bf16[32,8,1536]{2,1,0:T(8,128)(2,1)}), bf16[32,8,1536]{2,1,0:T(8,128)(2,1)}, u32[]{:S(2)}, u32[]{:S(2)}) async-start(bf16[32,8,1536]{2,1,0:T(8,128)(2,1)} %fusion.4), calls=%async_computation.3 | async-start | bytes 1572864 | tf_op jit(solution)/shard_map/all_to_all | solution.py:1008
  445.0 3.3 weight_gradient.7
  449.4 12.1 %all-to-all-done.2 = bf16[32,8,1536]{2,1,0:T(8,128)(2,1)} async-done(((bf16[32,8,1536]{2,1,0:T(8,128)(2,1)}), bf16[32,8,1536]{2,1,0:T(8,128)(2,1)}, u32[]{:S(2)}, u32[]{:S(2)}) %all-to-all-start.2) | async-done | bytes 786464 | tf_op jit(solution)/shard_map/all_to_all | solution.py:1008
  466.4 5.7 %all-to-all-start.3 = ((bf16[32,48,768]{2,1,0:T(8,128)(2,1)}), bf16[32,48,768]{2,1,0:T(8,128)(2,1)S(1)}, u32[]{:S(2)}, u32[]{:S(2)}) async-start(bf16[32,48,768]{2,1,0:T(8,128)(2,1)} %bitcast.100), calls=%async_computation.5 | async-start | bytes 4718592 | tf_op jit(solution)/shard_map/all_to_all | solution.py:1033
  473.9 11.3 %collective-permute-done.63 = bf16[136,1536]{1,0:T(8,128)(2,1)} collective-permute-done((bf16[136,1536]{1,0:T(8,128)(2,1)}, bf16[136,1536]{1,0:T(8,128)(2,1)}, u32[]{:S(2)}, u32[]{:S(2)}) %collective-permute-start.63) | collective-permute-done | bytes 417824 | tf_op jit(solution)/shard_map/ppermute | solution.py:77
  496.8 6.4 %all-to-all-done.3 = bf16[32,48,768]{2,1,0:T(8,128)(2,1)S(1)} async-done(((bf16[32,48,768]{2,1,0:T(8,128)(2,1)}), bf16[32,48,768]{2,1,0:T(8,128)(2,1)S(1)}, u32[]{:S(2)}, u32[]{:S(2)}) %all-to-all-start.3) | async-done | bytes 2359328 | tf_op jit(solution)/shard_map/all_to_all | solution.py:1033
  (602 shorter events, 199.3 us)
Async XLA Ops:
  14.3 23.7 %all-to-all-start = ((bf16[32,5,1536]{2,1,0:T(8,128)(2,1)}), bf16[32,5,1536]{2,1,0:T(8,128)(2,1)S(1)}, u32[]{:S(2)}, u32[]{:S(2)}) async-start(bf16[32,5,1536]{2,1,0:T(8,128)(2,1)} %pad_maximum_fusion), calls=%async_computation | async-start | bytes 1572864 | tf_op jit(solution)/shard_map/all_to_all | solution.py:703
  23.8 114.8 %all-gather.3.cloned.1.call-start = ((), (), s32[]{:S(2)}) async-start(), calls=%async_computation.6 | async-start | bytes 20275200 | tf_op jit(solution)/shard_map/all_gather | solution.py:705
  38.0 185.8 %all-gather.5.cloned.1.call-start = ((), (), s32[]{:S(2)}) async-start(), calls=%async_computation.7 | async-start | bytes 17031168 | tf_op jit(solution)/shard_map/all_gather | solution.py:706
  48.6 40.8 %all-to-all-start.1 = ((bf16[16,48,1536]{2,1,0:T(8,128)(2,1)}), bf16[16,48,1536]{2,1,0:T(8,128)(2,1)S(1)}, u32[]{:S(2)}, u32[]{:S(2)}) async-start(bf16[16,48,1536]{2,1,0:T(8,128)(2,1)} %broadcast_in_dim.85), calls=%async_computation.1 | async-start | bytes 4718592 | tf_op jit(solution)/shard_map/all_to_all | solution.py:555
  52.5 389.8 %reduce-scatter.5.cloned.1.call-start = ((), (), s32[]{:S(2)}) async-start(), calls=%async_computation.9 | async-start | bytes 8773632 | tf_op jit(solution)/shard_map/reduce_scatter | solution.py:549
  61.5 12.4 %collective-permute-start = (bf16[128,1536]{1,0:T(8,128)(2,1)}, bf16[128,1536]{1,0:T(8,128)(2,1)}, u32[]{:S(2)}, u32[]{:S(2)}) collective-permute-start(bf16[128,1536]{1,0:T(8,128)(2,1)} %get-tuple-element.331), channel_id=1, source_target_pairs={{0,1},{1,2},{2,3},{3,0},{4,5},{5,6},{6,7},{7,4},{8,9},{9,10},{10,1... | collective-permute-start | bytes 1179656 | tf_op jit(solution)/shard_map/ppermute | solution.py:77
  63.3 27.0 %collective-permute-start.1 = (bf16[128,1536]{1,0:T(8,128)(2,1)}, bf16[128,1536]{1,0:T(8,128)(2,1)}, u32[]{:S(2)}, u32[]{:S(2)}) collective-permute-start(bf16[128,1536]{1,0:T(8,128)(2,1)} %get-tuple-element.331), channel_id=1, source_target_pairs={{0,2},{1,3},{2,0},{3,1},{4,6},{5,7},{6,4},{7,5},{8,10},{9,11},{10,... | collective-permute-start | bytes 1179656 | tf_op jit(solution)/shard_map/ppermute | solution.py:77
  65.9 26.1 %collective-permute-start.2 = (bf16[128,1536]{1,0:T(8,128)(2,1)}, bf16[128,1536]{1,0:T(8,128)(2,1)}, u32[]{:S(2)}, u32[]{:S(2)}) collective-permute-start(bf16[128,1536]{1,0:T(8,128)(2,1)} %get-tuple-element.331), channel_id=1, source_target_pairs={{0,3},{1,0},{2,1},{3,2},{4,7},{5,4},{6,5},{7,6},{8,11},{9,8},{10,9... | collective-permute-start | bytes 1179656 | tf_op jit(solution)/shard_map/ppermute | solution.py:77
  89.4 10.3 %collective-permute-start.4 = (bf16[16,48,1536]{2,1,0:T(8,128)(2,1)S(1)}, bf16[16,48,1536]{2,1,0:T(8,128)(2,1)S(1)}, u32[]{:S(2)}, u32[]{:S(2)}) collective-permute-start(bf16[16,48,1536]{2,1,0:T(8,128)(2,1)S(1)} %all-to-all-done.1), channel_id=1, source_target_pairs={{0,4},{4,0},{1,5},{5,1},{2,6},{6,2},{3,7},{7,3},{8,12},{12,8},{9,1... | collective-permute-start | bytes 7077896 | tf_op jit(solution)/shard_map/ppermute | solution.py:72
  107.2 11.5 %collective-permute-start.5 = (bf16[64,1536]{1,0:T(8,128)(2,1)}, bf16[64,1536]{1,0:T(8,128)(2,1)S(1)}, u32[]{:S(2)}, u32[]{:S(2)}) collective-permute-start(bf16[64,1536]{1,0:T(8,128)(2,1)} %get-tuple-element.303), channel_id=1, source_target_pairs={{0,3},{1,0},{2,1},{3,2},{4,7},{5,4},{6,5},{7,6},{8,11},{9,8},{10,9... | collective-permute-start | bytes 589832 | tf_op jit(solution)/shard_map/ppermute | solution.py:77
  122.4 12.0 %collective-permute-start.8 = (bf16[64,1536]{1,0:T(8,128)(2,1)S(1)}, bf16[64,1536]{1,0:T(8,128)(2,1)S(1)}, u32[]{:S(2)}, u32[]{:S(2)}) collective-permute-start(bf16[64,1536]{1,0:T(8,128)(2,1)S(1)} %get-tuple-element.118.refs_0_), channel_id=1, source_target_pairs={{0,1},{1,2},{2,3},{3,0},{4,5},{5,6},{6,7},{7,4},{8,9},{9,10},{10,1... | collective-permute-start | bytes 589832 | tf_op jit(solution)/shard_map/ppermute | solution.py:77
  123.5 10.8 %collective-permute-start.9 = (bf16[64,1536]{1,0:T(8,128)(2,1)S(1)}, bf16[64,1536]{1,0:T(8,128)(2,1)S(1)}, u32[]{:S(2)}, u32[]{:S(2)}) collective-permute-start(bf16[64,1536]{1,0:T(8,128)(2,1)S(1)} %get-tuple-element.118.refs_0_), channel_id=1, source_target_pairs={{0,2},{1,3},{2,0},{3,1},{4,6},{5,7},{6,4},{7,5},{8,10},{9,11},{10,... | collective-permute-start | bytes 589832 | tf_op jit(solution)/shard_map/ppermute | solution.py:77
  149.7 10.7 %collective-permute-start.11 = (bf16[64,1536]{1,0:T(8,128)(2,1)S(1)}, bf16[64,1536]{1,0:T(8,128)(2,1)S(1)}, u32[]{:S(2)}, u32[]{:S(2)}) collective-permute-start(bf16[64,1536]{1,0:T(8,128)(2,1)S(1)} %get-tuple-element.121), channel_id=1, source_target_pairs={{0,3},{1,0},{2,1},{3,2},{4,7},{5,4},{6,5},{7,6},{8,11},{9,8},{10,9... | collective-permute-start | bytes 589832 | tf_op jit(solution)/shard_map/ppermute | solution.py:77
  152.7 12.3 %collective-permute-start.13 = (bf16[64,1536]{1,0:T(8,128)(2,1)S(1)}, bf16[64,1536]{1,0:T(8,128)(2,1)S(1)}, u32[]{:S(2)}, u32[]{:S(2)}) collective-permute-start(bf16[64,1536]{1,0:T(8,128)(2,1)S(1)} %get-tuple-element.123), channel_id=1, source_target_pairs={{0,1},{1,2},{2,3},{3,0},{4,5},{5,6},{6,7},{7,4},{8,9},{9,10},{10,1... | collective-permute-start | bytes 589832 | tf_op jit(solution)/shard_map/ppermute | solution.py:77
  165.3 11.8 %collective-permute-start.14 = (bf16[64,1536]{1,0:T(8,128)(2,1)S(1)}, bf16[64,1536]{1,0:T(8,128)(2,1)S(1)}, u32[]{:S(2)}, u32[]{:S(2)}) collective-permute-start(bf16[64,1536]{1,0:T(8,128)(2,1)S(1)} %get-tuple-element.125), channel_id=1, source_target_pairs={{0,1},{1,2},{2,3},{3,0},{4,5},{5,6},{6,7},{7,4},{8,9},{9,10},{10,1... | collective-permute-start | bytes 589832 | tf_op jit(solution)/shard_map/ppermute | solution.py:77
  165.4 11.8 %collective-permute-start.15 = (bf16[64,1536]{1,0:T(8,128)(2,1)S(1)}, bf16[64,1536]{1,0:T(8,128)(2,1)S(1)}, u32[]{:S(2)}, u32[]{:S(2)}) collective-permute-start(bf16[64,1536]{1,0:T(8,128)(2,1)S(1)} %get-tuple-element.125), channel_id=1, source_target_pairs={{0,2},{1,3},{2,0},{3,1},{4,6},{5,7},{6,4},{7,5},{8,10},{9,11},{10,... | collective-permute-start | bytes 589832 | tf_op jit(solution)/shard_map/ppermute | solution.py:77
  166.0 11.3 %collective-permute-start.16 = (bf16[64,1536]{1,0:T(8,128)(2,1)S(1)}, bf16[64,1536]{1,0:T(8,128)(2,1)S(1)}, u32[]{:S(2)}, u32[]{:S(2)}) collective-permute-start(bf16[64,1536]{1,0:T(8,128)(2,1)S(1)} %get-tuple-element.125), channel_id=1, source_target_pairs={{0,3},{1,0},{2,1},{3,2},{4,7},{5,4},{6,5},{7,6},{8,11},{9,8},{10,9... | collective-permute-start | bytes 589832 | tf_op jit(solution)/shard_map/ppermute | solution.py:77
  205.5 12.2 %collective-permute-start.21 = (bf16[64,1536]{1,0:T(8,128)(2,1)}, bf16[64,1536]{1,0:T(8,128)(2,1)}, u32[]{:S(2)}, u32[]{:S(2)}) collective-permute-start(bf16[64,1536]{1,0:T(8,128)(2,1)} %get-tuple-element.298), channel_id=1, source_target_pairs={{0,1},{1,2},{2,3},{3,0},{4,5},{5,6},{6,7},{7,4},{8,9},{9,10},{10,1... | collective-permute-start | bytes 589832 | tf_op jit(solution)/shard_map/ppermute | solution.py:77
  221.0 11.6 %collective-permute-start.22 = (bf16[64,1536]{1,0:T(8,128)(2,1)}, bf16[64,1536]{1,0:T(8,128)(2,1)}, u32[]{:S(2)}, u32[]{:S(2)}) collective-permute-start(bf16[64,1536]{1,0:T(8,128)(2,1)} %get-tuple-element.129.refs_0_), channel_id=1, source_target_pairs={{0,1},{1,2},{2,3},{3,0},{4,5},{5,6},{6,7},{7,4},{8,9},{9,10},{10,1... | collective-permute-start | bytes 589832 | tf_op jit(solution)/shard_map/ppermute | solution.py:77
  221.0 11.6 %collective-permute-start.23 = (bf16[64,1536]{1,0:T(8,128)(2,1)}, bf16[64,1536]{1,0:T(8,128)(2,1)}, u32[]{:S(2)}, u32[]{:S(2)}) collective-permute-start(bf16[64,1536]{1,0:T(8,128)(2,1)} %get-tuple-element.129.refs_0_), channel_id=1, source_target_pairs={{0,2},{1,3},{2,0},{3,1},{4,6},{5,7},{6,4},{7,5},{8,10},{9,11},{10,... | collective-permute-start | bytes 589832 | tf_op jit(solution)/shard_map/ppermute | solution.py:77
  222.2 10.6 %collective-permute-start.24 = (bf16[64,1536]{1,0:T(8,128)(2,1)}, bf16[64,1536]{1,0:T(8,128)(2,1)}, u32[]{:S(2)}, u32[]{:S(2)}) collective-permute-start(bf16[64,1536]{1,0:T(8,128)(2,1)} %get-tuple-element.129.refs_0_), channel_id=1, source_target_pairs={{0,3},{1,0},{2,1},{3,2},{4,7},{5,4},{6,5},{7,6},{8,11},{9,8},{10,9... | collective-permute-start | bytes 589832 | tf_op jit(solution)/shard_map/ppermute | solution.py:77
  248.7 21.3 %collective-permute-start.31 = (bf16[256,5760]{1,0:T(8,128)(2,1)}, bf16[256,5760]{1,0:T(8,128)(2,1)S(1)}, u32[]{:S(2)}, u32[]{:S(2)}) collective-permute-start(bf16[256,5760]{1,0:T(8,128)(2,1)} %get-tuple-element.136.refs_0_.refs_2_), channel_id=1, source_target_pairs={{0,4},{4,0},{1,5},{5,1},{2,6},{6,2},{3,7},{7,3},{8,12},{12,8},{9,1... | collective-permute-start | bytes 8847368 | tf_op jit(solution)/shard_map/ppermute | solution.py:72
  252.8 12.0 %collective-permute-start.27 = (bf16[64,1536]{1,0:T(8,128)(2,1)S(1)}, bf16[64,1536]{1,0:T(8,128)(2,1)S(1)}, u32[]{:S(2)}, u32[]{:S(2)}) collective-permute-start(bf16[64,1536]{1,0:T(8,128)(2,1)S(1)} %get-tuple-element.133), channel_id=1, source_target_pairs={{0,1},{1,2},{2,3},{3,0},{4,5},{5,6},{6,7},{7,4},{8,9},{9,10},{10,1... | collective-permute-start | bytes 589832 | tf_op jit(solution)/shard_map/ppermute | solution.py:77
  267.1 16.9 %collective-permute-start.28 = (bf16[64,1536]{1,0:T(8,128)(2,1)}, bf16[64,1536]{1,0:T(8,128)(2,1)}, u32[]{:S(2)}, u32[]{:S(2)}) collective-permute-start(bf16[64,1536]{1,0:T(8,128)(2,1)} %get-tuple-element.138.first_ref), channel_id=1, source_target_pairs={{0,1},{1,2},{2,3},{3,0},{4,5},{5,6},{6,7},{7,4},{8,9},{9,10},{10,1... | collective-permute-start | bytes 589832 | tf_op jit(solution)/shard_map/ppermute | solution.py:77
  267.1 16.9 %collective-permute-start.29 = (bf16[64,1536]{1,0:T(8,128)(2,1)}, bf16[64,1536]{1,0:T(8,128)(2,1)}, u32[]{:S(2)}, u32[]{:S(2)}) collective-permute-start(bf16[64,1536]{1,0:T(8,128)(2,1)} %get-tuple-element.138.first_ref), channel_id=1, source_target_pairs={{0,2},{1,3},{2,0},{3,1},{4,6},{5,7},{6,4},{7,5},{8,10},{9,11},{10,... | collective-permute-start | bytes 589832 | tf_op jit(solution)/shard_map/ppermute | solution.py:77
  268.7 15.3 %collective-permute-start.30 = (bf16[64,1536]{1,0:T(8,128)(2,1)}, bf16[64,1536]{1,0:T(8,128)(2,1)}, u32[]{:S(2)}, u32[]{:S(2)}) collective-permute-start(bf16[64,1536]{1,0:T(8,128)(2,1)} %get-tuple-element.138.first_ref), channel_id=1, source_target_pairs={{0,3},{1,0},{2,1},{3,2},{4,7},{5,4},{6,5},{7,6},{8,11},{9,8},{10,9... | collective-permute-start | bytes 589832 | tf_op jit(solution)/shard_map/ppermute | solution.py:77
  284.1 207.9 %reduce-scatter.3.cloned.1.call-start = ((), (), s32[]{:S(2)}) async-start(), calls=%async_computation.8 | async-start | bytes 10444800 | tf_op jit(solution)/shard_map/reduce_scatter | solution.py:549
  286.7 42.5 %collective-permute-start.40 = (bf16[256,1536]{1,0:T(8,128)(2,1)S(1)}, bf16[256,1536]{1,0:T(8,128)(2,1)S(1)}, u32[]{:S(2)}, u32[]{:S(2)}) collective-permute-start(bf16[256,1536]{1,0:T(8,128)(2,1)S(1)} %constant_dynamic-update-slice_fusion.2.refs_0_), channel_id=1, source_target_pairs={{0,4},{4,0},{1,5},{5,1},{2,6},{6,2},{3,7},{7,3},{8,12},{12,8},{9,1... | collective-permute-start | bytes 2359304 | tf_op jit(solution)/shard_map/ppermute | solution.py:72
  301.6 29.3 %collective-permute-start.41 = (bf16[256,1536]{1,0:T(8,128)(2,1)S(1)}, bf16[256,1536]{1,0:T(8,128)(2,1)S(1)}, u32[]{:S(2)}, u32[]{:S(2)}) collective-permute-start(bf16[256,1536]{1,0:T(8,128)(2,1)S(1)} %constant_dynamic-update-slice_fusion.6), channel_id=1, source_target_pairs={{0,4},{4,0},{1,5},{5,1},{2,6},{6,2},{3,7},{7,3},{8,12},{12,8},{9,1... | collective-permute-start | bytes 2359304 | tf_op jit(solution)/shard_map/ppermute | solution.py:72
  320.6 35.1 %collective-permute-start.43 = (bf16[256,1536]{1,0:T(8,128)(2,1)S(1)}, bf16[256,1536]{1,0:T(8,128)(2,1)S(1)}, u32[]{:S(2)}, u32[]{:S(2)}) collective-permute-start(bf16[256,1536]{1,0:T(8,128)(2,1)S(1)} %constant_dynamic-update-slice_fusion.10.refs_0_), channel_id=1, source_target_pairs={{0,4},{4,0},{1,5},{5,1},{2,6},{6,2},{3,7},{7,3},{8,12},{12,8},{9,1... | collective-permute-start | bytes 2359304 | tf_op jit(solution)/shard_map/ppermute | solution.py:72
  329.2 11.0 %collective-permute-start.38 = (bf16[64,1536]{1,0:T(8,128)(2,1)S(1)}, bf16[64,1536]{1,0:T(8,128)(2,1)S(1)}, u32[]{:S(2)}, u32[]{:S(2)}) collective-permute-start(bf16[64,1536]{1,0:T(8,128)(2,1)S(1)} %get-tuple-element.148.refs_4_), channel_id=1, source_target_pairs={{0,2},{1,3},{2,0},{3,1},{4,6},{5,7},{6,4},{7,5},{8,10},{9,11},{10,... | collective-permute-start | bytes 589832 | tf_op jit(solution)/shard_map/ppermute | solution.py:77
  359.4 12.3 %collective-permute-start.46 = (bf16[64,1536]{1,0:T(8,128)(2,1)}, bf16[64,1536]{1,0:T(8,128)(2,1)S(1)}, u32[]{:S(2)}, u32[]{:S(2)}) collective-permute-start(bf16[64,1536]{1,0:T(8,128)(2,1)} %get-tuple-element.162), channel_id=1, source_target_pairs={{0,3},{1,0},{2,1},{3,2},{4,7},{5,4},{6,5},{7,6},{8,11},{9,8},{10,9... | collective-permute-start | bytes 589832 | tf_op jit(solution)/shard_map/ppermute | solution.py:77
  361.8 9.9 %collective-permute-start.47 = (bf16[64,1536]{1,0:T(8,128)(2,1)S(1)}, bf16[64,1536]{1,0:T(8,128)(2,1)S(1)}, u32[]{:S(2)}, u32[]{:S(2)}) collective-permute-start(bf16[64,1536]{1,0:T(8,128)(2,1)S(1)} %get-tuple-element.163), channel_id=1, source_target_pairs={{0,2},{1,3},{2,0},{3,1},{4,6},{5,7},{6,4},{7,5},{8,10},{9,11},{10,... | collective-permute-start | bytes 589832 | tf_op jit(solution)/shard_map/ppermute | solution.py:77
  362.5 11.8 %collective-permute-start.48 = (bf16[64,1536]{1,0:T(8,128)(2,1)S(1)}, bf16[64,1536]{1,0:T(8,128)(2,1)S(1)}, u32[]{:S(2)}, u32[]{:S(2)}) collective-permute-start(bf16[64,1536]{1,0:T(8,128)(2,1)S(1)} %get-tuple-element.164), channel_id=1, source_target_pairs={{0,1},{1,2},{2,3},{3,0},{4,5},{5,6},{6,7},{7,4},{8,9},{9,10},{10,1... | collective-permute-start | bytes 589832 | tf_op jit(solution)/shard_map/ppermute | solution.py:77
  380.5 10.4 %collective-permute-start.51 = (bf16[64,1536]{1,0:T(8,128)(2,1)}, bf16[64,1536]{1,0:T(8,128)(2,1)}, u32[]{:S(2)}, u32[]{:S(2)}) collective-permute-start(bf16[64,1536]{1,0:T(8,128)(2,1)} %get-tuple-element.176), channel_id=1, source_target_pairs={{0,3},{1,0},{2,1},{3,2},{4,7},{5,4},{6,5},{7,6},{8,11},{9,8},{10,9... | collective-permute-start | bytes 589832 | tf_op jit(solution)/shard_map/ppermute | solution.py:77
  382.2 61.4 %collective-permute-start.59 = (bf16[256,1536]{1,0:T(8,128)(2,1)S(1)}, bf16[256,1536]{1,0:T(8,128)(2,1)S(1)}, u32[]{:S(2)}, u32[]{:S(2)}) collective-permute-start(bf16[256,1536]{1,0:T(8,128)(2,1)S(1)} %multiply_convert_fusion.refs_0_), channel_id=1, source_target_pairs={{0,4},{4,0},{1,5},{5,1},{2,6},{6,2},{3,7},{7,3},{8,12},{12,8},{9,1... | collective-permute-start | bytes 2359304 | tf_op jit(solution)/shard_map/ppermute | solution.py:72
  383.6 25.9 %collective-permute-start.53 = (bf16[64,1536]{1,0:T(8,128)(2,1)}, bf16[64,1536]{1,0:T(8,128)(2,1)}, u32[]{:S(2)}, u32[]{:S(2)}) collective-permute-start(bf16[64,1536]{1,0:T(8,128)(2,1)} %copy-done.55), channel_id=1, source_target_pairs={{0,3},{1,0},{2,1},{3,2},{4,7},{5,4},{6,5},{7,6},{8,11},{9,8},{10,9... | collective-permute-start | bytes 589832 | tf_op jit(solution)/shard_map/ppermute | solution.py:77
  388.1 21.5 %collective-permute-start.54 = (bf16[64,1536]{1,0:T(8,128)(2,1)S(1)}, bf16[64,1536]{1,0:T(8,128)(2,1)}, u32[]{:S(2)}, u32[]{:S(2)}) collective-permute-start(bf16[64,1536]{1,0:T(8,128)(2,1)S(1)} %copy-done.54), channel_id=1, source_target_pairs={{0,2},{1,3},{2,0},{3,1},{4,6},{5,7},{6,4},{7,5},{8,10},{9,11},{10,... | collective-permute-start | bytes 589832 | tf_op jit(solution)/shard_map/ppermute | solution.py:77
  388.7 20.9 %collective-permute-start.55 = (bf16[64,1536]{1,0:T(8,128)(2,1)S(1)}, bf16[64,1536]{1,0:T(8,128)(2,1)}, u32[]{:S(2)}, u32[]{:S(2)}) collective-permute-start(bf16[64,1536]{1,0:T(8,128)(2,1)S(1)} %copy-done.52), channel_id=1, source_target_pairs={{0,1},{1,2},{2,3},{3,0},{4,5},{5,6},{6,7},{7,4},{8,9},{9,10},{10,1... | collective-permute-start | bytes 589832 | tf_op jit(solution)/shard_map/ppermute | solution.py:77
  397.0 11.6 %collective-permute-start.52 = (f32[2,384]{1,0:T(2,128)}, f32[2,384]{1,0:T(2,128)}, u32[]{:S(2)}, u32[]{:S(2)}) collective-permute-start(f32[2,384]{1,0:T(2,128)} %pad_add_fusion.3), channel_id=1, source_target_pairs={{4,0},{8,4},{12,8},{5,1},{9,5},{13,9},{6,2},{10,6},{14,10},{7,3},{... | collective-permute-start | bytes 9224 | tf_op jit(solution)/shard_map/ppermute | solution.py:64
  408.6 35.1 %collective-permute-start.60 = (bf16[256,1536]{1,0:T(8,128)(2,1)}, bf16[256,1536]{1,0:T(8,128)(2,1)}, u32[]{:S(2)}, u32[]{:S(2)}) collective-permute-start(bf16[256,1536]{1,0:T(8,128)(2,1)} %copy-done.130), channel_id=1, source_target_pairs={{0,4},{4,0},{1,5},{5,1},{2,6},{6,2},{3,7},{7,3},{8,12},{12,8},{9,1... | collective-permute-start | bytes 2359304 | tf_op jit(solution)/shard_map/ppermute | solution.py:72
  420.0 10.5 %collective-permute-start.58 = (bf16[64,1536]{1,0:T(8,128)(2,1)S(1)}, bf16[64,1536]{1,0:T(8,128)(2,1)S(1)}, u32[]{:S(2)}, u32[]{:S(2)}) collective-permute-start(bf16[64,1536]{1,0:T(8,128)(2,1)S(1)} %get-tuple-element.292), channel_id=1, source_target_pairs={{0,1},{1,2},{2,3},{3,0},{4,5},{5,6},{6,7},{7,4},{8,9},{9,10},{10,1... | collective-permute-start | bytes 589832 | tf_op jit(solution)/shard_map/ppermute | solution.py:77
  424.0 20.9 %collective-permute-start.61 = (bf16[256,768]{1,0:T(8,128)(2,1)}, bf16[256,768]{1,0:T(8,128)(2,1)S(1)}, u32[]{:S(2)}, u32[]{:S(2)}) collective-permute-start(bf16[256,768]{1,0:T(8,128)(2,1)} %get-tuple-element.290), channel_id=1, source_target_pairs={{0,4},{4,0},{1,5},{5,1},{2,6},{6,2},{3,7},{7,3},{8,12},{12,8},{9,1... | collective-permute-start | bytes 1179656 | tf_op jit(solution)/shard_map/ppermute | solution.py:72
  435.7 25.8 %all-to-all-start.2 = ((bf16[32,8,1536]{2,1,0:T(8,128)(2,1)}), bf16[32,8,1536]{2,1,0:T(8,128)(2,1)}, u32[]{:S(2)}, u32[]{:S(2)}) async-start(bf16[32,8,1536]{2,1,0:T(8,128)(2,1)} %fusion.4), calls=%async_computation.3 | async-start | bytes 1572864 | tf_op jit(solution)/shard_map/all_to_all | solution.py:1008
  463.7 21.4 %collective-permute-start.63 = (bf16[136,1536]{1,0:T(8,128)(2,1)}, bf16[136,1536]{1,0:T(8,128)(2,1)}, u32[]{:S(2)}, u32[]{:S(2)}) collective-permute-start(bf16[136,1536]{1,0:T(8,128)(2,1)} %fusion.16), channel_id=1, source_target_pairs={{0,1},{1,2},{2,3},{3,0},{4,5},{5,6},{6,7},{7,4},{8,9},{9,10},{10,1... | collective-permute-start | bytes 1253384 | tf_op jit(solution)/shard_map/ppermute | solution.py:77
  464.0 21.1 %collective-permute-start.64 = (bf16[136,1536]{1,0:T(8,128)(2,1)}, bf16[136,1536]{1,0:T(8,128)(2,1)S(1)}, u32[]{:S(2)}, u32[]{:S(2)}) collective-permute-start(bf16[136,1536]{1,0:T(8,128)(2,1)} %fusion.16), channel_id=1, source_target_pairs={{0,2},{1,3},{2,0},{3,1},{4,6},{5,7},{6,4},{7,5},{8,10},{9,11},{10,... | collective-permute-start | bytes 1253384 | tf_op jit(solution)/shard_map/ppermute | solution.py:77
  464.3 21.8 %collective-permute-start.65 = (bf16[136,1536]{1,0:T(8,128)(2,1)}, bf16[136,1536]{1,0:T(8,128)(2,1)S(1)}, u32[]{:S(2)}, u32[]{:S(2)}) collective-permute-start(bf16[136,1536]{1,0:T(8,128)(2,1)} %fusion.16), channel_id=1, source_target_pairs={{0,3},{1,0},{2,1},{3,2},{4,7},{5,4},{6,5},{7,6},{8,11},{9,8},{10,9... | collective-permute-start | bytes 1253384 | tf_op jit(solution)/shard_map/ppermute | solution.py:77
  466.4 36.8 %all-to-all-start.3 = ((bf16[32,48,768]{2,1,0:T(8,128)(2,1)}), bf16[32,48,768]{2,1,0:T(8,128)(2,1)S(1)}, u32[]{:S(2)}, u32[]{:S(2)}) async-start(bf16[32,48,768]{2,1,0:T(8,128)(2,1)} %bitcast.100), calls=%async_computation.5 | async-start | bytes 4718592 | tf_op jit(solution)/shard_map/all_to_all | solution.py:1033
  (166 other events, 1576.7 us)
Sparse Core Ops, SparseCore 0:
  38.2 100.4 all-gather.2
  141.4 72.6 all-gather.4
  284.2 84.8 reduce-scatter.4
  374.5 92.6 reduce-scatter.2

commit v4 on v3

--- a/solution.py
+++ b/solution.py
@@ -861,6 +861,7 @@
         "assemble",
         20 * proj_b.size,
     )
+    d_proj_b, out_others = lax.optimization_barrier((d_proj_b, out_others))
     d_stream2, back_f, gain_b_grad = norm_backward(
         tp_scatter(tp_chunks(times_t(d_proj_b, project_b))), stream2, gain_b, d_stream3
     )
@@ -939,7 +940,6 @@
         ],
         axis=1,
     ).astype(BF16)
-    d_proj_a, out_others = lax.optimization_barrier((d_proj_a, out_others))
     stream4 = stream3 + add_parts([out_chunks[0], *out_others])
     d_chunks = tp_chunks(times_t(arrange(to_gathered, d_proj_a), project_a))
     keep, send = halves(d_proj_a, gated_rows)

time: 523 us -> 535 us (1.023)
  waiting for transfers between devices: 173 us -> 180 us
    unnamed x289 -> x317, local copies, waits for them, and re-layouts: 19.4 us -> 25.5 us
    ppermute x48, waiting for transfers between devices: 103 us -> 109 us  [shift_tp(): lax.ppermute(block, 'tp', [(i, (i + distance) % members) for i in range(m...]
  transfers between devices with their start and end apart: 75 -> 75, of which waited for: 39 -> 42; matrix products, arithmetic and copies ran while one was open for 20% -> 19% of each run, Pallas kernels for 15% -> 15%
where the time goes in v4:
time: 535 us; the launch traced here: 524 us
  waiting for transfers between devices  180 us (34%)
  starting transfers between devices  101 us (19%)
  Pallas kernels  93.1 us (17%)
  local copies, waits for them, and re-layouts  71 us (13%)
  other arithmetic  31.4 us (6%)
  matrix products  31 us (6%)
  between operations  17.1 us (3%)
    ppermute x48, waiting for transfers between devices, shift_tp(): lax.ppermute(block, 'tp', [(i, (i + distance) % members) for i in range(m...  109 us
    ppermute x48, starting transfers between devices, shift_tp(): lax.ppermute(block, 'tp', [(i, (i + distance) % members) for i in range(m...  50.8 us
    pallas_call x2, Pallas kernels, ffn_backward(): pl.pallas_call(functools.partial(ffn_backward_kernel, count, len(back_chu...  29.6 us
    pallas_call x4, Pallas kernels, gradient(): pl.pallas_call(functools.partial(gradient_kernel, edge, cut), grid=(steps...  26.2 us
    unnamed x317, local copies, waits for them, and re-layouts  25.5 us
    pallas_call x11, Pallas kernels, one_step(): pl.pallas_call(kernel, grid=(1,), in_specs=[whole(v.shape) for v in opera...  23.9 us
    ppermute x15, starting transfers between devices, swap_core(): return lax.ppermute(block, 'core', [(0, 1), (1, 0)])  18.1 us
    dot_general x9, matrix products, times(): lax.dot_general(left, right, (((1,), (0,)), ((), ())), preferred_element_...  17.2 us
  transfers between devices with their start and end apart: 75, of which 42 were waited for; matrix products, arithmetic and copies ran while one was open for 19% of the time, Pallas kernels for 15%

profile of v4, /device:TPU:1, one launch (start us, length us, event | category | flops | bytes accessed | tf_op | source)
XLA Modules:
  0.0 524.3 jit_solution(13536840875637438275)
XLA Ops:
  14.3 9.4 %all-to-all-start = ((bf16[32,5,1536]{2,1,0:T(8,128)(2,1)}), bf16[32,5,1536]{2,1,0:T(8,128)(2,1)S(1)}, u32[]{:S(2)}, u32[]{:S(2)}) async-start(bf16[32,5,1536]{2,1,0:T(8,128)(2,1)} %pad_maximum_fusion), calls=%async_computation | async-start | bytes 1572864 | tf_op jit(solution)/shard_map/all_to_all | solution.py:703
  25.9 12.1 %all-to-all-done = bf16[32,5,1536]{2,1,0:T(8,128)(2,1)S(1)} async-done(((bf16[32,5,1536]{2,1,0:T(8,128)(2,1)}), bf16[32,5,1536]{2,1,0:T(8,128)(2,1)S(1)}, u32[]{:S(2)}, u32[]{:S(2)}) %all-to-all-start) | async-done | bytes 491552 | tf_op jit(solution)/shard_map/all_to_all | solution.py:703
  48.7 3.9 all-to-all-start.1
  63.3 2.6 collective-permute-start.1
  70.0 3.9 collective-permute-done
  75.6 13.9 %all-to-all-done.1 = bf16[16,48,1536]{2,1,0:T(8,128)(2,1)S(1)} async-done(((bf16[16,48,1536]{2,1,0:T(8,128)(2,1)}), bf16[16,48,1536]{2,1,0:T(8,128)(2,1)S(1)}, u32[]{:S(2)}, u32[]{:S(2)}) %all-to-all-start.1) | async-done | bytes 2359328 | tf_op jit(solution)/shard_map/all_to_all | solution.py:555
  95.1 3.7 collective-permute-start.3
  104.1 3.0 fusion.151
  109.1 4.7 collective-permute-start.5
  116.5 4.0 collective-permute-done.5.refs_1_
  127.2 3.8 collective-permute-done.10.refs_3_
  131.0 5.3 %collective-permute-done.8.refs_1_ = bf16[64,1536]{1,0:T(8,128)(2,1)S(1)} collective-permute-done((bf16[64,1536]{1,0:T(8,128)(2,1)S(1)}, bf16[64,1536]{1,0:T(8,128)(2,1)S(1)}, u32[]{:S(2)}, u32[]{:S(2)}) %collective-permute-start.8) | collective-permute-done | bytes 196640 | tf_op jit(solution)/shard_map/ppermute | solution.py:77
  138.6 11.0 %ffn_forward.1 = (f32[64,1536]{1,0:T(8,128)S(1)}, bf16[64,1536]{1,0:T(8,128)(2,1)}, bf16[64,1536]{1,0:T(8,128)(2,1)S(1)}, bf16[64,1536]{1,0:T(8,128)(2,1)S(1)}) custom-call(bf16[64,1536]{1,0:T(8,128)(2,1)S(1)} %get-tuple-element.118.refs_0_, bf16[64,1536]{1,0:T(8,128)(2,1)S(1)} %collective-permute-done.8.refs_1_, ...), custom_call_target="tpu_custom_call" | custom-call | flops 4227858432 | bytes 16515072 | tf_op jit(solution)/shard_map/ffn_forward/pallas_call | solution.py:239
  153.4 7.2 %collective-permute-done.11.refs_1_ = bf16[64,1536]{1,0:T(8,128)(2,1)S(1)} collective-permute-done((bf16[64,1536]{1,0:T(8,128)(2,1)}, bf16[64,1536]{1,0:T(8,128)(2,1)S(1)}, u32[]{:S(2)}, u32[]{:S(2)}) %collective-permute-start.11) | collective-permute-done | bytes 196640 | tf_op jit(solution)/shard_map/ppermute | solution.py:77
  160.6 4.2 collective-permute-done.13.refs_3_
  168.5 9.2 %collective-permute-done.14 = bf16[64,1536]{1,0:T(8,128)(2,1)S(1)} collective-permute-done((bf16[64,1536]{1,0:T(8,128)(2,1)S(1)}, bf16[64,1536]{1,0:T(8,128)(2,1)S(1)}, u32[]{:S(2)}, u32[]{:S(2)}) %collective-permute-start.14) | collective-permute-done | bytes 196640 | tf_op jit(solution)/shard_map/ppermute | solution.py:77
  183.6 6.9 %collective-permute-done.17 = bf16[256,256]{1,0:T(8,128)(2,1)S(1)} collective-permute-done((bf16[256,256]{1,0:T(8,128)(2,1)S(1)}, bf16[256,256]{1,0:T(8,128)(2,1)S(1)}, u32[]{:S(2)}, u32[]{:S(2)}) %collective-permute-start.17) | collective-permute-done | bytes 131104 | tf_op jit(solution)/shard_map/ppermute | solution.py:68
  194.4 5.3 %attend.1 = bf16[256,384]{1,0:T(8,128)(2,1)S(1)} custom-call(bf16[256,384]{1,0:T(8,128)(2,1)S(1)} %get-tuple-element.126.q_ref, bf16[1024,256]{1,0:T(8,128)(2,1)S(1)} %pad_maximum_fusion.2.kv_ref, bf16[1024,256]{1,0:T(8,128)(2,1)S(1)} %select_convert_fusion.barred_ref), custom_call_target="tpu_custom_call" | custom-call | flops 402653184 | bytes 1441792 | tf_op jit(solution)/shard_map/attend/pallas_call | solution.py:137
  199.7 3.1 fusion.152
  211.0 2.6 collective-permute-done.20.refs_2_
  213.6 4.7 collective-permute-done.21.refs_3_
  224.4 9.0 %collective-permute-done.22.refs_1_ = bf16[64,1536]{1,0:T(8,128)(2,1)} collective-permute-done((bf16[64,1536]{1,0:T(8,128)(2,1)}, bf16[64,1536]{1,0:T(8,128)(2,1)}, u32[]{:S(2)}, u32[]{:S(2)}) %collective-permute-start.22) | collective-permute-done | bytes 196640 | tf_op jit(solution)/shard_map/ppermute | solution.py:77
  233.4 15.2 %ffn_both.1 = (f32[64,1536]{1,0:T(8,128)S(1)}, bf16[64,1536]{1,0:T(8,128)(2,1)S(1)}, bf16[64,1536]{1,0:T(8,128)(2,1)S(1)}, bf16[64,1536]{1,0:T(8,128)(2,1)S(1)},...) custom-call(s32[1]{0:T(128)} %bitcast.core_ref, ...), custom_call_target="tpu_custom_call" | custom-call | flops 8455716864 | bytes 22413312 | tf_op jit(solution)/shard_map/ffn_both/pallas_call | solution.py:330
  253.8 4.0 collective-permute-done.25.refs_1_
  257.9 3.1 collective-permute-done.26.refs_2_
  261.0 4.3 collective-permute-done.27.refs_3_
  274.3 10.4 %weight_gradient.4 = bf16[1536,2688]{1,0:T(8,128)(2,1)} custom-call(bf16[256,5760]{1,0:T(8,128)(2,1)S(1)} %copy-done, bf16[256,5760]{1,0:T(8,128)(2,1)} %copy-done.68, bf16[256,5760]{1,0:T(8,128)(2,1)S(1)} %copy-done, bf16[256,5760]{1,0:T(8,128)(2,1)} %copy-done.68, bf16[256,2688]{1,0:T(8,128)(2,1)S(1)} %get-tuple-element.137.refs_4_, ...), custom_call_target="tpu_custom_call" | custom-call | flops 4227858432 | bytes 8257536 | tf_op jit(solution)/shard_map/weight_gradient/pallas_call | solution.py:399
  292.4 9.4 %attend_backward.1 = (bf16[256,384]{1,0:T(8,128)(2,1)S(1)}, f32[512,256]{1,0:T(8,128)S(1)}, bf16[512,256]{1,0:T(8,128)(2,1)S(1)}, f32[1,64]{1,0:T(1,128)S(1)}) custom-call(bf16[64,1536]{1,0:T(8,128)(2,1)} %get-tuple-element.138.first_ref, bf16[64,1536]{1,0:T(8,128)(2,1)} %collective-permute-done.28.second_ref, ...), custom_call_target="tpu_custom_call" | custom-call | flops 1006632960 | bytes 4915712 | tf_op jit(solution)/shard_map/attend_backward/pallas_call | solution.py:137
  307.1 7.7 %collective-permute-done.33.far_ref = bf16[256,256]{1,0:T(8,128)(2,1)S(1)} collective-permute-done((bf16[256,256]{1,0:T(8,128)(2,1)S(1)}, bf16[256,256]{1,0:T(8,128)(2,1)S(1)}, u32[]{:S(2)}, u32[]{:S(2)}) %collective-permute-start.33) | collective-permute-done | bytes 131104 | tf_op jit(solution)/shard_map/ppermute | solution.py:68
  316.7 2.7 fusion.153
  321.9 4.5 collective-permute-done.37.refs_1_
  326.4 4.1 collective-permute-start.46
  337.1 3.7 weight_gradient.5.refs_6_
  341.3 3.9 collective-permute-done.41.refs_6_
  345.8 14.5 %ffn_backward.1 = (f32[64,1536]{1,0:T(8,128)S(1)}, bf16[64,1536]{1,0:T(8,128)(2,1)}, bf16[64,1536]{1,0:T(8,128)(2,1)}, bf16[64,1536]{1,0:T(8,128)(2,1)}, bf16[25...) custom-call(s32[1]{0:T(128)} %bitcast.core_ref, bf16[64,1536]{1,0:T(8,128)(2,1)S(1)} %copy-done.8, ...), custom_call_target="tpu_custom_call" | custom-call | flops 7046430720 | bytes 19267584 | tf_op jit(solution)/shard_map/ffn_backward/pallas_call | solution.py:330
  362.9 3.7 collective-permute-done.47.refs_3_
  369.0 8.8 %weight_gradient.6 = bf16[1536,3200]{1,0:T(8,128)(2,1)} custom-call(bf16[256,1536]{1,0:T(8,128)(2,1)S(1)} %constant_dynamic-update-slice_fusion.10.refs_0_, bf16[256,1536]{1,0:T(8,128)(2,1)S(1)} %collective-permute-done.46.refs_1_, bf16[256,1536]{1,0:T(8,128)(2,1)S(1)} %constant_dynamic-update-slice_fusion.14.refs_2_, ...), custom_call_target="tpu_custom_call", output_to_operand_aliasing={{}: (6, {})} | custom-call | flops 4227858432 | bytes 8257536 | tf_op jit(solution)/shard_map/weight_gradient/pallas_call | solution.py:399
  402.5 4.1 collective-permute-done.53
  411.5 3.0 multiply_reduce_fusion.3
  422.1 4.9 fusion.154
  434.3 3.4 collective-permute-done.56.refs_1_
  438.4 3.2 collective-permute-done.58.refs_3_
  446.8 5.2 all-to-all-start.2
  454.8 3.3 weight_gradient.7
  459.3 12.5 %all-to-all-done.2 = bf16[32,8,1536]{2,1,0:T(8,128)(2,1)} async-done(((bf16[32,8,1536]{2,1,0:T(8,128)(2,1)}), bf16[32,8,1536]{2,1,0:T(8,128)(2,1)}, u32[]{:S(2)}, u32[]{:S(2)}) %all-to-all-start.2) | async-done | bytes 786464 | tf_op jit(solution)/shard_map/all_to_all | solution.py:1008
  476.8 6.4 %all-to-all-start.3 = ((bf16[32,48,768]{2,1,0:T(8,128)(2,1)}), bf16[32,48,768]{2,1,0:T(8,128)(2,1)S(1)}, u32[]{:S(2)}, u32[]{:S(2)}) async-start(bf16[32,48,768]{2,1,0:T(8,128)(2,1)} %bitcast.99), calls=%async_computation.5 | async-start | bytes 4718592 | tf_op jit(solution)/shard_map/all_to_all | solution.py:1033
  484.9 10.8 %collective-permute-done.63 = bf16[136,1536]{1,0:T(8,128)(2,1)} collective-permute-done((bf16[136,1536]{1,0:T(8,128)(2,1)}, bf16[136,1536]{1,0:T(8,128)(2,1)}, u32[]{:S(2)}, u32[]{:S(2)}) %collective-permute-start.63) | collective-permute-done | bytes 417824 | tf_op jit(solution)/shard_map/ppermute | solution.py:77
  507.4 6.9 %all-to-all-done.3 = bf16[32,48,768]{2,1,0:T(8,128)(2,1)S(1)} async-done(((bf16[32,48,768]{2,1,0:T(8,128)(2,1)}), bf16[32,48,768]{2,1,0:T(8,128)(2,1)S(1)}, u32[]{:S(2)}, u32[]{:S(2)}) %all-to-all-start.3) | async-done | bytes 2359328 | tf_op jit(solution)/shard_map/all_to_all | solution.py:1033
  (627 shorter events, 210.1 us)
Async XLA Ops:
  14.3 23.7 %all-to-all-start = ((bf16[32,5,1536]{2,1,0:T(8,128)(2,1)}), bf16[32,5,1536]{2,1,0:T(8,128)(2,1)S(1)}, u32[]{:S(2)}, u32[]{:S(2)}) async-start(bf16[32,5,1536]{2,1,0:T(8,128)(2,1)} %pad_maximum_fusion), calls=%async_computation | async-start | bytes 1572864 | tf_op jit(solution)/shard_map/all_to_all | solution.py:703
  23.8 114.8 %all-gather.3.cloned.1.call-start = ((), (), s32[]{:S(2)}) async-start(), calls=%async_computation.6 | async-start | bytes 20275200 | tf_op jit(solution)/shard_map/all_gather | solution.py:705
  38.0 186.4 %all-gather.5.cloned.1.call-start = ((), (), s32[]{:S(2)}) async-start(), calls=%async_computation.7 | async-start | bytes 17031168 | tf_op jit(solution)/shard_map/all_gather | solution.py:706
  48.7 40.8 %all-to-all-start.1 = ((bf16[16,48,1536]{2,1,0:T(8,128)(2,1)}), bf16[16,48,1536]{2,1,0:T(8,128)(2,1)S(1)}, u32[]{:S(2)}, u32[]{:S(2)}) async-start(bf16[16,48,1536]{2,1,0:T(8,128)(2,1)} %broadcast_in_dim.85), calls=%async_computation.1 | async-start | bytes 4718592 | tf_op jit(solution)/shard_map/all_to_all | solution.py:555
  52.5 399.5 %reduce-scatter.5.cloned.1.call-start = ((), (), s32[]{:S(2)}) async-start(), calls=%async_computation.9 | async-start | bytes 8773632 | tf_op jit(solution)/shard_map/reduce_scatter | solution.py:549
  61.5 12.4 %collective-permute-start = (bf16[128,1536]{1,0:T(8,128)(2,1)}, bf16[128,1536]{1,0:T(8,128)(2,1)}, u32[]{:S(2)}, u32[]{:S(2)}) collective-permute-start(bf16[128,1536]{1,0:T(8,128)(2,1)} %get-tuple-element.331), channel_id=1, source_target_pairs={{0,1},{1,2},{2,3},{3,0},{4,5},{5,6},{6,7},{7,4},{8,9},{9,10},{10,1... | collective-permute-start | bytes 1179656 | tf_op jit(solution)/shard_map/ppermute | solution.py:77
  63.3 27.0 %collective-permute-start.1 = (bf16[128,1536]{1,0:T(8,128)(2,1)}, bf16[128,1536]{1,0:T(8,128)(2,1)}, u32[]{:S(2)}, u32[]{:S(2)}) collective-permute-start(bf16[128,1536]{1,0:T(8,128)(2,1)} %get-tuple-element.331), channel_id=1, source_target_pairs={{0,2},{1,3},{2,0},{3,1},{4,6},{5,7},{6,4},{7,5},{8,10},{9,11},{10,... | collective-permute-start | bytes 1179656 | tf_op jit(solution)/shard_map/ppermute | solution.py:77
  66.0 26.1 %collective-permute-start.2 = (bf16[128,1536]{1,0:T(8,128)(2,1)}, bf16[128,1536]{1,0:T(8,128)(2,1)}, u32[]{:S(2)}, u32[]{:S(2)}) collective-permute-start(bf16[128,1536]{1,0:T(8,128)(2,1)} %get-tuple-element.331), channel_id=1, source_target_pairs={{0,3},{1,0},{2,1},{3,2},{4,7},{5,4},{6,5},{7,6},{8,11},{9,8},{10,9... | collective-permute-start | bytes 1179656 | tf_op jit(solution)/shard_map/ppermute | solution.py:77
  89.5 10.2 %collective-permute-start.4 = (bf16[16,48,1536]{2,1,0:T(8,128)(2,1)S(1)}, bf16[16,48,1536]{2,1,0:T(8,128)(2,1)S(1)}, u32[]{:S(2)}, u32[]{:S(2)}) collective-permute-start(bf16[16,48,1536]{2,1,0:T(8,128)(2,1)S(1)} %all-to-all-done.1), channel_id=1, source_target_pairs={{0,4},{4,0},{1,5},{5,1},{2,6},{6,2},{3,7},{7,3},{8,12},{12,8},{9,1... | collective-permute-start | bytes 7077896 | tf_op jit(solution)/shard_map/ppermute | solution.py:72
  109.1 11.5 %collective-permute-start.5 = (bf16[64,1536]{1,0:T(8,128)(2,1)}, bf16[64,1536]{1,0:T(8,128)(2,1)S(1)}, u32[]{:S(2)}, u32[]{:S(2)}) collective-permute-start(bf16[64,1536]{1,0:T(8,128)(2,1)} %get-tuple-element.303), channel_id=1, source_target_pairs={{0,3},{1,0},{2,1},{3,2},{4,7},{5,4},{6,5},{7,6},{8,11},{9,8},{10,9... | collective-permute-start | bytes 589832 | tf_op jit(solution)/shard_map/ppermute | solution.py:77
  124.3 12.0 %collective-permute-start.8 = (bf16[64,1536]{1,0:T(8,128)(2,1)S(1)}, bf16[64,1536]{1,0:T(8,128)(2,1)S(1)}, u32[]{:S(2)}, u32[]{:S(2)}) collective-permute-start(bf16[64,1536]{1,0:T(8,128)(2,1)S(1)} %get-tuple-element.118.refs_0_), channel_id=1, source_target_pairs={{0,1},{1,2},{2,3},{3,0},{4,5},{5,6},{6,7},{7,4},{8,9},{9,10},{10,1... | collective-permute-start | bytes 589832 | tf_op jit(solution)/shard_map/ppermute | solution.py:77
  125.4 10.8 %collective-permute-start.9 = (bf16[64,1536]{1,0:T(8,128)(2,1)S(1)}, bf16[64,1536]{1,0:T(8,128)(2,1)S(1)}, u32[]{:S(2)}, u32[]{:S(2)}) collective-permute-start(bf16[64,1536]{1,0:T(8,128)(2,1)S(1)} %get-tuple-element.118.refs_0_), channel_id=1, source_target_pairs={{0,2},{1,3},{2,0},{3,1},{4,6},{5,7},{6,4},{7,5},{8,10},{9,11},{10,... | collective-permute-start | bytes 589832 | tf_op jit(solution)/shard_map/ppermute | solution.py:77
  149.6 11.0 %collective-permute-start.11 = (bf16[64,1536]{1,0:T(8,128)(2,1)}, bf16[64,1536]{1,0:T(8,128)(2,1)S(1)}, u32[]{:S(2)}, u32[]{:S(2)}) collective-permute-start(bf16[64,1536]{1,0:T(8,128)(2,1)} %get-tuple-element.121), channel_id=1, source_target_pairs={{0,3},{1,0},{2,1},{3,2},{4,7},{5,4},{6,5},{7,6},{8,11},{9,8},{10,9... | collective-permute-start | bytes 589832 | tf_op jit(solution)/shard_map/ppermute | solution.py:77
  152.7 12.1 %collective-permute-start.13 = (bf16[64,1536]{1,0:T(8,128)(2,1)S(1)}, bf16[64,1536]{1,0:T(8,128)(2,1)S(1)}, u32[]{:S(2)}, u32[]{:S(2)}) collective-permute-start(bf16[64,1536]{1,0:T(8,128)(2,1)S(1)} %get-tuple-element.123), channel_id=1, source_target_pairs={{0,1},{1,2},{2,3},{3,0},{4,5},{5,6},{6,7},{7,4},{8,9},{9,10},{10,1... | collective-permute-start | bytes 589832 | tf_op jit(solution)/shard_map/ppermute | solution.py:77
  165.8 11.9 %collective-permute-start.14 = (bf16[64,1536]{1,0:T(8,128)(2,1)S(1)}, bf16[64,1536]{1,0:T(8,128)(2,1)S(1)}, u32[]{:S(2)}, u32[]{:S(2)}) collective-permute-start(bf16[64,1536]{1,0:T(8,128)(2,1)S(1)} %get-tuple-element.125), channel_id=1, source_target_pairs={{0,1},{1,2},{2,3},{3,0},{4,5},{5,6},{6,7},{7,4},{8,9},{9,10},{10,1... | collective-permute-start | bytes 589832 | tf_op jit(solution)/shard_map/ppermute | solution.py:77
  165.8 11.9 %collective-permute-start.15 = (bf16[64,1536]{1,0:T(8,128)(2,1)S(1)}, bf16[64,1536]{1,0:T(8,128)(2,1)S(1)}, u32[]{:S(2)}, u32[]{:S(2)}) collective-permute-start(bf16[64,1536]{1,0:T(8,128)(2,1)S(1)} %get-tuple-element.125), channel_id=1, source_target_pairs={{0,2},{1,3},{2,0},{3,1},{4,6},{5,7},{6,4},{7,5},{8,10},{9,11},{10,... | collective-permute-start | bytes 589832 | tf_op jit(solution)/shard_map/ppermute | solution.py:77
  166.4 11.3 %collective-permute-start.16 = (bf16[64,1536]{1,0:T(8,128)(2,1)S(1)}, bf16[64,1536]{1,0:T(8,128)(2,1)S(1)}, u32[]{:S(2)}, u32[]{:S(2)}) collective-permute-start(bf16[64,1536]{1,0:T(8,128)(2,1)S(1)} %get-tuple-element.125), channel_id=1, source_target_pairs={{0,3},{1,0},{2,1},{3,2},{4,7},{5,4},{6,5},{7,6},{8,11},{9,8},{10,9... | collective-permute-start | bytes 589832 | tf_op jit(solution)/shard_map/ppermute | solution.py:77
  206.1 12.2 %collective-permute-start.21 = (bf16[64,1536]{1,0:T(8,128)(2,1)}, bf16[64,1536]{1,0:T(8,128)(2,1)}, u32[]{:S(2)}, u32[]{:S(2)}) collective-permute-start(bf16[64,1536]{1,0:T(8,128)(2,1)} %get-tuple-element.298), channel_id=1, source_target_pairs={{0,1},{1,2},{2,3},{3,0},{4,5},{5,6},{6,7},{7,4},{8,9},{9,10},{10,1... | collective-permute-start | bytes 589832 | tf_op jit(solution)/shard_map/ppermute | solution.py:77
  221.6 11.7 %collective-permute-start.22 = (bf16[64,1536]{1,0:T(8,128)(2,1)}, bf16[64,1536]{1,0:T(8,128)(2,1)}, u32[]{:S(2)}, u32[]{:S(2)}) collective-permute-start(bf16[64,1536]{1,0:T(8,128)(2,1)} %get-tuple-element.129.refs_0_), channel_id=1, source_target_pairs={{0,1},{1,2},{2,3},{3,0},{4,5},{5,6},{6,7},{7,4},{8,9},{9,10},{10,1... | collective-permute-start | bytes 589832 | tf_op jit(solution)/shard_map/ppermute | solution.py:77
  221.6 11.7 %collective-permute-start.23 = (bf16[64,1536]{1,0:T(8,128)(2,1)}, bf16[64,1536]{1,0:T(8,128)(2,1)}, u32[]{:S(2)}, u32[]{:S(2)}) collective-permute-start(bf16[64,1536]{1,0:T(8,128)(2,1)} %get-tuple-element.129.refs_0_), channel_id=1, source_target_pairs={{0,2},{1,3},{2,0},{3,1},{4,6},{5,7},{6,4},{7,5},{8,10},{9,11},{10,... | collective-permute-start | bytes 589832 | tf_op jit(solution)/shard_map/ppermute | solution.py:77
  222.7 10.7 %collective-permute-start.24 = (bf16[64,1536]{1,0:T(8,128)(2,1)}, bf16[64,1536]{1,0:T(8,128)(2,1)}, u32[]{:S(2)}, u32[]{:S(2)}) collective-permute-start(bf16[64,1536]{1,0:T(8,128)(2,1)} %get-tuple-element.129.refs_0_), channel_id=1, source_target_pairs={{0,3},{1,0},{2,1},{3,2},{4,7},{5,4},{6,5},{7,6},{8,11},{9,8},{10,9... | collective-permute-start | bytes 589832 | tf_op jit(solution)/shard_map/ppermute | solution.py:77
  249.3 21.5 %collective-permute-start.31 = (bf16[256,5760]{1,0:T(8,128)(2,1)}, bf16[256,5760]{1,0:T(8,128)(2,1)S(1)}, u32[]{:S(2)}, u32[]{:S(2)}) collective-permute-start(bf16[256,5760]{1,0:T(8,128)(2,1)} %get-tuple-element.136.refs_0_.refs_2_), channel_id=1, source_target_pairs={{0,4},{4,0},{1,5},{5,1},{2,6},{6,2},{3,7},{7,3},{8,12},{12,8},{9,1... | collective-permute-start | bytes 8847368 | tf_op jit(solution)/shard_map/ppermute | solution.py:72
  253.3 12.0 %collective-permute-start.27 = (bf16[64,1536]{1,0:T(8,128)(2,1)S(1)}, bf16[64,1536]{1,0:T(8,128)(2,1)S(1)}, u32[]{:S(2)}, u32[]{:S(2)}) collective-permute-start(bf16[64,1536]{1,0:T(8,128)(2,1)S(1)} %get-tuple-element.133), channel_id=1, source_target_pairs={{0,1},{1,2},{2,3},{3,0},{4,5},{5,6},{6,7},{7,4},{8,9},{9,10},{10,1... | collective-permute-start | bytes 589832 | tf_op jit(solution)/shard_map/ppermute | solution.py:77
  267.7 17.0 %collective-permute-start.28 = (bf16[64,1536]{1,0:T(8,128)(2,1)}, bf16[64,1536]{1,0:T(8,128)(2,1)}, u32[]{:S(2)}, u32[]{:S(2)}) collective-permute-start(bf16[64,1536]{1,0:T(8,128)(2,1)} %get-tuple-element.138.first_ref), channel_id=1, source_target_pairs={{0,1},{1,2},{2,3},{3,0},{4,5},{5,6},{6,7},{7,4},{8,9},{9,10},{10,1... | collective-permute-start | bytes 589832 | tf_op jit(solution)/shard_map/ppermute | solution.py:77
  267.7 17.0 %collective-permute-start.29 = (bf16[64,1536]{1,0:T(8,128)(2,1)}, bf16[64,1536]{1,0:T(8,128)(2,1)}, u32[]{:S(2)}, u32[]{:S(2)}) collective-permute-start(bf16[64,1536]{1,0:T(8,128)(2,1)} %get-tuple-element.138.first_ref), channel_id=1, source_target_pairs={{0,2},{1,3},{2,0},{3,1},{4,6},{5,7},{6,4},{7,5},{8,10},{9,11},{10,... | collective-permute-start | bytes 589832 | tf_op jit(solution)/shard_map/ppermute | solution.py:77
  269.4 15.3 %collective-permute-start.30 = (bf16[64,1536]{1,0:T(8,128)(2,1)}, bf16[64,1536]{1,0:T(8,128)(2,1)}, u32[]{:S(2)}, u32[]{:S(2)}) collective-permute-start(bf16[64,1536]{1,0:T(8,128)(2,1)} %get-tuple-element.138.first_ref), channel_id=1, source_target_pairs={{0,3},{1,0},{2,1},{3,2},{4,7},{5,4},{6,5},{7,6},{8,11},{9,8},{10,9... | collective-permute-start | bytes 589832 | tf_op jit(solution)/shard_map/ppermute | solution.py:77
  284.7 217.8 %reduce-scatter.3.cloned.1.call-start = ((), (), s32[]{:S(2)}) async-start(), calls=%async_computation.8 | async-start | bytes 10444800 | tf_op jit(solution)/shard_map/reduce_scatter | solution.py:549
  287.4 46.8 %collective-permute-start.43 = (bf16[256,1536]{1,0:T(8,128)(2,1)S(1)}, bf16[256,1536]{1,0:T(8,128)(2,1)S(1)}, u32[]{:S(2)}, u32[]{:S(2)}) collective-permute-start(bf16[256,1536]{1,0:T(8,128)(2,1)S(1)} %constant_dynamic-update-slice_fusion.2.refs_0_), channel_id=1, source_target_pairs={{0,4},{4,0},{1,5},{5,1},{2,6},{6,2},{3,7},{7,3},{8,12},{12,8},{9,1... | collective-permute-start | bytes 2359304 | tf_op jit(solution)/shard_map/ppermute | solution.py:72
  288.8 27.8 %collective-permute-start.34 = (bf16[64,1536]{1,0:T(8,128)(2,1)S(1)}, bf16[64,1536]{1,0:T(8,128)(2,1)S(1)}, u32[]{:S(2)}, u32[]{:S(2)}) collective-permute-start(bf16[64,1536]{1,0:T(8,128)(2,1)S(1)} %copy-done.66), channel_id=1, source_target_pairs={{0,3},{1,0},{2,1},{3,2},{4,7},{5,4},{6,5},{7,6},{8,11},{9,8},{10,9... | collective-permute-start | bytes 589832 | tf_op jit(solution)/shard_map/ppermute | solution.py:77
  289.3 27.3 %collective-permute-start.35 = (bf16[64,1536]{1,0:T(8,128)(2,1)S(1)}, bf16[64,1536]{1,0:T(8,128)(2,1)S(1)}, u32[]{:S(2)}, u32[]{:S(2)}) collective-permute-start(bf16[64,1536]{1,0:T(8,128)(2,1)S(1)} %copy-done.64), channel_id=1, source_target_pairs={{0,2},{1,3},{2,0},{3,1},{4,6},{5,7},{6,4},{7,5},{8,10},{9,11},{10,... | collective-permute-start | bytes 589832 | tf_op jit(solution)/shard_map/ppermute | solution.py:77
  291.5 25.2 %collective-permute-start.36 = (bf16[64,1536]{1,0:T(8,128)(2,1)S(1)}, bf16[64,1536]{1,0:T(8,128)(2,1)S(1)}, u32[]{:S(2)}, u32[]{:S(2)}) collective-permute-start(bf16[64,1536]{1,0:T(8,128)(2,1)S(1)} %copy-done.62), channel_id=1, source_target_pairs={{0,1},{1,2},{2,3},{3,0},{4,5},{5,6},{6,7},{7,4},{8,9},{9,10},{10,1... | collective-permute-start | bytes 589832 | tf_op jit(solution)/shard_map/ppermute | solution.py:77
  314.8 21.6 %collective-permute-start.44 = (bf16[256,1536]{1,0:T(8,128)(2,1)S(1)}, bf16[256,1536]{1,0:T(8,128)(2,1)S(1)}, u32[]{:S(2)}, u32[]{:S(2)}) collective-permute-start(bf16[256,1536]{1,0:T(8,128)(2,1)S(1)} %constant_dynamic-update-slice_fusion.6), channel_id=1, source_target_pairs={{0,4},{4,0},{1,5},{5,1},{2,6},{6,2},{3,7},{7,3},{8,12},{12,8},{9,1... | collective-permute-start | bytes 2359304 | tf_op jit(solution)/shard_map/ppermute | solution.py:72
  321.1 12.0 %collective-permute-start.39 = (bf16[64,1536]{1,0:T(8,128)(2,1)S(1)}, bf16[64,1536]{1,0:T(8,128)(2,1)S(1)}, u32[]{:S(2)}, u32[]{:S(2)}) collective-permute-start(bf16[64,1536]{1,0:T(8,128)(2,1)S(1)} %get-tuple-element.295), channel_id=1, source_target_pairs={{0,1},{1,2},{2,3},{3,0},{4,5},{5,6},{6,7},{7,4},{8,9},{9,10},{10,1... | collective-permute-start | bytes 589832 | tf_op jit(solution)/shard_map/ppermute | solution.py:77
  326.4 36.5 %collective-permute-start.46 = (bf16[256,1536]{1,0:T(8,128)(2,1)S(1)}, bf16[256,1536]{1,0:T(8,128)(2,1)S(1)}, u32[]{:S(2)}, u32[]{:S(2)}) collective-permute-start(bf16[256,1536]{1,0:T(8,128)(2,1)S(1)} %constant_dynamic-update-slice_fusion.10.refs_0_), channel_id=1, source_target_pairs={{0,4},{4,0},{1,5},{5,1},{2,6},{6,2},{3,7},{7,3},{8,12},{12,8},{9,1... | collective-permute-start | bytes 2359304 | tf_op jit(solution)/shard_map/ppermute | solution.py:72
  334.2 10.9 %collective-permute-start.41 = (bf16[64,1536]{1,0:T(8,128)(2,1)S(1)}, bf16[64,1536]{1,0:T(8,128)(2,1)S(1)}, u32[]{:S(2)}, u32[]{:S(2)}) collective-permute-start(bf16[64,1536]{1,0:T(8,128)(2,1)S(1)} %get-tuple-element.152.refs_4_), channel_id=1, source_target_pairs={{0,2},{1,3},{2,0},{3,1},{4,6},{5,7},{6,4},{7,5},{8,10},{9,11},{10,... | collective-permute-start | bytes 589832 | tf_op jit(solution)/shard_map/ppermute | solution.py:77
  366.6 11.3 %collective-permute-start.49 = (bf16[64,1536]{1,0:T(8,128)(2,1)}, bf16[64,1536]{1,0:T(8,128)(2,1)S(1)}, u32[]{:S(2)}, u32[]{:S(2)}) collective-permute-start(bf16[64,1536]{1,0:T(8,128)(2,1)} %get-tuple-element.166), channel_id=1, source_target_pairs={{0,3},{1,0},{2,1},{3,2},{4,7},{5,4},{6,5},{7,6},{8,11},{9,8},{10,9... | collective-permute-start | bytes 589832 | tf_op jit(solution)/shard_map/ppermute | solution.py:77
  368.5 12.1 %collective-permute-start.51 = (bf16[64,1536]{1,0:T(8,128)(2,1)}, bf16[64,1536]{1,0:T(8,128)(2,1)S(1)}, u32[]{:S(2)}, u32[]{:S(2)}) collective-permute-start(bf16[64,1536]{1,0:T(8,128)(2,1)} %get-tuple-element.168), channel_id=1, source_target_pairs={{0,1},{1,2},{2,3},{3,0},{4,5},{5,6},{6,7},{7,4},{8,9},{9,10},{10,1... | collective-permute-start | bytes 589832 | tf_op jit(solution)/shard_map/ppermute | solution.py:77
  384.5 69.0 %collective-permute-start.59 = (bf16[256,1536]{1,0:T(8,128)(2,1)S(1)}, bf16[256,1536]{1,0:T(8,128)(2,1)S(1)}, u32[]{:S(2)}, u32[]{:S(2)}) collective-permute-start(bf16[256,1536]{1,0:T(8,128)(2,1)S(1)} %multiply_convert_fusion.refs_0_), channel_id=1, source_target_pairs={{0,4},{4,0},{1,5},{5,1},{2,6},{6,2},{3,7},{7,3},{8,12},{12,8},{9,1... | collective-permute-start | bytes 2359304 | tf_op jit(solution)/shard_map/ppermute | solution.py:72
  395.5 11.0 %collective-permute-start.53 = (bf16[64,1536]{1,0:T(8,128)(2,1)}, bf16[64,1536]{1,0:T(8,128)(2,1)S(1)}, u32[]{:S(2)}, u32[]{:S(2)}) collective-permute-start(bf16[64,1536]{1,0:T(8,128)(2,1)} %get-tuple-element.180), channel_id=1, source_target_pairs={{0,2},{1,3},{2,0},{3,1},{4,6},{5,7},{6,4},{7,5},{8,10},{9,11},{10,... | collective-permute-start | bytes 589832 | tf_op jit(solution)/shard_map/ppermute | solution.py:77
  396.9 10.3 %collective-permute-start.54 = (bf16[64,1536]{1,0:T(8,128)(2,1)}, bf16[64,1536]{1,0:T(8,128)(2,1)}, u32[]{:S(2)}, u32[]{:S(2)}) collective-permute-start(bf16[64,1536]{1,0:T(8,128)(2,1)} %get-tuple-element.180), channel_id=1, source_target_pairs={{0,3},{1,0},{2,1},{3,2},{4,7},{5,4},{6,5},{7,6},{8,11},{9,8},{10,9... | collective-permute-start | bytes 589832 | tf_op jit(solution)/shard_map/ppermute | solution.py:77
  409.7 43.8 %collective-permute-start.60 = (bf16[256,1536]{1,0:T(8,128)(2,1)}, bf16[256,1536]{1,0:T(8,128)(2,1)}, u32[]{:S(2)}, u32[]{:S(2)}) collective-permute-start(bf16[256,1536]{1,0:T(8,128)(2,1)} %get-tuple-element.362), channel_id=1, source_target_pairs={{0,4},{4,0},{1,5},{5,1},{2,6},{6,2},{3,7},{7,3},{8,12},{12,8},{9,1... | collective-permute-start | bytes 2359304 | tf_op jit(solution)/shard_map/ppermute | solution.py:72
  430.6 11.0 %collective-permute-start.58 = (bf16[64,1536]{1,0:T(8,128)(2,1)S(1)}, bf16[64,1536]{1,0:T(8,128)(2,1)S(1)}, u32[]{:S(2)}, u32[]{:S(2)}) collective-permute-start(bf16[64,1536]{1,0:T(8,128)(2,1)S(1)} %get-tuple-element.292), channel_id=1, source_target_pairs={{0,1},{1,2},{2,3},{3,0},{4,5},{5,6},{6,7},{7,4},{8,9},{9,10},{10,1... | collective-permute-start | bytes 589832 | tf_op jit(solution)/shard_map/ppermute | solution.py:77
  437.7 17.0 %collective-permute-start.61 = (bf16[256,768]{1,0:T(8,128)(2,1)}, bf16[256,768]{1,0:T(8,128)(2,1)S(1)}, u32[]{:S(2)}, u32[]{:S(2)}) collective-permute-start(bf16[256,768]{1,0:T(8,128)(2,1)} %get-tuple-element.290), channel_id=1, source_target_pairs={{0,4},{4,0},{1,5},{5,1},{2,6},{6,2},{3,7},{7,3},{8,12},{12,8},{9,1... | collective-permute-start | bytes 1179656 | tf_op jit(solution)/shard_map/ppermute | solution.py:72
  446.8 25.0 %all-to-all-start.2 = ((bf16[32,8,1536]{2,1,0:T(8,128)(2,1)}), bf16[32,8,1536]{2,1,0:T(8,128)(2,1)}, u32[]{:S(2)}, u32[]{:S(2)}) async-start(bf16[32,8,1536]{2,1,0:T(8,128)(2,1)} %fusion.4), calls=%async_computation.3 | async-start | bytes 1572864 | tf_op jit(solution)/shard_map/all_to_all | solution.py:1008
  474.1 21.6 %collective-permute-start.63 = (bf16[136,1536]{1,0:T(8,128)(2,1)}, bf16[136,1536]{1,0:T(8,128)(2,1)}, u32[]{:S(2)}, u32[]{:S(2)}) collective-permute-start(bf16[136,1536]{1,0:T(8,128)(2,1)} %fusion.16), channel_id=1, source_target_pairs={{0,1},{1,2},{2,3},{3,0},{4,5},{5,6},{6,7},{7,4},{8,9},{9,10},{10,1... | collective-permute-start | bytes 1253384 | tf_op jit(solution)/shard_map/ppermute | solution.py:77
  474.1 21.6 %collective-permute-start.64 = (bf16[136,1536]{1,0:T(8,128)(2,1)}, bf16[136,1536]{1,0:T(8,128)(2,1)S(1)}, u32[]{:S(2)}, u32[]{:S(2)}) collective-permute-start(bf16[136,1536]{1,0:T(8,128)(2,1)} %fusion.16), channel_id=1, source_target_pairs={{0,2},{1,3},{2,0},{3,1},{4,6},{5,7},{6,4},{7,5},{8,10},{9,11},{10,... | collective-permute-start | bytes 1253384 | tf_op jit(solution)/shard_map/ppermute | solution.py:77
  475.5 21.2 %collective-permute-start.65 = (bf16[136,1536]{1,0:T(8,128)(2,1)}, bf16[136,1536]{1,0:T(8,128)(2,1)S(1)}, u32[]{:S(2)}, u32[]{:S(2)}) collective-permute-start(bf16[136,1536]{1,0:T(8,128)(2,1)} %fusion.16), channel_id=1, source_target_pairs={{0,3},{1,0},{2,1},{3,2},{4,7},{5,4},{6,5},{7,6},{8,11},{9,8},{10,9... | collective-permute-start | bytes 1253384 | tf_op jit(solution)/shard_map/ppermute | solution.py:77
  476.8 37.5 %all-to-all-start.3 = ((bf16[32,48,768]{2,1,0:T(8,128)(2,1)}), bf16[32,48,768]{2,1,0:T(8,128)(2,1)S(1)}, u32[]{:S(2)}, u32[]{:S(2)}) async-start(bf16[32,48,768]{2,1,0:T(8,128)(2,1)} %bitcast.99), calls=%async_computation.5 | async-start | bytes 4718592 | tf_op jit(solution)/shard_map/all_to_all | solution.py:1033
  (179 other events, 1564.1 us)
Sparse Core Ops, SparseCore 0:
  38.2 100.3 all-gather.2
  141.4 72.6 all-gather.4
  284.9 84.1 reduce-scatter.4
  381.4 94.4 reduce-scatter.2
